TPU v7x, 32 devices: a whole 2x2x4 slice. The times are simulated.
32 devices in a mesh: ent: 8 (over y, x, core), rel: 4 (over z).
Axes of the slice: x: 2, y: 2, z: 4, core: 2. Of those that a mesh axis runs over, the one named last changes fastest.
Arguments:
- entity_table: bfloat16 [128, 1024], P('ent'), may hold values from -1.5 to 1.5
- phases: float32 [4096, 512], P('rel'), may hold values from -3.140625 to 3.140625
- head_owner: int32 [16384, 1], P(('ent', 'rel')), may hold values from 0 to 31; in each aligned block of 512 rows (0 to 511, 512 to 1023, ...) at most 32 rows name the same one
- head_row: int32 [16384], P(('ent', 'rel')), may hold values from 0 to 3
- relation: int32 [16384], P(('ent', 'rel')), may hold values from 0 to 1023
- tail_ids: int32 [16384], P(('ent', 'rel')), may hold values from 0 to 127
- known_tails: int32 [16384, 32], P(('ent', 'rel')), may hold values from 0 to 127
Outputs:
- entity_gradient: float32 [128, 1024], P(('ent', 'rel'))
- relation_gradient: float32 [4096, 512], P('rel')
Inputs may be any that keep to these rules, and one draw needn't show every extreme that they name: `head_owner`: owner o of the 32 holds working-set rows o * 4 to o * 4 + 3 and is device (o // 4, o mod 4) of ent and rel. Among the 512 triples of one device at most 32 have heads held by one owner, and exactly 32 in some devices. The triples of block b of 512 belong to relation group b mod 4.
All inputs are finite; a program needn't handle non-finite values.
Results may differ from a plain program's by a relative error of at most 0.004.
Values may be sent and summed in bfloat16 or wider, within the bound.
No kernel may reach another device: no remote copies, remote signals or barrier semaphores. Data moves between devices by JAX's collectives and lax.ppermute only.
A program may use at most 64 MiB of HBM per device.

v0:
```python
import jax
import jax.numpy as jnp
from jax import lax
from jax.sharding import PartitionSpec as P


def local(entity_table, phases, head_owner, head_row, relation, tail_ids, known_tails):
    n_ent = lax.axis_size("ent")
    n_rel = lax.axis_size("rel")
    owner_count = n_ent * n_rel
    rows_dev = head_row.shape[0]
    owner_rows = entity_table.shape[0] // n_rel
    half = phases.shape[1]
    width = 2 * half
    table_all = lax.all_gather(entity_table, "ent", axis=0, tiled=True)
    entities = table_all.shape[0]
    table_sq = jnp.sum(jnp.square(table_all.astype(jnp.float32)), axis=1)
    columns = lax.broadcasted_iota(jnp.int32, (1, entities), 1)
    heads = head_owner[:, 0] * owner_rows + head_row
    head_f = table_all[heads].astype(jnp.float32)
    angles = phases[relation]
    cosine = jnp.cos(angles)
    sine_part = jnp.sin(angles)
    head_re = head_f[:, :half]
    head_im = head_f[:, half:]
    query_re = head_re * cosine - head_im * sine_part
    query_im = head_re * sine_part + head_im * cosine
    query = jnp.concatenate([query_re, query_im], axis=1).astype(jnp.bfloat16)
    query_f = query.astype(jnp.float32)
    query_sq = jnp.sum(query_f * query_f, axis=1)
    cross = lax.dot_general(
        query, table_all, (((1,), (1,)), ((), ())), preferred_element_type=jnp.float32
    )
    scores = 2.0 * cross - query_sq[:, None] - table_sq[None, :]
    listed = jnp.zeros(scores.shape, jnp.bool_)
    for column_j in range(known_tails.shape[1]):
        listed = listed | (known_tails[:, column_j : column_j + 1] == columns)
    is_target = columns == tail_ids[:, None]
    masked = listed & jnp.logical_not(is_target)
    row_max = jnp.max(jnp.where(masked, -jnp.inf, scores), axis=1)
    raw_prob = jnp.where(masked, 0.0, jnp.exp(scores - row_max[:, None]))
    prob = raw_prob / jnp.sum(raw_prob, axis=1, keepdims=True)
    weights = (prob - is_target.astype(jnp.float32)).astype(jnp.bfloat16)
    dquery = 2.0 * jnp.dot(weights, table_all, preferred_element_type=jnp.float32)
    grad_re = dquery[:, :half]
    grad_im = dquery[:, half:]
    head_rows = jnp.concatenate(
        [grad_re * cosine + grad_im * sine_part, -grad_re * sine_part + grad_im * cosine], axis=1
    ).astype(jnp.bfloat16)
    dangle = -query_im * grad_re + query_re * grad_im
    rel_local = jax.ops.segment_sum(dangle, relation, num_segments=phases.shape[0])
    relation_gradient = lax.psum(rel_local, "ent")
    counts = jnp.sum(weights.astype(jnp.float32), axis=0)
    cross_t = lax.dot_general(
        weights, query, (((0,), (0,)), ((), ())), preferred_element_type=jnp.float32
    )
    result = 2.0 * (cross_t - counts[:, None] * table_all.astype(jnp.float32))
    whole = result.reshape(n_ent, n_rel, owner_rows, width)
    by_group = lax.psum_scatter(whole, "rel", scatter_dimension=1, tiled=True)
    summed = lax.psum_scatter(by_group, "ent", scatter_dimension=0, tiled=True).reshape(
        owner_rows, width
    )
    capacity = 2 * rows_dev // owner_count
    owners = head_owner[:, 0]
    owner_hot = (owners[:, None] == lax.broadcasted_iota(jnp.int32, (1, owner_count), 1)).astype(
        jnp.int32
    )
    earlier = jnp.cumsum(owner_hot, axis=0) - owner_hot
    position = jnp.sum(earlier * owner_hot, axis=1)
    slot_ids = owners * capacity + position
    send_rows = jnp.zeros((owner_count * capacity, width), jnp.bfloat16).at[slot_ids].set(head_rows)
    send_labels = jnp.full((owner_count * capacity,), -1, jnp.int32).at[slot_ids].set(head_row)
    recv_rows, recv_labels = (
        lax.all_to_all(
            lax.all_to_all(
                send_rows.reshape(n_ent, n_rel, capacity, width),
                "ent",
                split_axis=0,
                concat_axis=0,
                tiled=True,
            ),
            "rel",
            split_axis=1,
            concat_axis=1,
            tiled=True,
        ),
        lax.all_to_all(
            lax.all_to_all(
                send_labels.reshape(n_ent, n_rel, capacity),
                "ent",
                split_axis=0,
                concat_axis=0,
                tiled=True,
            ),
            "rel",
            split_axis=1,
            concat_axis=1,
            tiled=True,
        ),
    )
    picks = (
        recv_labels.reshape(1, -1) == lax.broadcasted_iota(jnp.int32, (owner_rows, 1), 0)
    ).astype(jnp.bfloat16)
    summed = summed + jnp.dot(
        picks, recv_rows.reshape(-1, width), preferred_element_type=jnp.float32
    )
    return (summed, relation_gradient)


def solution(mesh):
    in_specs = (
        P("ent", None),
        P("rel", None),
        P(("ent", "rel"), None),
        P(("ent", "rel")),
        P(("ent", "rel")),
        P(("ent", "rel")),
        P(("ent", "rel"), None),
    )
    out_specs = (P(("ent", "rel"), None), P("rel", None))
    return jax.shard_map(local, mesh=mesh, in_specs=in_specs, out_specs=out_specs, check_vma=False)
```

profile of v0, /device:TPU:0, one launch (start us, length us, event | category | flops | bytes accessed | tf_op | source)
XLA Modules:
  0.0 223.3 jit_solution(4587688843785948707)
XLA Ops:
  7.2 0.8 fusion.54
  8.0 1.2 reduce-window.6
  9.2 0.2 slice_reduce_fusion
  9.4 0.8 fusion.53
  10.2 0.7 compare_select_fusion
  10.9 2.6 %scatter_custom_fusion = s32[1024]{0:T(1024)S(1)} fusion(s32[512]{0:T(512)S(1)} %bitcast.81, s32[512]{0:T(512)} %param.10, s32[]{:T(128)} %constant.5.clone.1), kind=kCustom, calls=%fused_computation.122 | custom fusion | bytes 4608 | tf_op jit(solution)/shard_map/scatter | solution.py:72
  13.6 0.7 reshape.101
  14.3 5.2 %all-to-all-start = ((s32[8,1,128]{2,1,0:T(1,128)}), s32[8,1,128]{2,1,0:T(1,128)S(1)}, u32[]{:S(2)}, u32[]{:S(2)}) async-start(s32[8,1,128]{2,1,0:T(1,128)} %reshape.101), calls=%async_computation.1 | async-start | bytes 8192 | tf_op jit(solution)/shard_map/all_to_all | solution.py:88
  19.5 0.7 compare_select_fusion.2
  20.2 1.6 fusion.65
  21.8 1.1 fusion.64
  22.9 0.7 compare_select_fusion.1
  23.6 10.0 %all_gather.3 = bf16[128,1024]{1,0:T(8,128)(2,1)S(1)} all-gather(bf16[16,1024]{1,0:T(8,128)(2,1)} %param.7), channel_id=1, replica_groups=mesh['ent'=8,'rel'=4] {'ent'}, dimensions={0}, use_global_device_ids=true | all-gather | bytes 294912 | tf_op jit(solution)/shard_map/all_gather | solution.py:15
  33.8 2.1 gather_fusion
  35.8 1.6 convert_element_type.29
  37.4 1.6 gather_fusion.1
  39.0 3.7 %fusion.63 = (f32[512,512]{1,0:T(8,128)S(1)}, f32[512,512]{1,0:T(8,128)S(1)}) fusion(f32[512,512]{1,0:T(8,128)S(1)} %gather_fusion.1), kind=kLoop, calls=%fused_computation.128 | loop fusion | bytes 3145728 | tf_op jit(solution)/shard_map/sin | solution.py:23
  42.8 1.5 fusion.61
  44.3 0.3 multiply_reduce_fusion
  44.6 1.5 select_reduce_fusion
  46.1 0.8 convert_reduce_fusion
  46.9 0.5 convolution_multiply_fusion
  47.4 1.6 add_convert_fusion.1
  49.0 4.8 %scatter_custom_fusion.1 = bf16[1024,1024]{1,0:T(8,128)(2,1)} fusion(s32[512]{0:T(512)S(1)} %bitcast.82, bf16[512,512]{1,0:T(8,128)(2,1)} %get-tuple-element.13, bf16[]{:T(256)} %constant.33, bf16[512,512]{1,0:T(8,128)(2,1)} %get-tuple-element.12, bf16[]{:T(256)} %constant.7.clone.1), kind=kCustom, calls=%fused_computation.14 | custom fusion | flops 2097152 | bytes 3145732 | tf_op jit(solution)/shard_map/scatter | solution.py:71
  53.8 4.4 %all-to-all-start.2 = ((bf16[8,4,32,1024]{3,2,1,0:T(8,128)(2,1)}), bf16[8,4,32,1024]{3,2,1,0:T(8,128)(2,1)}, u32[]{:S(2)}, u32[]{:S(2)}) async-start(bf16[8,4,32,1024]{3,2,1,0:T(8,128)(2,1)} %bitcast.73), calls=%async_computation.3 | async-start | bytes 4194304 | tf_op jit(solution)/shard_map/all_to_all | solution.py:75
  58.2 0.5 broadcast.56
  58.6 1.2 reduce.2
  59.8 0.8 reshape.102
  60.6 0.6 copy.23
  61.2 1.4 reshape.103
  62.6 22.3 %all-to-all-done.2 = bf16[8,4,32,1024]{3,2,1,0:T(8,128)(2,1)} async-done(((bf16[8,4,32,1024]{3,2,1,0:T(8,128)(2,1)}), bf16[8,4,32,1024]{3,2,1,0:T(8,128)(2,1)}, u32[]{:S(2)}, u32[]{:S(2)}) %all-to-all-start.2) | async-done | bytes 2097184 | tf_op jit(solution)/shard_map/all_to_all | solution.py:75
  84.8 4.9 %all-to-all-start.1 = ((s32[4,1,256]{2,1,0:T(1,128)}), s32[4,1,256]{2,1,0:T(1,128)S(1)}, u32[]{:S(2)}, u32[]{:S(2)}) async-start(s32[4,1,256]{2,1,0:T(1,128)} %reshape.103), calls=%async_computation.2 | async-start | bytes 8192 | tf_op jit(solution)/shard_map/all_to_all | solution.py:87
  89.7 3.2 %copy.18 = bf16[8,4,32,1024]{3,2,0,1:T(8,128)(2,1)} copy(bf16[8,4,32,1024]{3,2,1,0:T(8,128)(2,1)} %all-to-all-done.2) | data formatting | bytes 4194304 | tf_op jit(solution)/shard_map/all_to_all | solution.py:75
  92.9 2.4 %all-to-all-done.1 = s32[4,1,256]{2,1,0:T(1,128)S(1)} async-done(((s32[4,1,256]{2,1,0:T(1,128)}), s32[4,1,256]{2,1,0:T(1,128)S(1)}, u32[]{:S(2)}, u32[]{:S(2)}) %all-to-all-start.1) | async-done | bytes 4128 | tf_op jit(solution)/shard_map/all_to_all | solution.py:87
  95.3 4.5 %all-to-all-start.3 = ((bf16[8,4,32,1024]{3,2,0,1:T(8,128)(2,1)}), bf16[8,4,32,1024]{3,2,0,1:T(8,128)(2,1)}, u32[]{:S(2)}, u32[]{:S(2)}) async-start(bf16[8,4,32,1024]{3,2,0,1:T(8,128)(2,1)} %copy.18), calls=%async_computation.4 | async-start | bytes 4194304 | tf_op jit(solution)/shard_map/all_to_all | solution.py:74
  99.8 2.3 %fusion = f32[128,1024]{1,0:T(8,128)} fusion(bf16[512,128]{0,1:T(8,128)(2,1)S(1)} %get-tuple-element.5, bf16[128,1024]{1,0:T(8,128)(2,1)S(1)} %all_gather.3, bf16[512,512]{1,0:T(8,128)(2,1)} %copy-done.4, bf16[512,512]{1,0:T(8,128)(2,1)} %copy-done.3, f32[128]{0:T(128)S(1)} %copy-done.8), kind=kOutput, calls=%fused_computation.8 | convolution fusion | flops 136839168 | bytes 1966592 | tf_op jit(solution)/shard_map/dot_general | solution.py:54
  102.1 2.0 reshape.44
  104.1 2.1 copy.13
  106.3 6.5 %scatter_custom_fusion.2 = f32[1024,512]{1,0:T(8,128)} fusion(s32[512]{0:T(512)} %param.11, f32[512,512]{1,0:T(8,128)S(1)} %get-tuple-element.9, f32[512,512]{1,0:T(8,128)} %get-tuple-element.15, f32[]{:T(128)} %constant.10.clone.1, f32[512,1024]{1,0:T(8,128)} %copy-done.1), kind=kCustom, calls=%fused_computation.18 | custom fusion | flops 1310720 | bytes 6291968 | tf_op jit(solution)/shard_map/scatter-add | solution.py:51
  112.8 32.0 %reduce-scatter.2.cloned.1.call-done = f32[8,1,4,1024]{3,0,2,1:T(8,128)} async-done(((f32[8,4,4,1024]{3,0,2,1:T(8,128)}), f32[8,1,4,1024]{3,0,2,1:T(8,128)}) %reduce-scatter.2.cloned.1.call-update) | async-done | bytes 131088 | tf_op jit(solution)/shard_map/reduce_scatter | solution.py:59
  144.8 1.6 copy.14
  146.5 0.6 dynamic-slice
  147.1 0.6 reduce.3
  147.8 4.5 %all-to-all-done.3 = bf16[8,4,32,1024]{3,2,0,1:T(8,128)(2,1)} async-done(((bf16[8,4,32,1024]{3,2,0,1:T(8,128)(2,1)}), bf16[8,4,32,1024]{3,2,0,1:T(8,128)(2,1)}, u32[]{:S(2)}, u32[]{:S(2)}) %all-to-all-start.3) | async-done | bytes 2097184 | tf_op jit(solution)/shard_map/all_to_all | solution.py:74
  152.3 3.2 %copy.19 = bf16[8,4,32,1024]{3,2,1,0:T(8,128)(2,1)} copy(bf16[8,4,32,1024]{3,2,0,1:T(8,128)(2,1)} %all-to-all-done.3) | data formatting | bytes 4194304 | tf_op jit(solution)/shard_map/all_to_all | solution.py:74
  155.5 56.3 %all-reduce.4.cloned.1.call-done = (f32[8,1,4,1024]{3,2,1,0:T(4,128)}, f32[1024,512]{1,0:T(8,128)}) async-done(((f32[8,1,4,1024]{3,2,1,0:T(4,128)}, f32[1024,512]{1,0:T(8,128)}), (f32[8,1,4,1024]{3,2,1,0:T(4,128)}, f32[1024,512]{1,0:T(8,128)})) %all-reduce.4.cloned.1.call-update) | async-done | bytes 2228240
  211.8 3.4 %convolution_add_fusion = f32[4,1024]{1,0:T(4,128)} fusion(bf16[1024,1024]{1,0:T(8,128)(2,1)} %bitcast.74, f32[8,1,4,1024]{3,2,1,0:T(4,128)} %get-tuple-element.2, u32[]{:T(128)} %bitcast.40, s32[1024]{0:T(1024)S(1)} %eq.669), kind=kOutput, calls=%fused_computation.12 | convolution fusion | flops 8396800 | bytes 2134020 | tf_op jit(solution)/shard_map/dot_general | solution.py:104
  215.2 1.3 copy.26
  (35 shorter events, 0.7 us)
Async XLA Ops:
  7.2 30.2 %copy-start = (f32[1024,512]{1,0:T(8,128)S(1)}, f32[1024,512]{1,0:T(8,128)}, u32[]{:S(2)}) copy-start(f32[1024,512]{1,0:T(8,128)} %param.8) | copy-start | bytes 6291460
  14.3 39.5 %all-to-all-start = ((s32[8,1,128]{2,1,0:T(1,128)}), s32[8,1,128]{2,1,0:T(1,128)S(1)}, u32[]{:S(2)}, u32[]{:S(2)}) async-start(s32[8,1,128]{2,1,0:T(1,128)} %reshape.101), calls=%async_computation.1 | async-start | bytes 8192 | tf_op jit(solution)/shard_map/all_to_all | solution.py:88
  39.0 3.7 %copy-start.2 = (f32[512,1024]{1,0:T(8,128)S(1)}, f32[512,1024]{1,0:T(8,128)}, u32[]{:S(2)}) copy-start(f32[512,1024]{1,0:T(8,128)} %convert_element_type.29) | copy-start | bytes 6291460
  42.7 1.8 copy-start.6
  42.7 1.8 copy-start.7
  44.3 1.8 copy-start.3
  44.3 1.8 copy-start.4
  47.4 1.6 copy-start.1
  53.8 31.0 %all-to-all-start.2 = ((bf16[8,4,32,1024]{3,2,1,0:T(8,128)(2,1)}), bf16[8,4,32,1024]{3,2,1,0:T(8,128)(2,1)}, u32[]{:S(2)}, u32[]{:S(2)}) async-start(bf16[8,4,32,1024]{3,2,1,0:T(8,128)(2,1)} %bitcast.73), calls=%async_computation.3 | async-start | bytes 4194304 | tf_op jit(solution)/shard_map/all_to_all | solution.py:75
  84.8 10.4 %all-to-all-start.1 = ((s32[4,1,256]{2,1,0:T(1,128)}), s32[4,1,256]{2,1,0:T(1,128)S(1)}, u32[]{:S(2)}, u32[]{:S(2)}) async-start(s32[4,1,256]{2,1,0:T(1,128)} %reshape.103), calls=%async_computation.2 | async-start | bytes 8192 | tf_op jit(solution)/shard_map/all_to_all | solution.py:87
  92.9 6.9 %copy-start.8 = (f32[128]{0:T(128)S(1)}, f32[128]{0:T(128)}, u32[]{:S(2)}) copy-start(f32[128]{0:T(128)} %get-tuple-element.4) | copy-start | bytes 1540
  95.3 57.0 %all-to-all-start.3 = ((bf16[8,4,32,1024]{3,2,0,1:T(8,128)(2,1)}), bf16[8,4,32,1024]{3,2,0,1:T(8,128)(2,1)}, u32[]{:S(2)}, u32[]{:S(2)}) async-start(bf16[8,4,32,1024]{3,2,0,1:T(8,128)(2,1)} %copy.18), calls=%async_computation.4 | async-start | bytes 4194304 | tf_op jit(solution)/shard_map/all_to_all | solution.py:74
  99.7 45.1 %reduce-scatter.2.cloned.1.call-start = ((), (), s32[]{:S(2)}) async-start(), calls=%async_computation.5 | async-start | bytes 655360 | tf_op jit(solution)/shard_map/reduce_scatter | solution.py:59
  106.3 105.5 %all-reduce.4.cloned.1.call-start = ((), (), s32[]{:S(2)}) async-start(), calls=%async_computation.6 | async-start | bytes 4456448
  112.8 33.7 %copy-start.9 = (u32[32]{0:T(128)S(1)}, u32[32]{0:T(128)}, u32[]{:S(2)}) copy-start(u32[32]{0:T(128)} %constant.30) | copy-start | bytes 388
  211.8 3.4 %copy-start.5 = (f32[1024,512]{1,0:T(8,128)S(1)}, f32[1024,512]{1,0:T(8,128)}, u32[]{:S(2)}) copy-start(f32[1024,512]{1,0:T(8,128)} %get-tuple-element.52) | copy-start | bytes 6291460
Sparse Core Ops, SparseCore 0:
  106.4 38.3 reduce-scatter.1
  148.1 63.6 all-reduce.3
where the time goes:
time: 224 us; the launch traced here: 223 us
  waiting for transfers between devices  117 us (52%)
  local copies, waits for them, and re-layouts  31.2 us (14%)
  other arithmetic  23.9 us (11%)
  starting transfers between devices  19 us (8%)
  between operations  14.2 us (6%)
  blocking collectives  9.99 us (4%)
  matrix products  7.6 us (3%)
    unnamed x3, waiting for transfers between devices  56.3 us
    reduce_scatter x1, waiting for transfers between devices, local(): by_group = lax.psum_scatter(whole, 'rel', scatter_dimension=1, tiled=True)  32 us
    all_to_all x1, waiting for transfers between devices, local(): lax.all_to_all(send_rows.reshape(n_ent, n_rel, capacity, width), 'ent', s...  22.3 us
    all_gather x1, blocking collectives, local(): table_all = lax.all_gather(entity_table, 'ent', axis=0, tiled=True)  9.99 us
    scatter-add x1, other arithmetic, local(): jax.ops.segment_sum(dangle, relation, num_segments=phases.shape[0])  6.49 us
    all_to_all x1, starting transfers between devices, local(): lax.all_to_all(send_labels.reshape(n_ent, n_rel, capacity), 'ent', split_...  5.17 us
    unnamed x26, local copies, waits for them, and re-layouts  4.88 us
    all_to_all x1, starting transfers between devices, local(): lax.all_to_all(lax.all_to_all(send_labels.reshape(n_ent, n_rel, capacity)...  4.87 us
  transfers between devices with their start and end apart: 6, of which 5 were waited for; matrix products, arithmetic and copies ran while one was open for 23% of the time, Pallas kernels for 0%

commit v1 on v0

v1 whole, which is shorter than its diff:
```python
import functools

import jax
import jax.numpy as jnp
from jax import lax
from jax.experimental import pallas as pl
from jax.experimental.pallas import tpu as pltpu
from jax.sharding import PartitionSpec as P

F32 = jnp.float32
BF16 = jnp.bfloat16
I32 = jnp.int32
VMEM_BYTES = 40 * 1024 * 1024
NT = (((1,), (1,)), ((), ()))

SIN_C = (0.9999999957, -0.1666665799, 0.008333051133, -0.0001980908535, 2.605256611e-06)
COS_C = (0.9999999998, -0.4999999936, 0.04166663628, -0.00138883618, 2.476018568e-05, -2.605198025e-07)


def params():
    return pltpu.CompilerParams(vmem_limit_bytes=VMEM_BYTES)


def cost(flops, nbytes, trans=0):
    return pl.CostEstimate(flops=flops, bytes_accessed=nbytes, transcendentals=trans)


def horner(coeffs, y):
    acc = jnp.full_like(y, coeffs[-1])
    for c in coeffs[-2::-1]:
        acc = acc * y + c
    return acc


def prepare_kernel(flip_ref, angles_ref, owner_ref, row_ref, tail_ref, known_ref, cos_ref, sin_ref, code_ref, *, owner_rows):
    u = angles_ref[...] * 0.5
    y = u * u
    s = u * horner(SIN_C, y)
    c = horner(COS_C, y)
    sin_ref[...] = 2.0 * s * c
    cos_ref[...] = 1.0 - 2.0 * s * s
    flip = flip_ref[0]
    n = owner_ref.shape[1]
    entities = code_ref.shape[1]
    heads = (owner_ref[...] * owner_rows + row_ref[...]) ^ flip
    tails = tail_ref[...] ^ flip
    known = known_ref[...] ^ flip
    bits = lax.shift_left(jnp.ones_like(known), known & 31)
    word_of = lax.shift_right_logical(known, 5)
    sub = lax.broadcasted_iota(I32, (8, n), 0)
    pieces = []
    for w in range(entities // 32):
        hit = jnp.where(word_of == w, bits, 0)
        word = hit[0:8]
        for r in range(8, hit.shape[0], 8):
            word = word | hit[r : r + 8]
        for shift in (4, 2, 1):
            word = word | pltpu.roll(word, shift, 0)
        for g in range(4):
            e = sub + (32 * w + 8 * g)
            listed = lax.shift_right_logical(word, sub + 8 * g) & 1
            target = jnp.where(e == tails, 1, 0)
            head = jnp.where(e == heads, 4, 0)
            pieces.append((listed & (1 - target)) | (target * 2) | head)
    code_ref[...] = jnp.concatenate(pieces, axis=0).T


def score_kernel(par_ref, *refs, peers):
    table_refs = refs[:peers]
    cos_ref, sin_ref, code_ref, keep_ref, send_ref, w_ref, q_ref, hr_ref, table, tsq = refs[peers:]
    half = cos_ref.shape[1]

    @pl.when(pl.program_id(0) == 0)
    def _():
        step = table_refs[0].shape[0]
        for i in range(peers):
            block = table_refs[i][...]
            table[i * step : (i + 1) * step, :] = block
        f = table[...].astype(F32)
        norm = jnp.sum(f * f, axis=1, keepdims=True)
        tsq[...] = jnp.broadcast_to(norm, (norm.shape[0], 128)).T[0:8]

    tab = table[...]
    cosine = cos_ref[...]
    sine = sin_ref[...]
    code = code_ref[...]
    hot = jnp.where((code & 4) != 0, 1.0, 0.0).astype(BF16)
    head = jnp.dot(hot, tab, preferred_element_type=F32)
    hre = head[:, :half]
    him = head[:, half:]
    qre = hre * cosine - him * sine
    qim = hre * sine + him * cosine
    q = jnp.concatenate([qre, qim], axis=1).astype(BF16)
    q_ref[...] = q
    qf = q.astype(F32)
    qsq = jnp.sum(qf * qf, axis=1, keepdims=True)
    cross = lax.dot_general(q, tab, NT, preferred_element_type=F32)
    scores = 2.0 * cross - qsq - tsq[0:1, :]
    masked = (code & 1) != 0
    target = jnp.where((code & 2) != 0, 1.0, 0.0)
    row_max = jnp.max(jnp.where(masked, -jnp.inf, scores), axis=1, keepdims=True)
    raw = jnp.where(masked, 0.0, jnp.exp(scores - row_max))
    prob = raw / jnp.sum(raw, axis=1, keepdims=True)
    w = (prob - target).astype(BF16)
    w_ref[...] = w
    dq = 2.0 * jnp.dot(w, tab, preferred_element_type=F32)
    dre = dq[:, :half]
    dim = dq[:, half:]
    dangle = (qre * dim - qim * dre).astype(BF16)
    quarter = half // 2
    first = dangle[:, :quarter]
    second = dangle[:, quarter:]
    even = par_ref[0] == 0
    keep_ref[...] = jnp.where(even, first, second)
    send_ref[...] = jnp.where(even, second, first)
    hr_ref[...] = jnp.concatenate([dre * cosine + dim * sine, dim * cosine - dre * sine], axis=1).astype(BF16)


def entity_kernel(pos_ref, w_ref, q_ref, hr_ref, owner_ref, row_ref, *refs, peers, n_rel, owner_rows):
    table_refs = refs[:peers]
    keep_ref, send_ref, wt, hot, counts, sel = refs[peers:]
    entities = w_ref.shape[1]
    n = w_ref.shape[0]

    @pl.when(pl.program_id(0) == 0)
    def _():
        def row_id(i):
            j = i % owner_rows
            p = (i // owner_rows) % peers
            k = (i // (owner_rows * peers)) % n_rel
            b = i // (owner_rows * peers * n_rel)
            return ((p * 2 + b) * n_rel + (k ^ pos_ref[1])) * owner_rows + j

        e = row_id(lax.broadcasted_iota(I32, (entities, entities), 0))
        pick = jnp.where(e == lax.broadcasted_iota(I32, (entities, entities), 1), 1.0, 0.0).astype(BF16)
        sel[...] = pick
        wtf = lax.dot_general(pick, w_ref[...], NT, preferred_element_type=F32)
        wt[...] = wtf.astype(BF16)
        counts[...] = jnp.broadcast_to(jnp.sum(wtf, axis=1, keepdims=True), counts.shape)
        heads = (owner_ref[...] * owner_rows + row_ref[...]) ^ pos_ref[0]
        eh = row_id(lax.broadcasted_iota(I32, (entities, n), 0))
        hot[...] = jnp.where(eh == heads, 1.0, 0.0).astype(BF16)

    tab = jnp.concatenate([r[...] for r in table_refs], axis=0)
    tab = jnp.dot(sel[...], tab, preferred_element_type=F32)
    cross = jnp.dot(wt[...], q_ref[...], preferred_element_type=F32)
    heads_sum = jnp.dot(hot[...], hr_ref[...], preferred_element_type=F32)
    total = 2.0 * (cross - counts[:, 0:1] * tab) + heads_sum
    keep_ref[...] = total[: entities // 2]
    send_ref[...] = total[entities // 2 :]


def scatter_kernel(chip_ref, mine_ref, theirs_ref, keep_ref, got_ref, *outs, peers, rows):
    ids = jnp.concatenate([mine_ref[...], theirs_ref[...]], axis=1)
    d = jnp.concatenate([keep_ref[...], got_ref[...]], axis=0)
    n = ids.shape[1]
    iota = lax.broadcasted_iota(I32, (rows, n), 0)
    for p in range(peers):
        base = (chip_ref[0] ^ p) * rows
        hot = jnp.where(iota == ids - base, 1.0, 0.0).astype(BF16)
        outs[p][...] = jnp.dot(hot, d, preferred_element_type=F32).astype(outs[p].dtype)


def place_kernel(pos_ref, *refs, peers, rows):
    out_ref = refs[-1]
    quarter = refs[0].shape[1]
    chip, par = pos_ref[0], pos_ref[1]
    for side in range(2):
        col = pl.multiple_of((par ^ side) * quarter, quarter)
        for p in range(peers):
            row = pl.multiple_of((chip ^ p) * rows, rows)
            out_ref[pl.ds(row, rows), pl.ds(col, quarter)] = refs[side * peers + p][...].astype(F32)


def local(entity_table, phases, head_owner, head_row, relation, tail_ids, known_tails):
    n_ent = lax.axis_size("ent")
    n_rel = lax.axis_size("rel")
    peers = n_ent // 2
    n = head_row.shape[0]
    rows_ent, width = entity_table.shape
    owner_rows = rows_ent // n_rel
    entities = rows_ent * n_ent
    half = width // 2
    quarter = half // 2
    rels = phases.shape[0]
    rows = rels // peers
    block = min(128, n)
    steps = n // block
    me_ent = lax.axis_index("ent")
    me_rel = lax.axis_index("rel")

    def swap(x, k):
        return lax.ppermute(x, "ent", [(i, i ^ k) for i in range(n_ent)])

    def swap_rel(x, k):
        return lax.ppermute(x, "rel", [(i, i ^ k) for i in range(n_rel)])

    smem = pl.BlockSpec(memory_space=pltpu.SMEM)

    owner_l = head_owner.reshape(1, n)
    row_l = head_row.reshape(1, n)
    rel_l = relation.reshape(1, n)
    tail_l = tail_ids.reshape(1, n)
    known_l = known_tails.T
    rel_mate = swap(rel_l, 1)
    pair = jnp.concatenate([entity_table, swap(entity_table, 1)], axis=0)
    tables = [pair] + [swap(pair, 2 * p) for p in range(1, peers)]

    flip = (me_ent * rows_ent).astype(I32)
    chip = (me_ent // 2).astype(I32)
    par = (me_ent % 2).astype(I32)

    angles = phases.at[relation].get(mode="promise_in_bounds")
    lane = lambda r: pl.BlockSpec((r, block), lambda i: (0, i))
    line = lambda c: pl.BlockSpec((block, c), lambda i: (i, 0))
    cosine, sine, code = pl.pallas_call(
        functools.partial(prepare_kernel, owner_rows=owner_rows),
        grid=(steps,),
        in_specs=[smem, line(half), lane(1), lane(1), lane(1), lane(known_l.shape[0])],
        out_specs=[line(half), line(half), line(entities)],
        out_shape=[
            jax.ShapeDtypeStruct((n, half), F32),
            jax.ShapeDtypeStruct((n, half), F32),
            jax.ShapeDtypeStruct((n, entities), I32),
        ],
        compiler_params=params(),
        cost_estimate=cost(30 * n * half, 12 * n * half),
        name="prepare",
    )(flip.reshape(1), angles, owner_l, row_l, tail_l, known_l)

    whole = lambda a: pl.BlockSpec(a.shape, lambda i: (0, 0))
    keep, send, w, q, hr = pl.pallas_call(
        functools.partial(score_kernel, peers=peers),
        grid=(steps,),
        in_specs=[smem] + [whole(t) for t in tables] + [line(half), line(half), line(entities)],
        out_specs=[line(quarter), line(quarter), line(entities), line(width), line(width)],
        out_shape=[
            jax.ShapeDtypeStruct((n, quarter), BF16),
            jax.ShapeDtypeStruct((n, quarter), BF16),
            jax.ShapeDtypeStruct((n, entities), BF16),
            jax.ShapeDtypeStruct((n, width), BF16),
            jax.ShapeDtypeStruct((n, width), BF16),
        ],
        scratch_shapes=[pltpu.VMEM((entities, width), BF16), pltpu.VMEM((8, entities), F32)],
        compiler_params=params(),
        cost_estimate=cost(6 * n * entities * width, 12 * n * width),
        name="score",
    )(par.reshape(1), *tables, cosine, sine, code)

    got = swap(send, 1)

    cols = 256 if width % 256 == 0 else width
    col = lambda r: pl.BlockSpec((r, cols), lambda i: (0, i))
    fixed = lambda r, c: pl.BlockSpec((r, c), lambda i: (0, 0))
    ent_keep, ent_send = pl.pallas_call(
        functools.partial(entity_kernel, peers=peers, n_rel=n_rel, owner_rows=owner_rows),
        grid=(width // cols,),
        in_specs=[smem, fixed(n, entities), col(n), col(n), fixed(1, n), fixed(1, n)] + [col(2 * rows_ent)] * peers,
        out_specs=[col(entities // 2), col(entities // 2)],
        out_shape=[jax.ShapeDtypeStruct((entities // 2, width), F32)] * 2,
        scratch_shapes=[
            pltpu.VMEM((entities, n), BF16),
            pltpu.VMEM((entities, n), BF16),
            pltpu.VMEM((entities, 128), F32),
            pltpu.VMEM((entities, entities), BF16),
        ],
        compiler_params=params(),
        cost_estimate=cost(4 * n * entities * width, 4 * n * width + 4 * entities * width),
        name="entity",
    )(jnp.stack([flip, me_rel.astype(I32)]), w, q, hr, owner_l, row_l, *tables)

    vm = pl.BlockSpec(memory_space=pltpu.VMEM)
    parts = pl.pallas_call(
        functools.partial(scatter_kernel, peers=peers, rows=rows),
        in_specs=[smem, vm, vm, vm, vm],
        out_specs=[vm] * peers,
        out_shape=[jax.ShapeDtypeStruct((rows, quarter), F32 if p == 0 else BF16) for p in range(peers)],
        compiler_params=params(),
        cost_estimate=cost(4 * n * rels * quarter, 4 * n * quarter + 2 * rels * quarter),
        name="scatter",
    )(chip.reshape(1), rel_l, rel_mate, keep, got)

    total = parts[0]
    for p in range(1, peers):
        total = total + swap(parts[p], 2 * p).astype(F32)
    final = total.astype(BF16)
    mine = [final] + [swap(final, 2 * p) for p in range(1, peers)]
    theirs = [swap(x, 1) for x in mine]
    relation_gradient = pl.pallas_call(
        functools.partial(place_kernel, peers=peers, rows=rows),
        in_specs=[smem] + [vm] * (2 * peers),
        out_specs=vm,
        out_shape=jax.ShapeDtypeStruct((rels, half), F32),
        compiler_params=params(),
        cost_estimate=cost(rels * half, 6 * rels * half),
        name="place",
    )(jnp.stack([chip, par]), *mine, *theirs)

    ent = ent_keep + swap(ent_send, 1)
    ent = ent.reshape(n_rel, peers * owner_rows, width)
    acc = ent[0]
    for k in range(1, n_rel):
        acc = acc + swap_rel(ent[k], k)
    acc = acc.reshape(peers, owner_rows, width)
    entity_gradient = acc[0]
    for p in range(1, peers):
        entity_gradient = entity_gradient + swap(acc[p], 2 * p)
    return entity_gradient, relation_gradient


def solution(mesh):
    in_specs = (
        P("ent", None),
        P("rel", None),
        P(("ent", "rel"), None),
        P(("ent", "rel")),
        P(("ent", "rel")),
        P(("ent", "rel")),
        P(("ent", "rel"), None),
    )
    out_specs = (P(("ent", "rel"), None), P("rel", None))
    return jax.shard_map(local, mesh=mesh, in_specs=in_specs, out_specs=out_specs, check_vma=False)
```

time: 224 us -> 55 us (0.25)
  waiting for transfers between devices: 117 us -> 17.5 us
  local copies, waits for them, and re-layouts: 31.2 us -> 3.18 us
  other arithmetic: 23.9 us -> 1.57 us
  between operations: 14.2 us -> 0.84 us
  Pallas kernels: 0 us -> 10.7 us
  blocking collectives: 9.99 us -> 0 us
  matrix products: 7.6 us -> 0 us
    unnamed x3 -> x0, waiting for transfers between devices: 56.3 us -> none
    reduce_scatter x1 -> x0, waiting for transfers between devices: 32 us -> none  [local(): by_group = lax.psum_scatter(whole, 'rel', scatter_dimension=1, tiled=True)]
    all_to_all x4 -> x0, waiting for transfers between devices: 29.1 us -> none  [the longest x1 22.3 us: local(): lax.all_to_all(send_rows.reshape(n_ent, n_rel, capacity, width), 'ent', s...]
    ppermute x0 -> x23, starting transfers between devices: none -> 21 us  [the longest x20 16.6 us: swap(): return lax.ppermute(x, 'ent', [(i, i ^ k) for i in range(n_ent)])]
    all_to_all x4 -> x0, starting transfers between devices: 18.9 us -> none  [the longest x1 5.17 us: local(): lax.all_to_all(send_labels.reshape(n_ent, n_rel, capacity), 'ent', split_...]
    ppermute x0 -> x23, waiting for transfers between devices: none -> 17.5 us  [the longest x20 17.5 us: swap(): return lax.ppermute(x, 'ent', [(i, i ^ k) for i in range(n_ent)])]
    pallas_call x0 -> x5, Pallas kernels: none -> 10.7 us  [the longest x1 3.86 us: local(): pl.pallas_call(functools.partial(score_kernel, peers=peers), grid=(steps,...]
    all_gather x1 -> x0, blocking collectives: 9.99 us -> none  [local(): table_all = lax.all_gather(entity_table, 'ent', axis=0, tiled=True)]
  transfers between devices with their start and end apart: 6 -> 23, of which waited for: 5 -> 9; matrix products, arithmetic and copies ran while one was open for 23% -> 8% of each run, Pallas kernels for 0% -> 5%
where the time goes in v1:
time: 55 us; the launch traced here: 54.8 us
  starting transfers between devices  21 us (38%)
  waiting for transfers between devices  17.5 us (32%)
  Pallas kernels  10.7 us (19%)
  local copies, waits for them, and re-layouts  3.18 us (6%)
  other arithmetic  1.57 us (3%)
  between operations  0.84 us (2%)
    ppermute x20, waiting for transfers between devices, swap(): return lax.ppermute(x, 'ent', [(i, i ^ k) for i in range(n_ent)])  17.5 us
    ppermute x20, starting transfers between devices, swap(): return lax.ppermute(x, 'ent', [(i, i ^ k) for i in range(n_ent)])  16.6 us
    ppermute x3, starting transfers between devices, swap_rel(): return lax.ppermute(x, 'rel', [(i, i ^ k) for i in range(n_rel)])  4.39 us
    pallas_call x1, Pallas kernels, local(): pl.pallas_call(functools.partial(score_kernel, peers=peers), grid=(steps,...  3.86 us
    pallas_call x1, Pallas kernels, local(): pl.pallas_call(functools.partial(entity_kernel, peers=peers, n_rel=n_rel,...  2.23 us
    pallas_call x1, Pallas kernels, local(): pl.pallas_call(functools.partial(place_kernel, peers=peers, rows=rows), i...  2.01 us
    pallas_call x1, Pallas kernels, local(): pl.pallas_call(functools.partial(prepare_kernel, owner_rows=owner_rows),...  1.86 us
    gather x1, local copies, waits for them, and re-layouts, local(): angles = phases.at[relation].get(mode='promise_in_bounds')  1.62 us
  transfers between devices with their start and end apart: 23, of which 9 were waited for; matrix products, arithmetic and copies ran while one was open for 8% of the time, Pallas kernels for 5%

profile of v1, /device:TPU:0, one launch (start us, length us, event | category | flops | bytes accessed | tf_op | source)
XLA Modules:
  0.0 54.8 jit_solution(17885956986380570578)
XLA Ops:
  0.6 0.0 copy-start
  0.6 0.5 collective-permute-start
  1.2 0.9 %constant_dynamic-update-slice_fusion.1 = bf16[32,1024]{1,0:T(8,128)(2,1)S(1)} fusion(bf16[16,1024]{1,0:T(8,128)(2,1)} %param.7), kind=kLoop, calls=%fused_computation.11 | loop fusion | bytes 65536
  2.0 0.7 %compare_select_fusion = s32[512]{0:T(512)S(1)} fusion(s32[512]{0:T(512)} %param.11), kind=kLoop, calls=%fused_computation.8 | loop fusion | flops 1536 | bytes 4096 | tf_op jit(solution)/shard_map/select_n | solution.py:213
  2.7 0.0 copy-start.1
  2.7 0.0 copy-start.3
  2.8 0.0 copy-start.4
  2.8 1.6 %gather_fusion = f32[512,512]{1,0:T(8,128)S(1)} fusion(f32[1024,512]{1,0:T(8,128)S(1)} %copy-done, s32[1024]{0:T(1024)S(1)} %pad_clamp_fusion), kind=kCustom, calls=%fused_computation | custom fusion | bytes 2099200 | tf_op jit(solution)/shard_map/gather | solution.py:213
  4.4 1.9 %prepare.1 = (f32[512,512]{1,0:T(8,128)S(1)}, f32[512,512]{1,0:T(8,128)S(1)}, s32[512,128]{1,0:T(8,128)S(1)}) custom-call(s32[1]{0:T(128)} %bitcast.flip_ref, f32[512,512]{1,0:T(8,128)S(1)} %gather_fusion, s32[1,512]{1,0:T(1,128)S(1)} %bitcast.10, s32[1,512]{1,0:T(1,128)S(1)} %bitcast.12, s32[1,512]{1,0:T(1,128)S(1)} %bitcast.14, s32[32,512]{1,0:T(8,128)S(1)} %bitcast.9), custom_call_target="tpu_custom_call" | custom-call | flops 7864320 | bytes 3145728 | tf_op jit(solution)/shard_map/prepare/pallas_call | solution.py:216
  6.3 2.6 %collective-permute-start.1 = (bf16[32,1024]{1,0:T(8,128)(2,1)S(1)}, bf16[32,1024]{1,0:T(8,128)(2,1)S(1)}, u32[]{:S(2)}, u32[]{:S(2)}) collective-permute-start(bf16[32,1024]{1,0:T(8,128)(2,1)S(1)} %constant_dynamic-update-slice_fusion.refs_0_), channel_id=1, source_target_pairs={{0,8},{4,12},{8,0},{12,4},{16,24},{20,28},{24,16},{28,20},{1,9},{5... | collective-permute-start | bytes 196616 | tf_op jit(solution)/shard_map/ppermute | solution.py:193
  8.9 1.5 %collective-permute-start.2 = (bf16[32,1024]{1,0:T(8,128)(2,1)S(1)}, bf16[32,1024]{1,0:T(8,128)(2,1)S(1)}, u32[]{:S(2)}, u32[]{:S(2)}) collective-permute-start(bf16[32,1024]{1,0:T(8,128)(2,1)S(1)} %constant_dynamic-update-slice_fusion.refs_0_), channel_id=1, source_target_pairs={{0,16},{4,20},{8,24},{12,28},{16,0},{20,4},{24,8},{28,12},{1,17},{... | collective-permute-start | bytes 196616 | tf_op jit(solution)/shard_map/ppermute | solution.py:193
  10.5 0.0 collective-permute-start.3
  10.5 0.1 pad_add_fusion.pos_ref
  10.6 1.0 %collective-permute-done.1.refs_1_ = bf16[32,1024]{1,0:T(8,128)(2,1)S(1)} collective-permute-done((bf16[32,1024]{1,0:T(8,128)(2,1)S(1)}, bf16[32,1024]{1,0:T(8,128)(2,1)S(1)}, u32[]{:S(2)}, u32[]{:S(2)}) %collective-permute-start.1) | collective-permute-done | bytes 65568 | tf_op jit(solution)/shard_map/ppermute | solution.py:193
  11.5 1.7 %collective-permute-done.2.refs_2_ = bf16[32,1024]{1,0:T(8,128)(2,1)S(1)} collective-permute-done((bf16[32,1024]{1,0:T(8,128)(2,1)S(1)}, bf16[32,1024]{1,0:T(8,128)(2,1)S(1)}, u32[]{:S(2)}, u32[]{:S(2)}) %collective-permute-start.2) | collective-permute-done | bytes 65568 | tf_op jit(solution)/shard_map/ppermute | solution.py:193
  13.2 2.4 %collective-permute-done.3.refs_3_ = bf16[32,1024]{1,0:T(8,128)(2,1)S(1)} collective-permute-done((bf16[32,1024]{1,0:T(8,128)(2,1)S(1)}, bf16[32,1024]{1,0:T(8,128)(2,1)S(1)}, u32[]{:S(2)}, u32[]{:S(2)}) %collective-permute-start.3) | collective-permute-done | bytes 65568 | tf_op jit(solution)/shard_map/ppermute | solution.py:193
  15.6 3.9 %score.1 = (bf16[512,256]{1,0:T(8,128)(2,1)S(1)}, bf16[512,256]{1,0:T(8,128)(2,1)S(1)}, bf16[512,128]{1,0:T(8,128)(2,1)S(1)}, bf16[512,1024]{1,0:T(8,128)(2,1)S(1)}, bf16[512,1024]{1,0:T(8,128)(2,1)S(1)}) custom-call(s32[1]{0:T(128)} %bitcast.2.par_ref, bf16[32,1024]{1,0:T(8,128)(2,1)S(1)} %constant_dynamic-update-slice_fusion.refs_0_, ...), custom_call_target="tpu_custom_call" | custom-call | flops 402653184 | bytes 6291456 | tf_op jit(solution)/shard_map/score/pallas_call | solution.py:232
  19.5 0.0 copy-start.5
  19.5 2.2 %entity.1 = (f32[64,1024]{1,0:T(8,128)S(1)}, f32[64,1024]{1,0:T(8,128)S(1)}) custom-call(s32[2]{0:T(128)S(1)} %pad_add_fusion.pos_ref, bf16[512,128]{1,0:T(8,128)(2,1)S(1)} %get-tuple-element.19.w_ref, bf16[512,1024]{1,0:T(8,128)(2,1)S(1)} %get-tuple-element.20.q_ref, bf16[512,1024]{1,0:T(8,128)(2,1)S(1)} %get-tuple-element.21.hr_ref, ...), custom_call_target="tpu_custom_call" | custom-call | flops 268435456 | bytes 2621440 | tf_op jit(solution)/shard_map/entity/pallas_call | solution.py:255
  21.8 0.1 collective-permute-start.4
  21.8 0.5 collective-permute-start.12
  22.3 1.0 %collective-permute-done.4 = f32[64,1024]{1,0:T(8,128)S(1)} collective-permute-done((f32[64,1024]{1,0:T(8,128)S(1)}, f32[64,1024]{1,0:T(8,128)S(1)}, u32[]{:S(2)}, u32[]{:S(2)}) %collective-permute-start.4) | collective-permute-done | bytes 262176 | tf_op jit(solution)/shard_map/ppermute | solution.py:193
  23.4 0.6 %fusion.4 = (f32[16,1024]{1,0:T(8,128)S(1)}, f32[16,1024]{1,0:T(8,128)}, f32[16,1024]{1,0:T(8,128)S(1)}) fusion(f32[64,1024]{1,0:T(8,128)S(1)} %add.44), kind=kLoop, calls=%fused_computation.14 | loop fusion | bytes 393216 | tf_op jit(solution)/shard_map/slice | solution.py:303
  24.0 3.6 %collective-permute-start.7 = (f32[16,1024]{1,0:T(8,128)}, f32[16,1024]{1,0:T(8,128)S(1)}, u32[]{:S(2)}, u32[]{:S(2)}) collective-permute-start(f32[16,1024]{1,0:T(8,128)} %get-tuple-element.31), channel_id=1, source_target_pairs={{0,3},{1,2},{2,1},{3,0},{4,7},{5,6},{6,5},{7,4},{8,11},{9,10},{10,... | collective-permute-start | bytes 196616 | tf_op jit(solution)/shard_map/ppermute | solution.py:196
  27.6 0.8 %collective-permute-start.5 = (f32[16,1024]{1,0:T(8,128)S(1)}, f32[16,1024]{1,0:T(8,128)S(1)}, u32[]{:S(2)}, u32[]{:S(2)}) collective-permute-start(f32[16,1024]{1,0:T(8,128)S(1)} %get-tuple-element.30), channel_id=1, source_target_pairs={{0,1},{1,0},{2,3},{3,2},{4,5},{5,4},{6,7},{7,6},{8,9},{9,8},{10,11... | collective-permute-start | bytes 196616 | tf_op jit(solution)/shard_map/ppermute | solution.py:196
  28.4 1.2 %collective-permute-done.11.theirs_ref = s32[1,512]{1,0:T(1,128)S(1)} collective-permute-done((s32[1,512]{1,0:T(1,128)S(1)}, s32[1,512]{1,0:T(1,128)S(1)}, u32[]{:S(2)}, u32[]{:S(2)}) %collective-permute-start.11) | collective-permute-done | bytes 2080 | tf_op jit(solution)/shard_map/ppermute | solution.py:193
  29.6 0.7 %scatter.1 = (f32[256,256]{1,0:T(8,128)S(1)}, bf16[256,256]{1,0:T(8,128)(2,1)S(1)}, bf16[256,256]{1,0:T(8,128)(2,1)S(1)}, bf16[256,256]{1,0:T(8,128)(2,1)S(1)}) custom-call(s32[1]{0:T(128)} %bitcast.7.chip_ref, s32[1,512]{1,0:T(1,128)S(1)} %bitcast.16, s32[1,512]{1,0:T(1,128)S(1)} %collective-permute-done.11.theirs_ref, ...), custom_call_target="tpu_custom_call" | custom-call | flops 536870912 | bytes 1048576 | tf_op jit(solution)/shard_map/scatter/pallas_call | solution.py:273
  30.3 0.5 collective-permute-start.15
  30.8 1.5 %collective-permute-start.14 = (bf16[256,256]{1,0:T(8,128)(2,1)S(1)}, bf16[256,256]{1,0:T(8,128)(2,1)S(1)}, u32[]{:S(2)}, u32[]{:S(2)}) collective-permute-start(bf16[256,256]{1,0:T(8,128)(2,1)S(1)} %get-tuple-element.28), channel_id=1, source_target_pairs={{0,16},{4,20},{8,24},{12,28},{16,0},{20,4},{24,8},{28,12},{1,17},{... | collective-permute-start | bytes 393224 | tf_op jit(solution)/shard_map/ppermute | solution.py:193
  32.4 1.5 %collective-permute-start.13 = (bf16[256,256]{1,0:T(8,128)(2,1)S(1)}, bf16[256,256]{1,0:T(8,128)(2,1)S(1)}, u32[]{:S(2)}, u32[]{:S(2)}) collective-permute-start(bf16[256,256]{1,0:T(8,128)(2,1)S(1)} %get-tuple-element.27), channel_id=1, source_target_pairs={{0,8},{4,12},{8,0},{12,4},{16,24},{20,28},{24,16},{28,20},{1,9},{5... | collective-permute-start | bytes 393224 | tf_op jit(solution)/shard_map/ppermute | solution.py:193
  33.9 3.8 %collective-permute-done.15 = bf16[256,256]{1,0:T(8,128)(2,1)S(1)} collective-permute-done((bf16[256,256]{1,0:T(8,128)(2,1)S(1)}, bf16[256,256]{1,0:T(8,128)(2,1)S(1)}, u32[]{:S(2)}, u32[]{:S(2)}) %collective-permute-start.15) | collective-permute-done | bytes 131104 | tf_op jit(solution)/shard_map/ppermute | solution.py:193
  37.6 1.3 %collective-permute-done.14 = bf16[256,256]{1,0:T(8,128)(2,1)S(1)} collective-permute-done((bf16[256,256]{1,0:T(8,128)(2,1)S(1)}, bf16[256,256]{1,0:T(8,128)(2,1)S(1)}, u32[]{:S(2)}, u32[]{:S(2)}) %collective-permute-start.14) | collective-permute-done | bytes 131104 | tf_op jit(solution)/shard_map/ppermute | solution.py:193
  38.9 0.1 add_convert_fusion.refs_0_
  39.0 1.3 %collective-permute-start.16 = (bf16[256,256]{1,0:T(8,128)(2,1)S(1)}, bf16[256,256]{1,0:T(8,128)(2,1)S(1)}, u32[]{:S(2)}, u32[]{:S(2)}) collective-permute-start(bf16[256,256]{1,0:T(8,128)(2,1)S(1)} %add_convert_fusion.refs_0_), channel_id=1, source_target_pairs={{0,8},{4,12},{8,0},{12,4},{16,24},{20,28},{24,16},{28,20},{1,9},{5... | collective-permute-start | bytes 393224 | tf_op jit(solution)/shard_map/ppermute | solution.py:193
  40.3 0.6 %collective-permute-start.17 = (bf16[256,256]{1,0:T(8,128)(2,1)S(1)}, bf16[256,256]{1,0:T(8,128)(2,1)S(1)}, u32[]{:S(2)}, u32[]{:S(2)}) collective-permute-start(bf16[256,256]{1,0:T(8,128)(2,1)S(1)} %add_convert_fusion.refs_0_), channel_id=1, source_target_pairs={{0,16},{4,20},{8,24},{12,28},{16,0},{20,4},{24,8},{28,12},{1,17},{... | collective-permute-start | bytes 393224 | tf_op jit(solution)/shard_map/ppermute | solution.py:193
  40.9 1.7 %collective-permute-start.18 = (bf16[256,256]{1,0:T(8,128)(2,1)S(1)}, bf16[256,256]{1,0:T(8,128)(2,1)S(1)}, u32[]{:S(2)}, u32[]{:S(2)}) collective-permute-start(bf16[256,256]{1,0:T(8,128)(2,1)S(1)} %add_convert_fusion.refs_0_), channel_id=1, source_target_pairs={{0,24},{4,28},{8,16},{12,20},{16,8},{20,12},{24,0},{28,4},{1,25},{... | collective-permute-start | bytes 393224 | tf_op jit(solution)/shard_map/ppermute | solution.py:193
  42.6 1.3 %collective-permute-start.10 = (f32[4,1024]{1,0:T(4,128)S(1)}, f32[4,1024]{1,0:T(4,128)S(1)}, u32[]{:S(2)}, u32[]{:S(2)}) collective-permute-start(f32[4,1024]{1,0:T(4,128)S(1)} %get-tuple-element.34), channel_id=1, source_target_pairs={{0,24},{4,28},{8,16},{12,20},{16,8},{20,12},{24,0},{28,4},{1,25},{... | collective-permute-start | bytes 49160 | tf_op jit(solution)/shard_map/ppermute | solution.py:193
  43.9 1.4 %collective-permute-start.9 = (f32[4,1024]{1,0:T(4,128)S(1)}, f32[4,1024]{1,0:T(4,128)S(1)}, u32[]{:S(2)}, u32[]{:S(2)}) collective-permute-start(f32[4,1024]{1,0:T(4,128)S(1)} %get-tuple-element.35), channel_id=1, source_target_pairs={{0,16},{4,20},{8,24},{12,28},{16,0},{20,4},{24,8},{28,12},{1,17},{... | collective-permute-start | bytes 49160 | tf_op jit(solution)/shard_map/ppermute | solution.py:193
  45.3 3.1 %collective-permute-done.10 = f32[4,1024]{1,0:T(4,128)S(1)} collective-permute-done((f32[4,1024]{1,0:T(4,128)S(1)}, f32[4,1024]{1,0:T(4,128)S(1)}, u32[]{:S(2)}, u32[]{:S(2)}) %collective-permute-start.10) | collective-permute-done | bytes 16416 | tf_op jit(solution)/shard_map/ppermute | solution.py:193
  48.4 0.5 collective-permute-start.8
  49.0 0.1 pad_add_fusion.1.pos_ref
  49.0 0.0 collective-permute-start.19
  49.1 0.5 collective-permute-start.20
  49.5 0.1 collective-permute-start.21
  49.6 0.4 collective-permute-start.22
  50.1 2.1 %collective-permute-done.8 = f32[4,1024]{1,0:T(4,128)S(1)} collective-permute-done((f32[4,1024]{1,0:T(4,128)S(1)}, f32[4,1024]{1,0:T(4,128)S(1)}, u32[]{:S(2)}, u32[]{:S(2)}) %collective-permute-start.8) | collective-permute-done | bytes 16416 | tf_op jit(solution)/shard_map/ppermute | solution.py:193
  52.2 0.6 %fusion.3 = f32[4,1024]{1,0:T(4,128)} fusion(f32[4,1024]{1,0:T(4,128)S(1)} %collective-permute-done.10, f32[4,1024]{1,0:T(4,128)S(1)} %collective-permute-done.9, f32[4,1024]{1,0:T(4,128)S(1)} %collective-permute-done.8, f32[16,1024]{1,0:T(8,128)S(1)} %fusion.1), kind=kLoop, calls=%fused_computation.7 | loop fusion | flops 12288 | bytes 81920 | tf_op jit(solution)/shard_map/add | solution.py:307
  52.8 2.0 %place.1 = f32[1024,512]{1,0:T(8,128)} custom-call(s32[2]{0:T(128)S(1)} %pad_add_fusion.1.pos_ref, bf16[256,256]{1,0:T(8,128)(2,1)S(1)} %add_convert_fusion.refs_0_, bf16[256,256]{1,0:T(8,128)(2,1)S(1)} %collective-permute-done.16.refs_1_, bf16[256,256]{1,0:T(8,128)(2,1)S(1)} %collective-permute-done.17.refs_2_, ...), custom_call_target="tpu_custom_call" | custom-call | flops 524288 | bytes 3145728 | tf_op jit(solution)/shard_map/place/pallas_call | solution.py:289
  (28 shorter events, 0.1 us)
Async XLA Ops:
  0.6 2.1 %copy-start = (f32[1024,512]{1,0:T(8,128)S(1)}, f32[1024,512]{1,0:T(8,128)}, u32[]{:S(2)}) copy-start(f32[1024,512]{1,0:T(8,128)} %param.8) | copy-start | bytes 6291460
  0.6 5.7 %collective-permute-start = (bf16[16,1024]{1,0:T(8,128)(2,1)}, bf16[16,1024]{1,0:T(8,128)(2,1)S(1)}, u32[]{:S(2)}, u32[]{:S(2)}) collective-permute-start(bf16[16,1024]{1,0:T(8,128)(2,1)} %param.7), channel_id=1, source_target_pairs={{0,4},{4,0},{8,12},{12,8},{16,20},{20,16},{24,28},{28,24},{1,5},{5... | collective-permute-start | bytes 98312 | tf_op jit(solution)/shard_map/ppermute | solution.py:193
  2.7 1.7 %copy-start.1 = (s32[512,32]{0,1:T(8,128)S(1)}, s32[512,32]{0,1:T(8,128)}, u32[]{:S(2)}) copy-start(s32[512,32]{0,1:T(8,128)} %param.13) | copy-start | bytes 196612
  2.7 1.7 %copy-start.2 = (s32[512,1]{0,1:T(1,128)S(1)}, s32[512,1]{0,1:T(1,128)}, u32[]{:S(2)}) copy-start(s32[512,1]{0,1:T(1,128)} %param.9) | copy-start | bytes 6148
  2.7 1.7 %copy-start.3 = (s32[512]{0:T(512)S(1)}, s32[512]{0:T(512)}, u32[]{:S(2)}) copy-start(s32[512]{0:T(512)} %param.10) | copy-start | bytes 6148
  2.8 1.7 %copy-start.4 = (s32[512]{0:T(512)S(1)}, s32[512]{0:T(512)}, u32[]{:S(2)}) copy-start(s32[512]{0:T(512)} %param.12) | copy-start | bytes 6148
  6.3 5.2 %collective-permute-start.1 = (bf16[32,1024]{1,0:T(8,128)(2,1)S(1)}, bf16[32,1024]{1,0:T(8,128)(2,1)S(1)}, u32[]{:S(2)}, u32[]{:S(2)}) collective-permute-start(bf16[32,1024]{1,0:T(8,128)(2,1)S(1)} %constant_dynamic-update-slice_fusion.refs_0_), channel_id=1, source_target_pairs={{0,8},{4,12},{8,0},{12,4},{16,24},{20,28},{24,16},{28,20},{1,9},{5... | collective-permute-start | bytes 196616 | tf_op jit(solution)/shard_map/ppermute | solution.py:193
  8.9 4.3 %collective-permute-start.2 = (bf16[32,1024]{1,0:T(8,128)(2,1)S(1)}, bf16[32,1024]{1,0:T(8,128)(2,1)S(1)}, u32[]{:S(2)}, u32[]{:S(2)}) collective-permute-start(bf16[32,1024]{1,0:T(8,128)(2,1)S(1)} %constant_dynamic-update-slice_fusion.refs_0_), channel_id=1, source_target_pairs={{0,16},{4,20},{8,24},{12,28},{16,0},{20,4},{24,8},{28,12},{1,17},{... | collective-permute-start | bytes 196616 | tf_op jit(solution)/shard_map/ppermute | solution.py:193
  10.5 5.2 %collective-permute-start.3 = (bf16[32,1024]{1,0:T(8,128)(2,1)S(1)}, bf16[32,1024]{1,0:T(8,128)(2,1)S(1)}, u32[]{:S(2)}, u32[]{:S(2)}) collective-permute-start(bf16[32,1024]{1,0:T(8,128)(2,1)S(1)} %constant_dynamic-update-slice_fusion.refs_0_), channel_id=1, source_target_pairs={{0,24},{4,28},{8,16},{12,20},{16,8},{20,12},{24,0},{28,4},{1,25},{... | collective-permute-start | bytes 196616 | tf_op jit(solution)/shard_map/ppermute | solution.py:193
  19.5 8.9 %copy-start.5 = (s32[512]{0:T(512)S(1)}, s32[512]{0:T(512)}, u32[]{:S(2)}) copy-start(s32[512]{0:T(512)} %param.11) | copy-start | bytes 6148
  21.8 1.6 %collective-permute-start.4 = (f32[64,1024]{1,0:T(8,128)S(1)}, f32[64,1024]{1,0:T(8,128)S(1)}, u32[]{:S(2)}, u32[]{:S(2)}) collective-permute-start(f32[64,1024]{1,0:T(8,128)S(1)} %get-tuple-element.23), channel_id=1, source_target_pairs={{0,4},{4,0},{8,12},{12,8},{16,20},{20,16},{24,28},{28,24},{1,5},{5... | collective-permute-start | bytes 786440 | tf_op jit(solution)/shard_map/ppermute | solution.py:193
  21.8 7.8 %collective-permute-start.12 = (bf16[512,256]{1,0:T(8,128)(2,1)S(1)}, bf16[512,256]{1,0:T(8,128)(2,1)S(1)}, u32[]{:S(2)}, u32[]{:S(2)}) collective-permute-start(bf16[512,256]{1,0:T(8,128)(2,1)S(1)} %get-tuple-element.25), channel_id=1, source_target_pairs={{0,4},{4,0},{8,12},{12,8},{16,20},{20,16},{24,28},{28,24},{1,5},{5... | collective-permute-start | bytes 786440 | tf_op jit(solution)/shard_map/ppermute | solution.py:193
  24.0 8.3 %collective-permute-start.7 = (f32[16,1024]{1,0:T(8,128)}, f32[16,1024]{1,0:T(8,128)S(1)}, u32[]{:S(2)}, u32[]{:S(2)}) collective-permute-start(f32[16,1024]{1,0:T(8,128)} %get-tuple-element.31), channel_id=1, source_target_pairs={{0,3},{1,2},{2,1},{3,0},{4,7},{5,6},{6,5},{7,4},{8,11},{9,10},{10,... | collective-permute-start | bytes 196616 | tf_op jit(solution)/shard_map/ppermute | solution.py:196
  27.6 6.2 %collective-permute-start.6 = (f32[16,1024]{1,0:T(8,128)S(1)}, f32[16,1024]{1,0:T(8,128)S(1)}, u32[]{:S(2)}, u32[]{:S(2)}) collective-permute-start(f32[16,1024]{1,0:T(8,128)S(1)} %get-tuple-element.32), channel_id=1, source_target_pairs={{0,2},{1,3},{2,0},{3,1},{4,6},{5,7},{6,4},{7,5},{8,10},{9,11},{10,... | collective-permute-start | bytes 196616 | tf_op jit(solution)/shard_map/ppermute | solution.py:196
  27.6 6.2 %collective-permute-start.5 = (f32[16,1024]{1,0:T(8,128)S(1)}, f32[16,1024]{1,0:T(8,128)S(1)}, u32[]{:S(2)}, u32[]{:S(2)}) collective-permute-start(f32[16,1024]{1,0:T(8,128)S(1)} %get-tuple-element.30), channel_id=1, source_target_pairs={{0,1},{1,0},{2,3},{3,2},{4,5},{5,4},{6,7},{7,6},{8,9},{9,8},{10,11... | collective-permute-start | bytes 196616 | tf_op jit(solution)/shard_map/ppermute | solution.py:196
  28.4 1.2 %collective-permute-start.11 = (s32[1,512]{1,0:T(1,128)S(1)}, s32[1,512]{1,0:T(1,128)S(1)}, u32[]{:S(2)}, u32[]{:S(2)}) collective-permute-start(s32[1,512]{1,0:T(1,128)S(1)} %bitcast.15), channel_id=1, source_target_pairs={{0,4},{4,0},{8,12},{12,8},{16,20},{20,16},{24,28},{28,24},{1,5},{5... | collective-permute-start | bytes 6152 | tf_op jit(solution)/shard_map/ppermute | solution.py:193
  30.3 7.3 %collective-permute-start.15 = (bf16[256,256]{1,0:T(8,128)(2,1)S(1)}, bf16[256,256]{1,0:T(8,128)(2,1)S(1)}, u32[]{:S(2)}, u32[]{:S(2)}) collective-permute-start(bf16[256,256]{1,0:T(8,128)(2,1)S(1)} %get-tuple-element.29), channel_id=1, source_target_pairs={{0,24},{4,28},{8,16},{12,20},{16,8},{20,12},{24,0},{28,4},{1,25},{... | collective-permute-start | bytes 393224 | tf_op jit(solution)/shard_map/ppermute | solution.py:193
  30.8 8.1 %collective-permute-start.14 = (bf16[256,256]{1,0:T(8,128)(2,1)S(1)}, bf16[256,256]{1,0:T(8,128)(2,1)S(1)}, u32[]{:S(2)}, u32[]{:S(2)}) collective-permute-start(bf16[256,256]{1,0:T(8,128)(2,1)S(1)} %get-tuple-element.28), channel_id=1, source_target_pairs={{0,16},{4,20},{8,24},{12,28},{16,0},{20,4},{24,8},{28,12},{1,17},{... | collective-permute-start | bytes 393224 | tf_op jit(solution)/shard_map/ppermute | solution.py:193
  32.4 6.6 %collective-permute-start.13 = (bf16[256,256]{1,0:T(8,128)(2,1)S(1)}, bf16[256,256]{1,0:T(8,128)(2,1)S(1)}, u32[]{:S(2)}, u32[]{:S(2)}) collective-permute-start(bf16[256,256]{1,0:T(8,128)(2,1)S(1)} %get-tuple-element.27), channel_id=1, source_target_pairs={{0,8},{4,12},{8,0},{12,4},{16,24},{20,28},{24,16},{28,20},{1,9},{5... | collective-permute-start | bytes 393224 | tf_op jit(solution)/shard_map/ppermute | solution.py:193
  39.0 10.0 %collective-permute-start.16 = (bf16[256,256]{1,0:T(8,128)(2,1)S(1)}, bf16[256,256]{1,0:T(8,128)(2,1)S(1)}, u32[]{:S(2)}, u32[]{:S(2)}) collective-permute-start(bf16[256,256]{1,0:T(8,128)(2,1)S(1)} %add_convert_fusion.refs_0_), channel_id=1, source_target_pairs={{0,8},{4,12},{8,0},{12,4},{16,24},{20,28},{24,16},{28,20},{1,9},{5... | collective-permute-start | bytes 393224 | tf_op jit(solution)/shard_map/ppermute | solution.py:193
  40.3 9.2 %collective-permute-start.17 = (bf16[256,256]{1,0:T(8,128)(2,1)S(1)}, bf16[256,256]{1,0:T(8,128)(2,1)S(1)}, u32[]{:S(2)}, u32[]{:S(2)}) collective-permute-start(bf16[256,256]{1,0:T(8,128)(2,1)S(1)} %add_convert_fusion.refs_0_), channel_id=1, source_target_pairs={{0,16},{4,20},{8,24},{12,28},{16,0},{20,4},{24,8},{28,12},{1,17},{... | collective-permute-start | bytes 393224 | tf_op jit(solution)/shard_map/ppermute | solution.py:193
  40.9 8.7 %collective-permute-start.18 = (bf16[256,256]{1,0:T(8,128)(2,1)S(1)}, bf16[256,256]{1,0:T(8,128)(2,1)S(1)}, u32[]{:S(2)}, u32[]{:S(2)}) collective-permute-start(bf16[256,256]{1,0:T(8,128)(2,1)S(1)} %add_convert_fusion.refs_0_), channel_id=1, source_target_pairs={{0,24},{4,28},{8,16},{12,20},{16,8},{20,12},{24,0},{28,4},{1,25},{... | collective-permute-start | bytes 393224 | tf_op jit(solution)/shard_map/ppermute | solution.py:193
  42.6 5.8 %collective-permute-start.10 = (f32[4,1024]{1,0:T(4,128)S(1)}, f32[4,1024]{1,0:T(4,128)S(1)}, u32[]{:S(2)}, u32[]{:S(2)}) collective-permute-start(f32[4,1024]{1,0:T(4,128)S(1)} %get-tuple-element.34), channel_id=1, source_target_pairs={{0,24},{4,28},{8,16},{12,20},{16,8},{20,12},{24,0},{28,4},{1,25},{... | collective-permute-start | bytes 49160 | tf_op jit(solution)/shard_map/ppermute | solution.py:193
  43.9 5.1 %collective-permute-start.9 = (f32[4,1024]{1,0:T(4,128)S(1)}, f32[4,1024]{1,0:T(4,128)S(1)}, u32[]{:S(2)}, u32[]{:S(2)}) collective-permute-start(f32[4,1024]{1,0:T(4,128)S(1)} %get-tuple-element.35), channel_id=1, source_target_pairs={{0,16},{4,20},{8,24},{12,28},{16,0},{20,4},{24,8},{28,12},{1,17},{... | collective-permute-start | bytes 49160 | tf_op jit(solution)/shard_map/ppermute | solution.py:193
  48.4 3.7 %collective-permute-start.8 = (f32[4,1024]{1,0:T(4,128)S(1)}, f32[4,1024]{1,0:T(4,128)S(1)}, u32[]{:S(2)}, u32[]{:S(2)}) collective-permute-start(f32[4,1024]{1,0:T(4,128)S(1)} %get-tuple-element.33), channel_id=1, source_target_pairs={{0,8},{4,12},{8,0},{12,4},{16,24},{20,28},{24,16},{28,20},{1,9},{5... | collective-permute-start | bytes 49160 | tf_op jit(solution)/shard_map/ppermute | solution.py:193
  49.0 3.7 %collective-permute-start.19 = (bf16[256,256]{1,0:T(8,128)(2,1)S(1)}, bf16[256,256]{1,0:T(8,128)(2,1)S(1)}, u32[]{:S(2)}, u32[]{:S(2)}) collective-permute-start(bf16[256,256]{1,0:T(8,128)(2,1)S(1)} %add_convert_fusion.refs_0_), channel_id=1, source_target_pairs={{0,4},{4,0},{8,12},{12,8},{16,20},{20,16},{24,28},{28,24},{1,5},{5... | collective-permute-start | bytes 393224 | tf_op jit(solution)/shard_map/ppermute | solution.py:193
  49.1 3.7 %collective-permute-start.20 = (bf16[256,256]{1,0:T(8,128)(2,1)S(1)}, bf16[256,256]{1,0:T(8,128)(2,1)S(1)}, u32[]{:S(2)}, u32[]{:S(2)}) collective-permute-start(bf16[256,256]{1,0:T(8,128)(2,1)S(1)} %collective-permute-done.16.refs_1_), channel_id=1, source_target_pairs={{0,4},{4,0},{8,12},{12,8},{16,20},{20,16},{24,28},{28,24},{1,5},{5... | collective-permute-start | bytes 393224 | tf_op jit(solution)/shard_map/ppermute | solution.py:193
  49.5 3.2 %collective-permute-start.21 = (bf16[256,256]{1,0:T(8,128)(2,1)S(1)}, bf16[256,256]{1,0:T(8,128)(2,1)S(1)}, u32[]{:S(2)}, u32[]{:S(2)}) collective-permute-start(bf16[256,256]{1,0:T(8,128)(2,1)S(1)} %collective-permute-done.17.refs_2_), channel_id=1, source_target_pairs={{0,4},{4,0},{8,12},{12,8},{16,20},{20,16},{24,28},{28,24},{1,5},{5... | collective-permute-start | bytes 393224 | tf_op jit(solution)/shard_map/ppermute | solution.py:193
  49.6 3.1 %collective-permute-start.22 = (bf16[256,256]{1,0:T(8,128)(2,1)S(1)}, bf16[256,256]{1,0:T(8,128)(2,1)S(1)}, u32[]{:S(2)}, u32[]{:S(2)}) collective-permute-start(bf16[256,256]{1,0:T(8,128)(2,1)S(1)} %collective-permute-done.18.refs_3_), channel_id=1, source_target_pairs={{0,4},{4,0},{8,12},{12,8},{16,20},{20,16},{24,28},{28,24},{1,5},{5... | collective-permute-start | bytes 393224 | tf_op jit(solution)/shard_map/ppermute | solution.py:193

commit v2 on v0

v2 whole, which is shorter than its diff:
```python
import functools

import jax
import jax.numpy as jnp
from jax import lax
from jax.experimental import pallas as pl
from jax.experimental.pallas import tpu as pltpu
from jax.sharding import PartitionSpec as P

F32 = jnp.float32
BF16 = jnp.bfloat16
I32 = jnp.int32
VMEM_BYTES = 16 * 1024 * 1024
NT = (((1,), (1,)), ((), ()))

SIN_C = (0.9999999957, -0.1666665799, 0.008333051133, -0.0001980908535, 2.605256611e-06)
COS_C = (0.9999999998, -0.4999999936, 0.04166663628, -0.00138883618, 2.476018568e-05, -2.605198025e-07)


def params():
    return pltpu.CompilerParams(vmem_limit_bytes=VMEM_BYTES)


def cost(flops, nbytes, trans=0):
    return pl.CostEstimate(flops=flops, bytes_accessed=nbytes, transcendentals=trans)


def horner(coeffs, y):
    acc = jnp.full_like(y, coeffs[-1])
    for c in coeffs[-2::-1]:
        acc = acc * y + c
    return acc


def prepare_kernel(rel_hbm, phases_hbm, owner_hbm, row_hbm, tail_hbm, known_hbm, cos_ref, sin_ref, code_ref, rel_ref, phases_ref, owner_ref, row_ref, tail_ref, known_ref, sems, *, rows_ent, owner_rows):
    n = cos_ref.shape[0]
    copies = [
        pltpu.make_async_copy(src, dst, sems.at[i])
        for i, (src, dst) in enumerate(
            [
                (known_hbm, known_ref),
                (owner_hbm, owner_ref),
                (row_hbm, row_ref),
                (tail_hbm, tail_ref),
                (rel_hbm, rel_ref),
                (phases_hbm, phases_ref),
            ]
        )
    ]
    for copy in copies:
        copy.start()
    for copy in copies[:4]:
        copy.wait()
    flip = lax.axis_index("ent") * rows_ent
    entities = code_ref.shape[1]
    lanes = min(128, n)
    sub = lax.broadcasted_iota(I32, (8, lanes), 0)
    for start in range(0, n, lanes):
        at = slice(start, start + lanes)
        heads = (owner_ref[:, at] * owner_rows + row_ref[:, at]) ^ flip
        tails = tail_ref[:, at] ^ flip
        known = known_ref[:, at] ^ flip
        bits = lax.shift_left(jnp.ones_like(known), known & 31)
        word_of = lax.shift_right_logical(known, 5)
        pieces = []
        for w in range(entities // 32):
            hit = jnp.where(word_of == w, bits, 0)
            word = hit[0:8]
            for r in range(8, hit.shape[0], 8):
                word = word | hit[r : r + 8]
            for shift in (4, 2, 1):
                word = word | pltpu.roll(word, shift, 0)
            for g in range(4):
                e = sub + (32 * w + 8 * g)
                listed = lax.shift_right_logical(word, sub + 8 * g) & 1
                target = jnp.where(e == tails, 1, 0)
                head = jnp.where(e == heads, 4, 0)
                pieces.append((listed & (1 - target)) | (target * 2) | head)
        code_ref[at, :] = jnp.concatenate(pieces, axis=0).T

    for copy in copies[4:]:
        copy.wait()

    half = cos_ref.shape[1]
    place = lax.broadcasted_iota(I32, (8, half), 0)
    for start in range(0, n, 8):
        angle = jnp.broadcast_to(phases_ref[pl.ds(rel_ref[start], 1), :], (8, half))
        for j in range(1, 8):
            angle = jnp.where(place == j, jnp.broadcast_to(phases_ref[pl.ds(rel_ref[start + j], 1), :], (8, half)), angle)
        u = angle * 0.5
        y = u * u
        s = u * horner(SIN_C, y)
        t = 2.0 * s
        sin_ref[start : start + 8, :] = t * horner(COS_C, y)
        cos_ref[start : start + 8, :] = 1.0 - t * s


def score_kernel(*refs, peers, block):
    table_refs = refs[:peers]
    cos_ref, sin_ref, code_ref, keep_ref, send_ref, w_ref, q_ref = refs[peers:]
    n, half = cos_ref.shape
    quarter = half // 2
    tab = jnp.concatenate([r[...] for r in table_refs], axis=0)
    f = tab.astype(F32)
    norm = jnp.sum(f * f, axis=1, keepdims=True)
    tsq = jnp.broadcast_to(norm, (norm.shape[0], 128)).T[0:1]
    even = lax.axis_index("ent") % 2 == 0
    for start in range(0, n, block):
        at = slice(start, start + block)
        cosine = cos_ref[at, :]
        sine = sin_ref[at, :]
        code = code_ref[at, :]
        hot = jnp.where((code & 4) != 0, 1.0, 0.0).astype(BF16)
        head = jnp.dot(hot, tab, preferred_element_type=F32)
        hre = head[:, :half]
        him = head[:, half:]
        qre = hre * cosine - him * sine
        qim = hre * sine + him * cosine
        q = jnp.concatenate([qre, qim], axis=1).astype(BF16)
        q_ref[at, :] = q
        qf = q.astype(F32)
        qsq = jnp.sum(qf * qf, axis=1, keepdims=True)
        cross = lax.dot_general(q, tab, NT, preferred_element_type=F32)
        scores = 2.0 * cross - qsq - tsq
        masked = (code & 1) != 0
        target = jnp.where((code & 2) != 0, 1.0, 0.0)
        row_max = jnp.max(jnp.where(masked, -jnp.inf, scores), axis=1, keepdims=True)
        raw = jnp.where(masked, 0.0, jnp.exp(scores - row_max))
        prob = raw / jnp.sum(raw, axis=1, keepdims=True)
        w = (prob - target).astype(BF16)
        w_ref[at, :] = w
        dq = jnp.dot(w + w, tab, preferred_element_type=F32)
        dangle = (qre * dq[:, half:] - qim * dq[:, :half]).astype(BF16)
        first = dangle[:, :quarter]
        second = dangle[:, quarter:]
        keep_ref[at, :] = jnp.where(even, first, second)
        send_ref[at, :] = jnp.where(even, second, first)


def entity_kernel(w_ref, q_ref, cos_ref, sin_ref, owner_ref, row_ref, *refs, peers, n_rel, owner_rows, block):
    table_refs = refs[:peers]
    keep_ref, send_ref, hr = refs[peers:]
    n, entities = w_ref.shape
    half = cos_ref.shape[1]
    tab = jnp.concatenate([r[...] for r in table_refs], axis=0)
    for start in range(0, n, block):
        at = slice(start, start + block)
        w = w_ref[at, :]
        dq = jnp.dot(w + w, tab, preferred_element_type=F32)
        cosine = cos_ref[at, :]
        sine = sin_ref[at, :]
        dre = dq[:, :half]
        dim = dq[:, half:]
        hr[at, :half] = (dre * cosine + dim * sine).astype(BF16)
        hr[at, half:] = (dim * cosine - dre * sine).astype(BF16)

    flip = lax.axis_index("ent") * (n_rel * owner_rows)
    me_rel = lax.axis_index("rel")

    def row_id(i):
        at = i // owner_rows
        span = 2 * peers * n_rel
        rel_bit = jnp.zeros_like(i)
        span //= 2
        ent_bit = (at // span) & 1
        for bit in range(n_rel.bit_length() - 1):
            span //= 2
            rel_bit = rel_bit | (((at // span) & 1) << bit)
        for bit in range(1, peers.bit_length()):
            span //= 2
            ent_bit = ent_bit | (((at // span) & 1) << bit)
        return (ent_bit * n_rel + (rel_bit ^ me_rel)) * owner_rows + i % owner_rows

    e = row_id(lax.broadcasted_iota(I32, (entities, entities), 0))
    pick = jnp.where(e == lax.broadcasted_iota(I32, (entities, entities), 1), 1.0, 0.0).astype(BF16)
    wtf = lax.dot_general(pick, w_ref[...], NT, preferred_element_type=F32)
    counts = jnp.sum(wtf, axis=1, keepdims=True)
    heads = (owner_ref[...] * owner_rows + row_ref[...]) ^ flip
    eh = row_id(lax.broadcasted_iota(I32, (entities, n), 0))
    hot = jnp.where(eh == heads, 1.0, 0.0).astype(BF16)
    picked = jnp.dot(pick, tab, preferred_element_type=F32)
    cross = jnp.dot(wtf.astype(BF16), q_ref[...], preferred_element_type=F32)
    total = 2.0 * (cross - counts * picked) + jnp.dot(hot, hr[...], preferred_element_type=F32)
    keep_ref[...] = total[: entities // 2]
    send_ref[...] = total[entities // 2 :]


def scatter_kernel(mine_ref, theirs_ref, keep_ref, got_ref, *outs, peers, rows):
    chip = lax.axis_index("ent") // 2
    ids = jnp.concatenate([mine_ref[...], theirs_ref[...]], axis=1)
    d = jnp.concatenate([keep_ref[...], got_ref[...]], axis=0)
    n = ids.shape[1]
    iota = lax.broadcasted_iota(I32, (rows, n), 0)
    for p in range(peers):
        base = (chip ^ p) * rows
        hot = jnp.where(iota == ids - base, 1.0, 0.0).astype(BF16)
        outs[p][...] = jnp.dot(hot, d, preferred_element_type=F32).astype(outs[p].dtype)


def place_kernel(src_ref, *refs, side, peers, rows):
    if side:
        left_ref, right_ref, _, sum_ref, out_hbm, buf, sems = refs
    else:
        out_hbm, buf, sems = refs
    quarter = src_ref.shape[1]
    me = lax.axis_index("ent")
    chip, par = me // 2, me % 2
    col = pl.multiple_of((par ^ side) * quarter, quarter)
    copies = []
    for p in range(peers):
        row = pl.multiple_of((chip ^ p) * rows, rows)
        at = slice(p * rows, (p + 1) * rows)
        buf[at, :] = src_ref[at, :].astype(F32)
        copy = pltpu.make_async_copy(buf.at[at, :], out_hbm.at[pl.ds(row, rows), pl.ds(col, quarter)], sems.at[p])
        copy.start()
        copies.append(copy)
    if side:
        sum_ref[...] = left_ref[...] + right_ref[...]
    for copy in copies:
        copy.wait()


def local(entity_table, phases, head_owner, head_row, relation, tail_ids, known_tails):
    n_ent = lax.axis_size("ent")
    n_rel = lax.axis_size("rel")
    peers = n_ent // 2
    n = head_row.shape[0]
    rows_ent, width = entity_table.shape
    owner_rows = rows_ent // n_rel
    entities = rows_ent * n_ent
    half = width // 2
    quarter = half // 2
    rels = phases.shape[0]
    rows = rels // peers
    block = min(128, n)

    def swap(x, k):
        return lax.ppermute(x, "ent", [(i, i ^ k) for i in range(n_ent)])

    def swap_rel(x, k):
        return lax.ppermute(x, "rel", [(i, i ^ k) for i in range(n_rel)])

    hbm = pl.BlockSpec(memory_space=pltpu.HBM)

    owner_l = head_owner.reshape(1, n)
    row_l = head_row.reshape(1, n)
    rel_l = relation.reshape(1, n)
    tail_l = tail_ids.reshape(1, n)
    known_l = known_tails.T
    mate, rel_mate = lax.optimization_barrier((swap(entity_table, 1), swap(rel_l, 1)))
    pair = jnp.concatenate([entity_table, mate], axis=0)
    tables = [pair] + [swap(pair, 2 * p) for p in range(1, peers)]

    vm = pl.BlockSpec(memory_space=pltpu.VMEM)
    cosine, sine, code = pl.pallas_call(
        functools.partial(prepare_kernel, rows_ent=rows_ent, owner_rows=owner_rows),
        in_specs=[hbm] * 6,
        out_specs=[vm] * 3,
        scratch_shapes=[
            pltpu.SMEM((n,), I32),
            pltpu.VMEM((rels, half), F32),
            pltpu.VMEM((1, n), I32),
            pltpu.VMEM((1, n), I32),
            pltpu.VMEM((1, n), I32),
            pltpu.VMEM(known_l.shape, I32),
            pltpu.SemaphoreType.DMA((6,)),
        ],
        out_shape=[
            jax.ShapeDtypeStruct((n, half), F32),
            jax.ShapeDtypeStruct((n, half), F32),
            jax.ShapeDtypeStruct((n, entities), I32),
        ],
        compiler_params=params(),
        cost_estimate=cost(30 * n * half, 12 * n * half),
        name="prepare",
    )(*[pltpu.with_memory_space_constraint(x, pltpu.HBM) for x in (relation, phases, owner_l, row_l, tail_l, known_l)])

    keep, send, w, q = pl.pallas_call(
        functools.partial(score_kernel, peers=peers, block=block),
        in_specs=[vm] * (peers + 3),
        out_specs=[vm] * 4,
        out_shape=[
            jax.ShapeDtypeStruct((n, quarter), BF16),
            jax.ShapeDtypeStruct((n, quarter), BF16),
            jax.ShapeDtypeStruct((n, entities), BF16),
            jax.ShapeDtypeStruct((n, width), BF16),
        ],
        compiler_params=params(),
        cost_estimate=cost(6 * n * entities * width, 12 * n * width),
        name="score",
    )(*tables, cosine, sine, code)

    got = swap(send, 1)
    ent_keep, ent_send = pl.pallas_call(
        functools.partial(entity_kernel, peers=peers, n_rel=n_rel, owner_rows=owner_rows, block=block),
        in_specs=[vm] * (6 + peers),
        out_specs=[vm] * 2,
        out_shape=[jax.ShapeDtypeStruct((entities // 2, width), F32)] * 2,
        scratch_shapes=[pltpu.VMEM((n, width), BF16)],
        compiler_params=params(),
        cost_estimate=cost(6 * n * entities * width, 4 * n * width + 4 * entities * width),
        name="entity",
    )(w, q, cosine, sine, owner_l, row_l, *tables)

    parts = pl.pallas_call(
        functools.partial(scatter_kernel, peers=peers, rows=rows),
        in_specs=[vm] * 4,
        out_specs=[vm] * peers,
        out_shape=[jax.ShapeDtypeStruct((rows, quarter), F32 if p == 0 else BF16) for p in range(peers)],
        compiler_params=params(),
        cost_estimate=cost(4 * n * rels * quarter, 4 * n * quarter + 2 * rels * quarter),
        name="scatter",
    )(rel_l, rel_mate, keep, got)

    *parts, ent_keep, ent_send = lax.optimization_barrier((*parts, ent_keep, ent_send))

    received = [swap(parts[p], 2 * p) for p in range(1, peers)]
    total = parts[0]
    for part in received:
        total = total + part.astype(F32)
    final = total.astype(BF16)

    def fold(x, move, sent):
        middle = x.shape[0] // 2
        return x[:middle], move(x[middle:].astype(sent)).astype(F32)

    left, right = fold(ent_keep + swap(ent_send, 1), lambda x: swap_rel(x, 1), BF16)
    final, left, right = lax.optimization_barrier((final, left, right))
    for bit in range(1, n_rel.bit_length() - 1):
        left, right = fold(left + right, lambda x: swap_rel(x, 1 << bit), BF16)
    for bit in range(1, peers.bit_length() - 1):
        left, right = fold(left + right, lambda x: swap(x, 1 << bit), F32)

    mine = jnp.concatenate([final] + [swap(final, 2 * p) for p in range(1, peers)], axis=0)
    mine, left, right = lax.optimization_barrier((mine, left, right))
    left, right = fold(left + right, lambda x: swap(x, peers), F32)
    theirs = swap(mine, 1)

    def place(side, *args):
        shape = jax.ShapeDtypeStruct((rels, half), F32)
        return pl.pallas_call(
            functools.partial(place_kernel, side=side, peers=peers, rows=rows),
            in_specs=[vm] * 3 + [hbm] if side else [vm],
            out_specs=(vm, hbm) if side else hbm,
            out_shape=(jax.ShapeDtypeStruct((owner_rows, width), F32), shape) if side else shape,
            scratch_shapes=[pltpu.VMEM((rels, quarter), F32), pltpu.SemaphoreType.DMA((peers,))],
            input_output_aliases={3: 1} if side else {},
            compiler_params=params(),
            cost_estimate=cost(rels * half, 6 * rels * half),
            name="place",
        )(*args)

    return place(1, theirs, left, right, place(0, mine))


def solution(mesh):
    in_specs = (
        P("ent", None),
        P("rel", None),
        P(("ent", "rel"), None),
        P(("ent", "rel")),
        P(("ent", "rel")),
        P(("ent", "rel")),
        P(("ent", "rel"), None),
    )
    out_specs = (P(("ent", "rel"), None), P("rel", None))
    return jax.shard_map(local, mesh=mesh, in_specs=in_specs, out_specs=out_specs, check_vma=False)
```

time: 224 us -> 42.9 us (0.19)
  waiting for transfers between devices: 117 us -> 12 us
  local copies, waits for them, and re-layouts: 31.2 us -> 0.82 us
  other arithmetic: 23.9 us -> 0.17 us
  between operations: 14.2 us -> 0.81 us
  Pallas kernels: 0 us -> 10.4 us
  blocking collectives: 9.99 us -> 0 us
  matrix products: 7.6 us -> 0 us
    unnamed x3 -> x0, waiting for transfers between devices: 56.3 us -> none
    reduce_scatter x1 -> x0, waiting for transfers between devices: 32 us -> none  [local(): by_group = lax.psum_scatter(whole, 'rel', scatter_dimension=1, tiled=True)]
    all_to_all x4 -> x0, waiting for transfers between devices: 29.1 us -> none  [the longest x1 22.3 us: local(): lax.all_to_all(send_rows.reshape(n_ent, n_rel, capacity, width), 'ent', s...]
    all_to_all x4 -> x0, starting transfers between devices: 18.9 us -> none  [the longest x1 5.17 us: local(): lax.all_to_all(send_labels.reshape(n_ent, n_rel, capacity), 'ent', split_...]
    ppermute x0 -> x18, starting transfers between devices: none -> 18.5 us  [the longest x16 14.2 us: swap(): return lax.ppermute(x, 'ent', [(i, i ^ k) for i in range(n_ent)])]
    ppermute x0 -> x18, waiting for transfers between devices: none -> 12 us  [the longest x16 12 us: swap(): return lax.ppermute(x, 'ent', [(i, i ^ k) for i in range(n_ent)])]
    pallas_call x0 -> x6, Pallas kernels: none -> 10.4 us  [the longest x1 3.01 us: local(): pl.pallas_call(functools.partial(prepare_kernel, rows_ent=rows_ent, owner...]
    all_gather x1 -> x0, blocking collectives: 9.99 us -> none  [local(): table_all = lax.all_gather(entity_table, 'ent', axis=0, tiled=True)]
  transfers between devices with their start and end apart: 6 -> 18, of which waited for: 5 -> 12; matrix products, arithmetic and copies ran while one was open for 23% -> 2% of each run, Pallas kernels for 0% -> 12%
where the time goes in v2:
time: 42.9 us; the launch traced here: 42.7 us
  starting transfers between devices  18.5 us (43%)
  waiting for transfers between devices  12 us (28%)
  Pallas kernels  10.4 us (24%)
  local copies, waits for them, and re-layouts  0.82 us (2%)
  between operations  0.81 us (2%)
    ppermute x16, starting transfers between devices, swap(): return lax.ppermute(x, 'ent', [(i, i ^ k) for i in range(n_ent)])  14.2 us
    ppermute x16, waiting for transfers between devices, swap(): return lax.ppermute(x, 'ent', [(i, i ^ k) for i in range(n_ent)])  12 us
    ppermute x2, starting transfers between devices, swap_rel(): return lax.ppermute(x, 'rel', [(i, i ^ k) for i in range(n_rel)])  4.29 us
    pallas_call x1, Pallas kernels, local(): pl.pallas_call(functools.partial(prepare_kernel, rows_ent=rows_ent, owner...  3.01 us
    pallas_call x1, Pallas kernels, local(): pl.pallas_call(functools.partial(score_kernel, peers=peers, block=block),...  2.92 us
    pallas_call x2, Pallas kernels, place(): pl.pallas_call(functools.partial(place_kernel, side=side, peers=peers, ro...  2.63 us
    pallas_call x1, Pallas kernels, local(): pl.pallas_call(functools.partial(entity_kernel, peers=peers, n_rel=n_rel,...  1.15 us
  transfers between devices with their start and end apart: 18, of which 12 were waited for; matrix products, arithmetic and copies ran while one was open for 2% of the time, Pallas kernels for 12%

profile of v2, /device:TPU:0, one launch (start us, length us, event | category | flops | bytes accessed | tf_op | source)
XLA Modules:
  0.0 42.7 jit_solution(12147231686074673529)
XLA Ops:
  0.6 0.5 %collective-permute-start.1 = (s32[1,512]{1,0:T(1,128)}, s32[1,512]{1,0:T(1,128)S(1)}, u32[]{:S(2)}, u32[]{:S(2)}) collective-permute-start(s32[1,512]{1,0:T(1,128)} %bitcast.9), channel_id=1, source_target_pairs={{0,4},{4,0},{8,12},{12,8},{16,20},{20,16},{24,28},{28,24},{1,5},{5... | collective-permute-start | bytes 6152 | tf_op jit(solution)/shard_map/ppermute | solution.py:238
  1.1 0.1 collective-permute-start
  1.2 0.8 %constant_dynamic-update-slice_fusion.1 = bf16[32,1024]{1,0:T(8,128)(2,1)S(1)} fusion(bf16[16,1024]{1,0:T(8,128)(2,1)} %param.7), kind=kLoop, calls=%fused_computation.6 | loop fusion | bytes 65536
  2.0 0.2 collective-permute-done.1.theirs_ref
  2.2 0.4 collective-permute-done
  2.6 3.6 %collective-permute-start.4 = (bf16[32,1024]{1,0:T(8,128)(2,1)S(1)}, bf16[32,1024]{1,0:T(8,128)(2,1)S(1)}, u32[]{:S(2)}, u32[]{:S(2)}) collective-permute-start(bf16[32,1024]{1,0:T(8,128)(2,1)S(1)} %constant_dynamic-update-slice_fusion.refs_0_), channel_id=1, source_target_pairs={{0,24},{4,28},{8,16},{12,20},{16,8},{20,12},{24,0},{28,4},{1,25},{... | collective-permute-start | bytes 196616 | tf_op jit(solution)/shard_map/ppermute | solution.py:238
  6.2 0.5 %collective-permute-start.3 = (bf16[32,1024]{1,0:T(8,128)(2,1)S(1)}, bf16[32,1024]{1,0:T(8,128)(2,1)S(1)}, u32[]{:S(2)}, u32[]{:S(2)}) collective-permute-start(bf16[32,1024]{1,0:T(8,128)(2,1)S(1)} %constant_dynamic-update-slice_fusion.refs_0_), channel_id=1, source_target_pairs={{0,16},{4,20},{8,24},{12,28},{16,0},{20,4},{24,8},{28,12},{1,17},{... | collective-permute-start | bytes 196616 | tf_op jit(solution)/shard_map/ppermute | solution.py:238
  6.7 0.1 collective-permute-start.2
  6.7 3.0 %prepare.1 = (f32[512,512]{1,0:T(8,128)S(1)}, f32[512,512]{1,0:T(8,128)S(1)}, s32[512,128]{1,0:T(8,128)S(1)}) custom-call(s32[512]{0:T(512)} %rel_hbm.1, f32[1024,512]{1,0:T(8,128)} %phases_hbm.1, s32[1,512]{1,0:T(1,128)} %bitcast.5, s32[1,512]{1,0:T(1,128)} %bitcast.7, s32[1,512]{1,0:T(1,128)} %bitcast.12, s32[32,512]{1,0:T(8,128)} %bitcast.11), custom_call_target="tpu_custom_call" | custom-call | flops 7864320 | bytes 3145728 | tf_op jit(solution)/shard_map/prepare/pallas_call | solution.py:255
  9.8 0.0 collective-permute-done.4.refs_3_
  9.8 0.7 %collective-permute-done.3.refs_2_ = bf16[32,1024]{1,0:T(8,128)(2,1)S(1)} collective-permute-done((bf16[32,1024]{1,0:T(8,128)(2,1)S(1)}, bf16[32,1024]{1,0:T(8,128)(2,1)S(1)}, u32[]{:S(2)}, u32[]{:S(2)}) %collective-permute-start.3) | collective-permute-done | bytes 65568 | tf_op jit(solution)/shard_map/ppermute | solution.py:238
  10.4 0.5 %collective-permute-done.2.refs_1_ = bf16[32,1024]{1,0:T(8,128)(2,1)S(1)} collective-permute-done((bf16[32,1024]{1,0:T(8,128)(2,1)S(1)}, bf16[32,1024]{1,0:T(8,128)(2,1)S(1)}, u32[]{:S(2)}, u32[]{:S(2)}) %collective-permute-start.2) | collective-permute-done | bytes 65568 | tf_op jit(solution)/shard_map/ppermute | solution.py:238
  10.9 2.9 %score.1 = (bf16[512,256]{1,0:T(8,128)(2,1)S(1)}, bf16[512,256]{1,0:T(8,128)(2,1)S(1)}, bf16[512,128]{1,0:T(8,128)(2,1)S(1)}, bf16[512,1024]{1,0:T(8,128)(2,1)S(1)}) custom-call(bf16[32,1024]{1,0:T(8,128)(2,1)S(1)} %constant_dynamic-update-slice_fusion.refs_0_, bf16[32,1024]{1,0:T(8,128)(2,1)S(1)} %collective-permute-done.2.refs_1_, ...), custom_call_target="tpu_custom_call" | custom-call | flops 402653184 | bytes 6291456 | tf_op jit(solution)/shard_map/score/pallas_call | solution.py:278
  13.9 0.0 copy-start.2
  13.9 0.1 collective-permute-start.5
  14.0 0.0 copy-done
  14.0 0.0 copy-done.1
  14.0 1.2 %entity.1 = (f32[64,1024]{1,0:T(8,128)S(1)}, f32[64,1024]{1,0:T(8,128)S(1)}) custom-call(bf16[512,128]{1,0:T(8,128)(2,1)S(1)} %get-tuple-element.40.w_ref, bf16[512,1024]{1,0:T(8,128)(2,1)S(1)} %get-tuple-element.41.q_ref, f32[512,512]{1,0:T(8,128)S(1)} %get-tuple-element.31.refs_4_.cos_ref, f32[512,512]{1,0:T(8,128)S(1)} %get-tuple-element.32.refs_5_.sin_ref, ...), custom_call_target="tpu_custom_call" | custom-call | flops 402653184 | bytes 2621440 | tf_op jit(solution)/shard_map/entity/pallas_call | solution.py:294
  15.1 0.3 collective-permute-done.5.got_ref
  15.5 0.0 copy-done.2
  15.5 0.7 %scatter.1 = (f32[256,256]{1,0:T(8,128)S(1)}, bf16[256,256]{1,0:T(8,128)(2,1)S(1)}, bf16[256,256]{1,0:T(8,128)(2,1)S(1)}, bf16[256,256]{1,0:T(8,128)(2,1)S(1)}) custom-call(s32[1,512]{1,0:T(1,128)S(1)} %bitcast.10, s32[1,512]{1,0:T(1,128)S(1)} %collective-permute-done.1.theirs_ref, bf16[512,256]{1,0:T(8,128)(2,1)S(1)} %get-tuple-element.34.keep_ref, ...), custom_call_target="tpu_custom_call" | custom-call | flops 536870912 | bytes 1048576 | tf_op jit(solution)/shard_map/scatter/pallas_call | solution.py:305
  16.2 0.2 collective-permute-start.9
  16.4 1.0 %collective-permute-start.6 = (bf16[256,256]{1,0:T(8,128)(2,1)S(1)}, bf16[256,256]{1,0:T(8,128)(2,1)S(1)}, u32[]{:S(2)}, u32[]{:S(2)}) collective-permute-start(bf16[256,256]{1,0:T(8,128)(2,1)S(1)} %get-tuple-element.45), channel_id=1, source_target_pairs={{0,8},{4,12},{8,0},{12,4},{16,24},{20,28},{24,16},{28,20},{1,9},{5... | collective-permute-start | bytes 393224 | tf_op jit(solution)/shard_map/ppermute | solution.py:238
  17.4 1.4 %collective-permute-start.7 = (bf16[256,256]{1,0:T(8,128)(2,1)S(1)}, bf16[256,256]{1,0:T(8,128)(2,1)S(1)}, u32[]{:S(2)}, u32[]{:S(2)}) collective-permute-start(bf16[256,256]{1,0:T(8,128)(2,1)S(1)} %get-tuple-element.46), channel_id=1, source_target_pairs={{0,16},{4,20},{8,24},{12,28},{16,0},{20,4},{24,8},{28,12},{1,17},{... | collective-permute-start | bytes 393224 | tf_op jit(solution)/shard_map/ppermute | solution.py:238
  18.8 1.2 %collective-permute-start.8 = (bf16[256,256]{1,0:T(8,128)(2,1)S(1)}, bf16[256,256]{1,0:T(8,128)(2,1)S(1)}, u32[]{:S(2)}, u32[]{:S(2)}) collective-permute-start(bf16[256,256]{1,0:T(8,128)(2,1)S(1)} %get-tuple-element.47), channel_id=1, source_target_pairs={{0,24},{4,28},{8,16},{12,20},{16,8},{20,12},{24,0},{28,4},{1,25},{... | collective-permute-start | bytes 393224 | tf_op jit(solution)/shard_map/ppermute | solution.py:238
  19.9 0.0 collective-permute-done.9
  20.0 1.6 %collective-permute-start.10 = (bf16[32,1024]{1,0:T(8,128)(2,1)S(1)}, bf16[32,1024]{1,0:T(8,128)(2,1)S(1)}, u32[]{:S(2)}, u32[]{:S(2)}) collective-permute-start(bf16[32,1024]{1,0:T(8,128)(2,1)S(1)} %slice.45), channel_id=1, source_target_pairs={{0,1},{1,0},{2,3},{3,2},{4,5},{5,4},{6,7},{7,6},{8,9},{9,8},{10,11... | collective-permute-start | bytes 196616 | tf_op jit(solution)/shard_map/ppermute | solution.py:241
  21.6 1.1 %collective-permute-done.6 = bf16[256,256]{1,0:T(8,128)(2,1)S(1)} collective-permute-done((bf16[256,256]{1,0:T(8,128)(2,1)S(1)}, bf16[256,256]{1,0:T(8,128)(2,1)S(1)}, u32[]{:S(2)}, u32[]{:S(2)}) %collective-permute-start.6) | collective-permute-done | bytes 131104 | tf_op jit(solution)/shard_map/ppermute | solution.py:238
  22.7 1.9 %collective-permute-done.7 = bf16[256,256]{1,0:T(8,128)(2,1)S(1)} collective-permute-done((bf16[256,256]{1,0:T(8,128)(2,1)S(1)}, bf16[256,256]{1,0:T(8,128)(2,1)S(1)}, u32[]{:S(2)}, u32[]{:S(2)}) %collective-permute-start.7) | collective-permute-done | bytes 131104 | tf_op jit(solution)/shard_map/ppermute | solution.py:238
  24.6 1.3 %collective-permute-done.8 = bf16[256,256]{1,0:T(8,128)(2,1)S(1)} collective-permute-done((bf16[256,256]{1,0:T(8,128)(2,1)S(1)}, bf16[256,256]{1,0:T(8,128)(2,1)S(1)}, u32[]{:S(2)}, u32[]{:S(2)}) %collective-permute-start.8) | collective-permute-done | bytes 131104 | tf_op jit(solution)/shard_map/ppermute | solution.py:238
  25.9 0.1 add_convert_fusion
  26.0 0.0 collective-permute-done.10
  26.1 2.6 %collective-permute-start.14 = (bf16[16,1024]{1,0:T(8,128)(2,1)S(1)}, bf16[16,1024]{1,0:T(8,128)(2,1)S(1)}, u32[]{:S(2)}, u32[]{:S(2)}) collective-permute-start(bf16[16,1024]{1,0:T(8,128)(2,1)S(1)} %slice.46), channel_id=1, source_target_pairs={{0,2},{1,3},{2,0},{3,1},{4,6},{5,7},{6,4},{7,5},{8,10},{9,11},{10,... | collective-permute-start | bytes 98312 | tf_op jit(solution)/shard_map/ppermute | solution.py:241
  28.7 1.8 %collective-permute-start.13 = (bf16[256,256]{1,0:T(8,128)(2,1)S(1)}, bf16[256,256]{1,0:T(8,128)(2,1)S(1)}, u32[]{:S(2)}, u32[]{:S(2)}) collective-permute-start(bf16[256,256]{1,0:T(8,128)(2,1)S(1)} %add_convert_fusion), channel_id=1, source_target_pairs={{0,24},{4,28},{8,16},{12,20},{16,8},{20,12},{24,0},{28,4},{1,25},{... | collective-permute-start | bytes 393224 | tf_op jit(solution)/shard_map/ppermute | solution.py:238
  30.5 0.5 %collective-permute-start.12 = (bf16[256,256]{1,0:T(8,128)(2,1)S(1)}, bf16[256,256]{1,0:T(8,128)(2,1)S(1)}, u32[]{:S(2)}, u32[]{:S(2)}) collective-permute-start(bf16[256,256]{1,0:T(8,128)(2,1)S(1)} %add_convert_fusion), channel_id=1, source_target_pairs={{0,16},{4,20},{8,24},{12,28},{16,0},{20,4},{24,8},{28,12},{1,17},{... | collective-permute-start | bytes 393224 | tf_op jit(solution)/shard_map/ppermute | solution.py:238
  31.0 1.2 %collective-permute-start.11 = (bf16[256,256]{1,0:T(8,128)(2,1)S(1)}, bf16[256,256]{1,0:T(8,128)(2,1)S(1)}, u32[]{:S(2)}, u32[]{:S(2)}) collective-permute-start(bf16[256,256]{1,0:T(8,128)(2,1)S(1)} %add_convert_fusion), channel_id=1, source_target_pairs={{0,8},{4,12},{8,0},{12,4},{16,24},{20,28},{24,16},{28,20},{1,9},{5... | collective-permute-start | bytes 393224 | tf_op jit(solution)/shard_map/ppermute | solution.py:238
  32.2 0.0 collective-permute-done.14
  32.3 0.9 %collective-permute-start.15 = (f32[8,1024]{1,0:T(8,128)S(1)}, f32[8,1024]{1,0:T(8,128)S(1)}, u32[]{:S(2)}, u32[]{:S(2)}) collective-permute-start(f32[8,1024]{1,0:T(8,128)S(1)} %get-tuple-element.56), channel_id=1, source_target_pairs={{0,8},{4,12},{8,0},{12,4},{16,24},{20,28},{24,16},{28,20},{1,9},{5... | collective-permute-start | bytes 98312 | tf_op jit(solution)/shard_map/ppermute | solution.py:238
  33.2 2.9 %collective-permute-done.13 = bf16[256,256]{1,0:T(8,128)(2,1)S(1)} collective-permute-done((bf16[256,256]{1,0:T(8,128)(2,1)S(1)}, bf16[256,256]{1,0:T(8,128)(2,1)S(1)}, u32[]{:S(2)}, u32[]{:S(2)}) %collective-permute-start.13) | collective-permute-done | bytes 131104 | tf_op jit(solution)/shard_map/ppermute | solution.py:238
  36.1 0.8 %collective-permute-done.12 = bf16[256,256]{1,0:T(8,128)(2,1)S(1)} collective-permute-done((bf16[256,256]{1,0:T(8,128)(2,1)S(1)}, bf16[256,256]{1,0:T(8,128)(2,1)S(1)}, u32[]{:S(2)}, u32[]{:S(2)}) %collective-permute-start.12) | collective-permute-done | bytes 131104 | tf_op jit(solution)/shard_map/ppermute | solution.py:238
  36.9 0.0 collective-permute-done.11
  37.0 0.3 collective-permute-done.15
  37.3 0.0 collective-permute-start.16
  37.3 1.2 %collective-permute-start.17 = (f32[4,1024]{1,0:T(4,128)S(1)}, f32[4,1024]{1,0:T(4,128)S(1)}, u32[]{:S(2)}, u32[]{:S(2)}) collective-permute-start(f32[4,1024]{1,0:T(4,128)S(1)} %get-tuple-element.58), channel_id=1, source_target_pairs={{0,16},{4,20},{8,24},{12,28},{16,0},{20,4},{24,8},{28,12},{1,17},{... | collective-permute-start | bytes 49160 | tf_op jit(solution)/shard_map/ppermute | solution.py:238
  38.5 1.0 %place.2.refs_2_ = f32[1024,512]{1,0:T(8,128)} custom-call(bf16[1024,256]{1,0:T(8,128)(2,1)S(1)} %pad_maximum_fusion.src_ref), custom_call_target="tpu_custom_call" | custom-call | flops 524288 | bytes 3145728 | tf_op jit(solution)/shard_map/place/pallas_call | solution.py:341
  39.6 1.5 %collective-permute-done.17.refs_1_ = f32[4,1024]{1,0:T(4,128)S(1)} collective-permute-done((f32[4,1024]{1,0:T(4,128)S(1)}, f32[4,1024]{1,0:T(4,128)S(1)}, u32[]{:S(2)}, u32[]{:S(2)}) %collective-permute-start.17) | collective-permute-done | bytes 16416 | tf_op jit(solution)/shard_map/ppermute | solution.py:238
  41.1 0.0 collective-permute-done.16.src_ref
  41.1 1.6 %place.3 = (f32[4,1024]{1,0:T(4,128)}, f32[1024,512]{1,0:T(8,128)}) custom-call(bf16[1024,256]{1,0:T(8,128)(2,1)S(1)} %collective-permute-done.16.src_ref, f32[4,1024]{1,0:T(4,128)S(1)} %get-tuple-element.59.refs_0_, f32[4,1024]{1,0:T(4,128)S(1)} %collective-permute-done.17.refs_1_, f32[1024,512]{1,0:T(8,128)} %place.2.refs_2_), custom_call_target="tpu_custom_call", output_to_operand_aliasing={{1}: (3, {})} | custom-call | flops 524288 | bytes 3145728 | tf_op jit(solution)/shard_map/place/pallas_call | solution.py:341
  (14 shorter events, 0.2 us)
Async XLA Ops:
  0.6 1.5 %collective-permute-start.1 = (s32[1,512]{1,0:T(1,128)}, s32[1,512]{1,0:T(1,128)S(1)}, u32[]{:S(2)}, u32[]{:S(2)}) collective-permute-start(s32[1,512]{1,0:T(1,128)} %bitcast.9), channel_id=1, source_target_pairs={{0,4},{4,0},{8,12},{12,8},{16,20},{20,16},{24,28},{28,24},{1,5},{5... | collective-permute-start | bytes 6152 | tf_op jit(solution)/shard_map/ppermute | solution.py:238
  1.1 1.4 %collective-permute-start = (bf16[16,1024]{1,0:T(8,128)(2,1)}, bf16[16,1024]{1,0:T(8,128)(2,1)S(1)}, u32[]{:S(2)}, u32[]{:S(2)}) collective-permute-start(bf16[16,1024]{1,0:T(8,128)(2,1)} %param.7), channel_id=1, source_target_pairs={{0,4},{4,0},{8,12},{12,8},{16,20},{20,16},{24,28},{28,24},{1,5},{5... | collective-permute-start | bytes 98312 | tf_op jit(solution)/shard_map/ppermute | solution.py:238
  2.6 7.2 %collective-permute-start.4 = (bf16[32,1024]{1,0:T(8,128)(2,1)S(1)}, bf16[32,1024]{1,0:T(8,128)(2,1)S(1)}, u32[]{:S(2)}, u32[]{:S(2)}) collective-permute-start(bf16[32,1024]{1,0:T(8,128)(2,1)S(1)} %constant_dynamic-update-slice_fusion.refs_0_), channel_id=1, source_target_pairs={{0,24},{4,28},{8,16},{12,20},{16,8},{20,12},{24,0},{28,4},{1,25},{... | collective-permute-start | bytes 196616 | tf_op jit(solution)/shard_map/ppermute | solution.py:238
  6.2 4.3 %collective-permute-start.3 = (bf16[32,1024]{1,0:T(8,128)(2,1)S(1)}, bf16[32,1024]{1,0:T(8,128)(2,1)S(1)}, u32[]{:S(2)}, u32[]{:S(2)}) collective-permute-start(bf16[32,1024]{1,0:T(8,128)(2,1)S(1)} %constant_dynamic-update-slice_fusion.refs_0_), channel_id=1, source_target_pairs={{0,16},{4,20},{8,24},{12,28},{16,0},{20,4},{24,8},{28,12},{1,17},{... | collective-permute-start | bytes 196616 | tf_op jit(solution)/shard_map/ppermute | solution.py:238
  6.7 4.3 %collective-permute-start.2 = (bf16[32,1024]{1,0:T(8,128)(2,1)S(1)}, bf16[32,1024]{1,0:T(8,128)(2,1)S(1)}, u32[]{:S(2)}, u32[]{:S(2)}) collective-permute-start(bf16[32,1024]{1,0:T(8,128)(2,1)S(1)} %constant_dynamic-update-slice_fusion.refs_0_), channel_id=1, source_target_pairs={{0,8},{4,12},{8,0},{12,4},{16,24},{20,28},{24,16},{28,20},{1,9},{5... | collective-permute-start | bytes 196616 | tf_op jit(solution)/shard_map/ppermute | solution.py:238
  6.7 7.2 %copy-start = (s32[512,1]{0,1:T(1,128)S(1)}, s32[512,1]{0,1:T(1,128)}, u32[]{:S(2)}) copy-start(s32[512,1]{0,1:T(1,128)} %param.9) | copy-start | bytes 6148
  6.7 7.2 %copy-start.1 = (s32[512]{0:T(512)S(1)}, s32[512]{0:T(512)}, u32[]{:S(2)}) copy-start(s32[512]{0:T(512)} %param.10) | copy-start | bytes 6148
  13.9 1.6 %copy-start.2 = (s32[512]{0:T(512)S(1)}, s32[512]{0:T(512)}, u32[]{:S(2)}) copy-start(s32[512]{0:T(512)} %rel_hbm.1) | copy-start | bytes 6148
  13.9 1.6 %collective-permute-start.5 = (bf16[512,256]{1,0:T(8,128)(2,1)S(1)}, bf16[512,256]{1,0:T(8,128)(2,1)S(1)}, u32[]{:S(2)}, u32[]{:S(2)}) collective-permute-start(bf16[512,256]{1,0:T(8,128)(2,1)S(1)} %get-tuple-element.35), channel_id=1, source_target_pairs={{0,4},{4,0},{8,12},{12,8},{16,20},{20,16},{24,28},{28,24},{1,5},{5... | collective-permute-start | bytes 786440 | tf_op jit(solution)/shard_map/ppermute | solution.py:238
  16.2 3.7 %collective-permute-start.9 = (f32[64,1024]{1,0:T(8,128)S(1)}, f32[64,1024]{1,0:T(8,128)S(1)}, u32[]{:S(2)}, u32[]{:S(2)}) collective-permute-start(f32[64,1024]{1,0:T(8,128)S(1)} %get-tuple-element.49), channel_id=1, source_target_pairs={{0,4},{4,0},{8,12},{12,8},{16,20},{20,16},{24,28},{28,24},{1,5},{5... | collective-permute-start | bytes 786440 | tf_op jit(solution)/shard_map/ppermute | solution.py:238
  16.4 6.3 %collective-permute-start.6 = (bf16[256,256]{1,0:T(8,128)(2,1)S(1)}, bf16[256,256]{1,0:T(8,128)(2,1)S(1)}, u32[]{:S(2)}, u32[]{:S(2)}) collective-permute-start(bf16[256,256]{1,0:T(8,128)(2,1)S(1)} %get-tuple-element.45), channel_id=1, source_target_pairs={{0,8},{4,12},{8,0},{12,4},{16,24},{20,28},{24,16},{28,20},{1,9},{5... | collective-permute-start | bytes 393224 | tf_op jit(solution)/shard_map/ppermute | solution.py:238
  17.4 7.2 %collective-permute-start.7 = (bf16[256,256]{1,0:T(8,128)(2,1)S(1)}, bf16[256,256]{1,0:T(8,128)(2,1)S(1)}, u32[]{:S(2)}, u32[]{:S(2)}) collective-permute-start(bf16[256,256]{1,0:T(8,128)(2,1)S(1)} %get-tuple-element.46), channel_id=1, source_target_pairs={{0,16},{4,20},{8,24},{12,28},{16,0},{20,4},{24,8},{28,12},{1,17},{... | collective-permute-start | bytes 393224 | tf_op jit(solution)/shard_map/ppermute | solution.py:238
  18.8 7.2 %collective-permute-start.8 = (bf16[256,256]{1,0:T(8,128)(2,1)S(1)}, bf16[256,256]{1,0:T(8,128)(2,1)S(1)}, u32[]{:S(2)}, u32[]{:S(2)}) collective-permute-start(bf16[256,256]{1,0:T(8,128)(2,1)S(1)} %get-tuple-element.47), channel_id=1, source_target_pairs={{0,24},{4,28},{8,16},{12,20},{16,8},{20,12},{24,0},{28,4},{1,25},{... | collective-permute-start | bytes 393224 | tf_op jit(solution)/shard_map/ppermute | solution.py:238
  20.0 6.1 %collective-permute-start.10 = (bf16[32,1024]{1,0:T(8,128)(2,1)S(1)}, bf16[32,1024]{1,0:T(8,128)(2,1)S(1)}, u32[]{:S(2)}, u32[]{:S(2)}) collective-permute-start(bf16[32,1024]{1,0:T(8,128)(2,1)S(1)} %slice.45), channel_id=1, source_target_pairs={{0,1},{1,0},{2,3},{3,2},{4,5},{5,4},{6,7},{7,6},{8,9},{9,8},{10,11... | collective-permute-start | bytes 196616 | tf_op jit(solution)/shard_map/ppermute | solution.py:241
  26.1 6.1 %collective-permute-start.14 = (bf16[16,1024]{1,0:T(8,128)(2,1)S(1)}, bf16[16,1024]{1,0:T(8,128)(2,1)S(1)}, u32[]{:S(2)}, u32[]{:S(2)}) collective-permute-start(bf16[16,1024]{1,0:T(8,128)(2,1)S(1)} %slice.46), channel_id=1, source_target_pairs={{0,2},{1,3},{2,0},{3,1},{4,6},{5,7},{6,4},{7,5},{8,10},{9,11},{10,... | collective-permute-start | bytes 98312 | tf_op jit(solution)/shard_map/ppermute | solution.py:241
  28.7 7.3 %collective-permute-start.13 = (bf16[256,256]{1,0:T(8,128)(2,1)S(1)}, bf16[256,256]{1,0:T(8,128)(2,1)S(1)}, u32[]{:S(2)}, u32[]{:S(2)}) collective-permute-start(bf16[256,256]{1,0:T(8,128)(2,1)S(1)} %add_convert_fusion), channel_id=1, source_target_pairs={{0,24},{4,28},{8,16},{12,20},{16,8},{20,12},{24,0},{28,4},{1,25},{... | collective-permute-start | bytes 393224 | tf_op jit(solution)/shard_map/ppermute | solution.py:238
  30.5 6.4 %collective-permute-start.12 = (bf16[256,256]{1,0:T(8,128)(2,1)S(1)}, bf16[256,256]{1,0:T(8,128)(2,1)S(1)}, u32[]{:S(2)}, u32[]{:S(2)}) collective-permute-start(bf16[256,256]{1,0:T(8,128)(2,1)S(1)} %add_convert_fusion), channel_id=1, source_target_pairs={{0,16},{4,20},{8,24},{12,28},{16,0},{20,4},{24,8},{28,12},{1,17},{... | collective-permute-start | bytes 393224 | tf_op jit(solution)/shard_map/ppermute | solution.py:238
  31.0 5.9 %collective-permute-start.11 = (bf16[256,256]{1,0:T(8,128)(2,1)S(1)}, bf16[256,256]{1,0:T(8,128)(2,1)S(1)}, u32[]{:S(2)}, u32[]{:S(2)}) collective-permute-start(bf16[256,256]{1,0:T(8,128)(2,1)S(1)} %add_convert_fusion), channel_id=1, source_target_pairs={{0,8},{4,12},{8,0},{12,4},{16,24},{20,28},{24,16},{28,20},{1,9},{5... | collective-permute-start | bytes 393224 | tf_op jit(solution)/shard_map/ppermute | solution.py:238
  32.3 5.0 %collective-permute-start.15 = (f32[8,1024]{1,0:T(8,128)S(1)}, f32[8,1024]{1,0:T(8,128)S(1)}, u32[]{:S(2)}, u32[]{:S(2)}) collective-permute-start(f32[8,1024]{1,0:T(8,128)S(1)} %get-tuple-element.56), channel_id=1, source_target_pairs={{0,8},{4,12},{8,0},{12,4},{16,24},{20,28},{24,16},{28,20},{1,9},{5... | collective-permute-start | bytes 98312 | tf_op jit(solution)/shard_map/ppermute | solution.py:238
  37.3 3.8 %collective-permute-start.16 = (bf16[1024,256]{1,0:T(8,128)(2,1)S(1)}, bf16[1024,256]{1,0:T(8,128)(2,1)S(1)}, u32[]{:S(2)}, u32[]{:S(2)}) collective-permute-start(bf16[1024,256]{1,0:T(8,128)(2,1)S(1)} %pad_maximum_fusion.src_ref), channel_id=1, source_target_pairs={{0,4},{4,0},{8,12},{12,8},{16,20},{20,16},{24,28},{28,24},{1,5},{5... | collective-permute-start | bytes 1572872 | tf_op jit(solution)/shard_map/ppermute | solution.py:238
  37.3 3.8 %collective-permute-start.17 = (f32[4,1024]{1,0:T(4,128)S(1)}, f32[4,1024]{1,0:T(4,128)S(1)}, u32[]{:S(2)}, u32[]{:S(2)}) collective-permute-start(f32[4,1024]{1,0:T(4,128)S(1)} %get-tuple-element.58), channel_id=1, source_target_pairs={{0,16},{4,20},{8,24},{12,28},{16,0},{20,4},{24,8},{28,12},{1,17},{... | collective-permute-start | bytes 49160 | tf_op jit(solution)/shard_map/ppermute | solution.py:238

commit v3 on v2

--- a/solution.py
+++ b/solution.py
@@ -32,21 +32,14 @@
     return acc
 
 
-def prepare_kernel(rel_hbm, phases_hbm, owner_hbm, row_hbm, tail_hbm, known_hbm, cos_ref, sin_ref, code_ref, rel_ref, phases_ref, owner_ref, row_ref, tail_ref, known_ref, sems, *, rows_ent, owner_rows):
+def prepare_kernel(
+    rel_hbm, phases_hbm, owner_hbm, row_hbm, tail_hbm, known_hbm, table_hbm, cos_ref, sin_ref, code_ref, own_ref,
+    rel_ref, phases_ref, owner_ref, row_ref, tail_ref, known_ref, sems, *, rows_ent, owner_rows,
+):
     n = cos_ref.shape[0]
-    copies = [
-        pltpu.make_async_copy(src, dst, sems.at[i])
-        for i, (src, dst) in enumerate(
-            [
-                (known_hbm, known_ref),
-                (owner_hbm, owner_ref),
-                (row_hbm, row_ref),
-                (tail_hbm, tail_ref),
-                (rel_hbm, rel_ref),
-                (phases_hbm, phases_ref),
-            ]
-        )
-    ]
+    pairs = [(known_hbm, known_ref), (owner_hbm, owner_ref), (row_hbm, row_ref), (tail_hbm, tail_ref)]
+    pairs += [(rel_hbm, rel_ref), (phases_hbm, phases_ref), (table_hbm, own_ref)]
+    copies = [pltpu.make_async_copy(src, dst, sems.at[i]) for i, (src, dst) in enumerate(pairs)]
     for copy in copies:
         copy.start()
     for copy in copies[:4]:
@@ -80,7 +73,6 @@
 
     for copy in copies[4:]:
         copy.wait()
-
     half = cos_ref.shape[1]
     place = lax.broadcasted_iota(I32, (8, half), 0)
     for start in range(0, n, 8):
@@ -95,12 +87,17 @@
         cos_ref[start : start + 8, :] = 1.0 - t * s
 
 
+def candidates(own_ref, mate_ref, peers):
+    step = own_ref.shape[0] // peers
+    blocks = [ref[p * step : (p + 1) * step, :] for p in range(peers) for ref in (own_ref, mate_ref)]
+    return jnp.concatenate(blocks, axis=0)
+
+
 def score_kernel(*refs, peers, block):
-    table_refs = refs[:peers]
-    cos_ref, sin_ref, code_ref, keep_ref, send_ref, w_ref, q_ref = refs[peers:]
+    own_ref, mate_ref, cos_ref, sin_ref, code_ref, keep_ref, send_ref, w_ref, q_ref = refs
     n, half = cos_ref.shape
     quarter = half // 2
-    tab = jnp.concatenate([r[...] for r in table_refs], axis=0)
+    tab = candidates(own_ref, mate_ref, peers)
     f = tab.astype(F32)
     norm = jnp.sum(f * f, axis=1, keepdims=True)
     tsq = jnp.broadcast_to(norm, (norm.shape[0], 128)).T[0:1]
@@ -138,11 +135,10 @@
 
 
 def entity_kernel(w_ref, q_ref, cos_ref, sin_ref, owner_ref, row_ref, *refs, peers, n_rel, owner_rows, block):
-    table_refs = refs[:peers]
-    keep_ref, send_ref, hr = refs[peers:]
+    own_ref, mate_ref, keep_ref, send_ref, hr = refs
     n, entities = w_ref.shape
     half = cos_ref.shape[1]
-    tab = jnp.concatenate([r[...] for r in table_refs], axis=0)
+    tab = candidates(own_ref, mate_ref, peers)
     for start in range(0, n, block):
         at = slice(start, start + block)
         w = w_ref[at, :]
@@ -159,16 +155,10 @@
 
     def row_id(i):
         at = i // owner_rows
-        span = 2 * peers * n_rel
-        rel_bit = jnp.zeros_like(i)
-        span //= 2
-        ent_bit = (at // span) & 1
-        for bit in range(n_rel.bit_length() - 1):
-            span //= 2
-            rel_bit = rel_bit | (((at // span) & 1) << bit)
-        for bit in range(1, peers.bit_length()):
-            span //= 2
-            ent_bit = ent_bit | (((at // span) & 1) << bit)
+        ent_bit = (at // (peers * n_rel)) | ((at // 2 % peers) << 1)
+        rel_bit = at & 1
+        for bit in range(n_rel.bit_length() - 2, 0, -1):
+            rel_bit = rel_bit | (((at // (peers << bit)) & 1) << bit)
         return (ent_bit * n_rel + (rel_bit ^ me_rel)) * owner_rows + i % owner_rows
 
     e = row_id(lax.broadcasted_iota(I32, (entities, entities), 0))
@@ -197,11 +187,38 @@
         outs[p][...] = jnp.dot(hot, d, preferred_element_type=F32).astype(outs[p].dtype)
 
 
+def combine_kernel(own_ref, *refs, peers, cols):
+    got_refs, (left_ref, right_ref, keep_ref), outs = refs[: peers - 1], refs[peers - 1 : peers + 2], refs[peers + 2 :]
+    rows = own_ref.shape[0]
+    total = own_ref[...]
+    for got_ref in got_refs:
+        total = total + got_ref[...].astype(F32)
+    final = total.astype(BF16)
+    ent = left_ref[...] + right_ref[...].astype(F32)
+    span = ent.shape[0] // peers
+    for p in range(peers):
+        outs[p][:rows, :] = final
+        chunk = ent[p * span : (p + 1) * span]
+        if p == 0:
+            keep_ref[...] = chunk
+        else:
+            blocks = [chunk[:, i : i + cols] for i in range(0, chunk.shape[1], cols)]
+            outs[p][rows:, :] = jnp.concatenate(blocks, axis=0).astype(BF16)
+
+
+def collect_kernel(keep_ref, *refs, rows, cols):
+    got_refs, (mine_ref, other_ref) = refs[:-2], refs[-2:]
+    span, width = keep_ref.shape
+    total = keep_ref[...]
+    for got_ref in got_refs:
+        extra = got_ref[rows:, :].astype(F32)
+        total = total + jnp.concatenate([extra[i * span : (i + 1) * span] for i in range(width // cols)], axis=1)
+    mine_ref[...] = total[: span // 2]
+    other_ref[...] = total[span // 2 :]
+
+
 def place_kernel(src_ref, *refs, side, peers, rows):
-    if side:
-        left_ref, right_ref, _, sum_ref, out_hbm, buf, sems = refs
-    else:
-        out_hbm, buf, sems = refs
+    out_hbm, buf, sems = refs[-3:]
     quarter = src_ref.shape[1]
     me = lax.axis_index("ent")
     chip, par = me // 2, me % 2
@@ -211,11 +228,8 @@
         row = pl.multiple_of((chip ^ p) * rows, rows)
         at = slice(p * rows, (p + 1) * rows)
         buf[at, :] = src_ref[at, :].astype(F32)
-        copy = pltpu.make_async_copy(buf.at[at, :], out_hbm.at[pl.ds(row, rows), pl.ds(col, quarter)], sems.at[p])
-        copy.start()
-        copies.append(copy)
-    if side:
-        sum_ref[...] = left_ref[...] + right_ref[...]
+        copies.append(pltpu.make_async_copy(buf.at[at, :], out_hbm.at[pl.ds(row, rows), pl.ds(col, quarter)], sems.at[p]))
+        copies[-1].start()
     for copy in copies:
         copy.wait()
 
@@ -232,52 +246,61 @@
     quarter = half // 2
     rels = phases.shape[0]
     rows = rels // peers
-    block = min(128, n)
+    block = min(512, n)
 
     def swap(x, k):
         return lax.ppermute(x, "ent", [(i, i ^ k) for i in range(n_ent)])
 
+    def swap_each(xs, order):
+        got = dict(zip(order, lax.optimization_barrier([swap(xs[p], 2 * p) for p in order])))
+        return [got[p] for p in range(1, peers)]
+
+    def hold(x):
+        return pltpu.with_memory_space_constraint(x, pltpu.HBM)
+
+    middle = [peers // 2] if peers > 1 else []
+    near = [p for p in range(1, peers // 2)]
+    far = [p for p in range(peers // 2 + 1, peers)]
+    ORD = {"yxd": middle + near + far, "ydx": middle + far + near, "xyd": near + middle + far, "dyx": far + middle + near, "dxy": far + near + middle}
+
     def swap_rel(x, k):
         return lax.ppermute(x, "rel", [(i, i ^ k) for i in range(n_rel)])
 
     hbm = pl.BlockSpec(memory_space=pltpu.HBM)
+    vm = pl.BlockSpec(memory_space=pltpu.VMEM)
 
     owner_l = head_owner.reshape(1, n)
     row_l = head_row.reshape(1, n)
     rel_l = relation.reshape(1, n)
     tail_l = tail_ids.reshape(1, n)
     known_l = known_tails.T
-    mate, rel_mate = lax.optimization_barrier((swap(entity_table, 1), swap(rel_l, 1)))
-    pair = jnp.concatenate([entity_table, mate], axis=0)
-    tables = [pair] + [swap(pair, 2 * p) for p in range(1, peers)]
-
-    vm = pl.BlockSpec(memory_space=pltpu.VMEM)
-    cosine, sine, code = pl.pallas_call(
+    far = swap_each([entity_table] * peers, ORD["yxd"])
+    fetched = [relation, phases, owner_l, row_l, tail_l, known_l, entity_table]
+    cosine, sine, code, own = pl.pallas_call(
         functools.partial(prepare_kernel, rows_ent=rows_ent, owner_rows=owner_rows),
-        in_specs=[hbm] * 6,
-        out_specs=[vm] * 3,
-        scratch_shapes=[
-            pltpu.SMEM((n,), I32),
-            pltpu.VMEM((rels, half), F32),
-            pltpu.VMEM((1, n), I32),
-            pltpu.VMEM((1, n), I32),
-            pltpu.VMEM((1, n), I32),
-            pltpu.VMEM(known_l.shape, I32),
-            pltpu.SemaphoreType.DMA((6,)),
-        ],
+        in_specs=[hbm] * len(fetched),
+        out_specs=[vm] * 4,
         out_shape=[
             jax.ShapeDtypeStruct((n, half), F32),
             jax.ShapeDtypeStruct((n, half), F32),
             jax.ShapeDtypeStruct((n, entities), I32),
+            jax.ShapeDtypeStruct(entity_table.shape, BF16),
         ],
+        scratch_shapes=[pltpu.SMEM((n,), I32)]
+        + [pltpu.VMEM(x.shape, x.dtype) for x in fetched[1:6]]
+        + [pltpu.SemaphoreType.DMA((len(fetched),))],
         compiler_params=params(),
         cost_estimate=cost(30 * n * half, 12 * n * half),
         name="prepare",
-    )(*[pltpu.with_memory_space_constraint(x, pltpu.HBM) for x in (relation, phases, owner_l, row_l, tail_l, known_l)])
-
+    )(*[hold(x) for x in fetched])
+
+    cosine, sine, code, own, *far = lax.optimization_barrier((cosine, sine, code, own, *far))
+    held = jnp.concatenate([own, *far], axis=0)
+    mate, rel_mate = lax.optimization_barrier((swap(held, 1), swap(rel_l, 1)))
+    tables = [held, mate]
     keep, send, w, q = pl.pallas_call(
         functools.partial(score_kernel, peers=peers, block=block),
-        in_specs=[vm] * (peers + 3),
+        in_specs=[vm] * 5,
         out_specs=[vm] * 4,
         out_shape=[
             jax.ShapeDtypeStruct((n, quarter), BF16),
@@ -293,7 +316,7 @@
     got = swap(send, 1)
     ent_keep, ent_send = pl.pallas_call(
         functools.partial(entity_kernel, peers=peers, n_rel=n_rel, owner_rows=owner_rows, block=block),
-        in_specs=[vm] * (6 + peers),
+        in_specs=[vm] * 8,
         out_specs=[vm] * 2,
         out_shape=[jax.ShapeDtypeStruct((entities // 2, width), F32)] * 2,
         scratch_shapes=[pltpu.VMEM((n, width), BF16)],
@@ -314,43 +337,56 @@
 
     *parts, ent_keep, ent_send = lax.optimization_barrier((*parts, ent_keep, ent_send))
 
-    received = [swap(parts[p], 2 * p) for p in range(1, peers)]
-    total = parts[0]
-    for part in received:
-        total = total + part.astype(F32)
-    final = total.astype(BF16)
-
-    def fold(x, move, sent):
-        middle = x.shape[0] // 2
-        return x[:middle], move(x[middle:].astype(sent)).astype(F32)
-
-    left, right = fold(ent_keep + swap(ent_send, 1), lambda x: swap_rel(x, 1), BF16)
-    final, left, right = lax.optimization_barrier((final, left, right))
-    for bit in range(1, n_rel.bit_length() - 1):
-        left, right = fold(left + right, lambda x: swap_rel(x, 1 << bit), BF16)
-    for bit in range(1, peers.bit_length() - 1):
-        left, right = fold(left + right, lambda x: swap(x, 1 << bit), F32)
-
-    mine = jnp.concatenate([final] + [swap(final, 2 * p) for p in range(1, peers)], axis=0)
-    mine, left, right = lax.optimization_barrier((mine, left, right))
-    left, right = fold(left + right, lambda x: swap(x, peers), F32)
+    received = swap_each(parts, ORD["ydx"])
+
+    left, right = ent_keep, swap(ent_send, 1)
+    for bit in range(n_rel.bit_length() - 2, 0, -1):
+        middle = left.shape[0] // 2
+        left, right = (left + right)[:middle], swap_rel((left + right)[middle:].astype(BF16), 1 << bit)
+    span = 2 * owner_rows
+    extra = span * width // quarter
+    ent_own, *messages = pl.pallas_call(
+        functools.partial(combine_kernel, peers=peers, cols=quarter),
+        in_specs=[vm] * (peers + 2),
+        out_specs=[vm] * (peers + 1),
+        out_shape=[jax.ShapeDtypeStruct((span, width), F32), jax.ShapeDtypeStruct((rows, quarter), BF16)]
+        + [jax.ShapeDtypeStruct((rows + extra, quarter), BF16)] * (peers - 1),
+        compiler_params=params(),
+        cost_estimate=cost(4 * rows * quarter, 16 * rows * quarter),
+        name="combine",
+    )(parts[0], *received, left, right)
+    final, far = messages[0], swap_each(messages, ORD["dxy"])
+    mine = jnp.concatenate([final] + [x[:rows] for x in far], axis=0)
+    left, right = pl.pallas_call(
+        functools.partial(collect_kernel, rows=rows, cols=quarter),
+        in_specs=[vm] * peers,
+        out_specs=[vm] * 2,
+        out_shape=[jax.ShapeDtypeStruct((owner_rows, width), F32)] * 2,
+        compiler_params=params(),
+        cost_estimate=cost(peers * span * width, 4 * peers * span * width),
+        name="collect",
+    )(ent_own, *far)
     theirs = swap(mine, 1)
+    right = swap_rel(right, 1)
+
+    gradient = jax.ShapeDtypeStruct((rels, half), F32)
 
     def place(side, *args):
-        shape = jax.ShapeDtypeStruct((rels, half), F32)
         return pl.pallas_call(
             functools.partial(place_kernel, side=side, peers=peers, rows=rows),
-            in_specs=[vm] * 3 + [hbm] if side else [vm],
-            out_specs=(vm, hbm) if side else hbm,
-            out_shape=(jax.ShapeDtypeStruct((owner_rows, width), F32), shape) if side else shape,
+            in_specs=[vm, hbm][: len(args)],
+            out_specs=hbm,
+            out_shape=gradient,
             scratch_shapes=[pltpu.VMEM((rels, quarter), F32), pltpu.SemaphoreType.DMA((peers,))],
-            input_output_aliases={3: 1} if side else {},
+            input_output_aliases={1: 0} if side else {},
             compiler_params=params(),
             cost_estimate=cost(rels * half, 6 * rels * half),
             name="place",
         )(*args)
 
-    return place(1, theirs, left, right, place(0, mine))
+    relation_gradient = place(1, theirs, place(0, mine))
+    relation_gradient, left, right = lax.optimization_barrier((relation_gradient, left, right))
+    return left + right, relation_gradient
 
 
 def solution(mesh):

time: 42.9 us -> 39.1 us (0.911)
  starting transfers between devices: 18.5 us -> 17.2 us
  Pallas kernels: 10.4 us -> 9.21 us
  waiting for transfers between devices: 12 us -> 11 us
  local copies, waits for them, and re-layouts: 0.82 us -> 0.08 us
  other arithmetic: 0.17 us -> 0.68 us
    ppermute x16 -> x14, starting transfers between devices: 14.2 us -> 12.9 us  [swap(): return lax.ppermute(x, 'ent', [(i, i ^ k) for i in range(n_ent)])]
    ppermute x16 -> x14, waiting for transfers between devices: 12 us -> 10.9 us  [swap(): return lax.ppermute(x, 'ent', [(i, i ^ k) for i in range(n_ent)])]
    pallas_call x1, Pallas kernels: 2.92 us -> 2.09 us  [local(): pl.pallas_call(functools.partial(score_kernel, peers=peers, block=block),...]
    unnamed x7 -> x9, local copies, waits for them, and re-layouts: 0.77 us -> 0.02 us
    pallas_call x2, Pallas kernels: 2.63 us -> 2.03 us  [place(): pl.pallas_call(functools.partial(place_kernel, side=side, peers=peers, ro...]
    add x4 -> x2, other arithmetic: 0.06 us -> 0.64 us  [the longest x1 0.61 us: local(): return (left + right, relation_gradient)]
  transfers between devices with their start and end apart: 18 -> 16, of which waited for: 12 -> 9; matrix products, arithmetic and copies ran while one was open for 2% -> 0% of each run, Pallas kernels for 12% -> 16%
where the time goes in v3:
time: 39.1 us; the launch traced here: 39 us
  starting transfers between devices  17.2 us (44%)
  waiting for transfers between devices  11 us (28%)
  Pallas kernels  9.21 us (24%)
  between operations  0.83 us (2%)
  other arithmetic  0.68 us (2%)
    ppermute x14, starting transfers between devices, swap(): return lax.ppermute(x, 'ent', [(i, i ^ k) for i in range(n_ent)])  12.9 us
    ppermute x14, waiting for transfers between devices, swap(): return lax.ppermute(x, 'ent', [(i, i ^ k) for i in range(n_ent)])  10.9 us
    ppermute x2, starting transfers between devices, swap_rel(): return lax.ppermute(x, 'rel', [(i, i ^ k) for i in range(n_rel)])  4.3 us
    pallas_call x1, Pallas kernels, local(): pl.pallas_call(functools.partial(prepare_kernel, rows_ent=rows_ent, owner...  3.02 us
    pallas_call x1, Pallas kernels, local(): pl.pallas_call(functools.partial(score_kernel, peers=peers, block=block),...  2.09 us
    pallas_call x2, Pallas kernels, place(): pl.pallas_call(functools.partial(place_kernel, side=side, peers=peers, ro...  2.03 us
    pallas_call x1, Pallas kernels, local(): pl.pallas_call(functools.partial(entity_kernel, peers=peers, n_rel=n_rel,...  1.27 us
  transfers between devices with their start and end apart: 16, of which 9 were waited for; matrix products, arithmetic and copies ran while one was open for 0% of the time, Pallas kernels for 16%

profile of v3, /device:TPU:0, one launch (start us, length us, event | category | flops | bytes accessed | tf_op | source)
XLA Modules:
  0.0 39.0 jit_solution(3356657282947630006)
XLA Ops:
  0.6 0.0 copy-start.2
  0.6 3.0 %collective-permute-start = (bf16[16,1024]{1,0:T(8,128)(2,1)}, bf16[16,1024]{1,0:T(8,128)(2,1)S(1)}, u32[]{:S(2)}, u32[]{:S(2)}) collective-permute-start(bf16[16,1024]{1,0:T(8,128)(2,1)} %table_hbm.1), channel_id=1, source_target_pairs={{0,16},{4,20},{8,24},{12,28},{16,0},{20,4},{24,8},{28,12},{1,17},{... | collective-permute-start | bytes 98312 | tf_op jit(solution)/shard_map/ppermute | solution.py:252
  3.7 1.4 %collective-permute-start.2 = (bf16[16,1024]{1,0:T(8,128)(2,1)}, bf16[16,1024]{1,0:T(8,128)(2,1)S(1)}, u32[]{:S(2)}, u32[]{:S(2)}) collective-permute-start(bf16[16,1024]{1,0:T(8,128)(2,1)} %table_hbm.1), channel_id=1, source_target_pairs={{0,24},{4,28},{8,16},{12,20},{16,8},{20,12},{24,0},{28,4},{1,25},{... | collective-permute-start | bytes 98312 | tf_op jit(solution)/shard_map/ppermute | solution.py:252
  5.1 0.1 collective-permute-start.1
  5.2 0.0 copy-start
  5.2 0.0 copy-start.1
  5.2 3.0 %prepare.1 = (f32[512,512]{1,0:T(8,128)S(1)}, f32[512,512]{1,0:T(8,128)S(1)}, s32[512,128]{1,0:T(8,128)S(1)}, bf16[16,1024]{1,0:T(8,128)(2,1)S(1)}) custom-call(s32[512]{0:T(512)} %rel_hbm.1, f32[1024,512]{1,0:T(8,128)} %phases_hbm.1, s32[1,512]{1,0:T(1,128)} %bitcast.5, s32[1,512]{1,0:T(1,128)} %bitcast.7, s32[1,512]{1,0:T(1,128)} %bitcast.12, ...), custom_call_target="tpu_custom_call" | custom-call | flops 7864320 | bytes 3145728 | tf_op jit(solution)/shard_map/prepare/pallas_call | solution.py:279
  8.3 0.0 collective-permute-done
  8.3 0.6 %collective-permute-done.2 = bf16[16,1024]{1,0:T(8,128)(2,1)S(1)} collective-permute-done((bf16[16,1024]{1,0:T(8,128)(2,1)}, bf16[16,1024]{1,0:T(8,128)(2,1)S(1)}, u32[]{:S(2)}, u32[]{:S(2)}) %collective-permute-start.2) | collective-permute-done | bytes 32800 | tf_op jit(solution)/shard_map/ppermute | solution.py:252
  8.8 0.4 collective-permute-done.1
  9.3 0.1 collective-permute-start.3
  9.3 0.0 copy-done.2
  9.4 0.5 %collective-permute-start.4 = (s32[1,512]{1,0:T(1,128)S(1)}, s32[1,512]{1,0:T(1,128)S(1)}, u32[]{:S(2)}, u32[]{:S(2)}) collective-permute-start(s32[1,512]{1,0:T(1,128)S(1)} %bitcast.9), channel_id=1, source_target_pairs={{0,4},{4,0},{8,12},{12,8},{16,20},{20,16},{24,28},{28,24},{1,5},{5... | collective-permute-start | bytes 6152 | tf_op jit(solution)/shard_map/ppermute | solution.py:252
  9.8 0.8 %collective-permute-done.4.theirs_ref = s32[1,512]{1,0:T(1,128)S(1)} collective-permute-done((s32[1,512]{1,0:T(1,128)S(1)}, s32[1,512]{1,0:T(1,128)S(1)}, u32[]{:S(2)}, u32[]{:S(2)}) %collective-permute-start.4) | collective-permute-done | bytes 2080 | tf_op jit(solution)/shard_map/ppermute | solution.py:252
  10.7 0.0 collective-permute-done.3.refs_1_
  10.7 2.1 %score.1 = (bf16[512,256]{1,0:T(8,128)(2,1)S(1)}, bf16[512,256]{1,0:T(8,128)(2,1)S(1)}, bf16[512,128]{1,0:T(8,128)(2,1)S(1)}, bf16[512,1024]{1,0:T(8,128)(2,1)S(1)}) custom-call(bf16[64,1024]{1,0:T(8,128)(2,1)S(1)} %constant_dynamic-update-slice_fusion.refs_0_, bf16[64,1024]{1,0:T(8,128)(2,1)S(1)} %collective-permute-done.3.refs_1_, ...), custom_call_target="tpu_custom_call" | custom-call | flops 402653184 | bytes 6291456 | tf_op jit(solution)/shard_map/score/pallas_call | solution.py:301
  12.8 0.4 collective-permute-start.5
  13.2 0.0 copy-done
  13.2 0.0 copy-done.1
  13.2 1.3 %entity.1 = (f32[64,1024]{1,0:T(8,128)S(1)}, f32[64,1024]{1,0:T(8,128)S(1)}) custom-call(bf16[512,128]{1,0:T(8,128)(2,1)S(1)} %get-tuple-element.72.w_ref, bf16[512,1024]{1,0:T(8,128)(2,1)S(1)} %get-tuple-element.73.q_ref, f32[512,512]{1,0:T(8,128)S(1)} %get-tuple-element.63.refs_2_.cos_ref, f32[512,512]{1,0:T(8,128)S(1)} %get-tuple-element.64.refs_3_.sin_ref, ...), custom_call_target="tpu_custom_call" | custom-call | flops 402653184 | bytes 2621440 | tf_op jit(solution)/shard_map/entity/pallas_call | solution.py:317
  14.4 0.0 collective-permute-done.5.got_ref
  14.4 0.7 %scatter.1 = (f32[256,256]{1,0:T(8,128)S(1)}, bf16[256,256]{1,0:T(8,128)(2,1)S(1)}, bf16[256,256]{1,0:T(8,128)(2,1)S(1)}, bf16[256,256]{1,0:T(8,128)(2,1)S(1)}) custom-call(s32[1,512]{1,0:T(1,128)S(1)} %bitcast.10, s32[1,512]{1,0:T(1,128)S(1)} %collective-permute-done.4.theirs_ref, bf16[512,256]{1,0:T(8,128)(2,1)S(1)} %get-tuple-element.66.keep_ref, ...), custom_call_target="tpu_custom_call" | custom-call | flops 536870912 | bytes 1048576 | tf_op jit(solution)/shard_map/scatter/pallas_call | solution.py:328
  15.2 0.3 collective-permute-start.9
  15.5 1.5 %collective-permute-start.6 = (bf16[256,256]{1,0:T(8,128)(2,1)S(1)}, bf16[256,256]{1,0:T(8,128)(2,1)S(1)}, u32[]{:S(2)}, u32[]{:S(2)}) collective-permute-start(bf16[256,256]{1,0:T(8,128)(2,1)S(1)} %get-tuple-element.77), channel_id=1, source_target_pairs={{0,16},{4,20},{8,24},{12,28},{16,0},{20,4},{24,8},{28,12},{1,17},{... | collective-permute-start | bytes 393224 | tf_op jit(solution)/shard_map/ppermute | solution.py:252
  17.0 0.9 %collective-permute-start.7 = (bf16[256,256]{1,0:T(8,128)(2,1)S(1)}, bf16[256,256]{1,0:T(8,128)(2,1)S(1)}, u32[]{:S(2)}, u32[]{:S(2)}) collective-permute-start(bf16[256,256]{1,0:T(8,128)(2,1)S(1)} %get-tuple-element.78), channel_id=1, source_target_pairs={{0,24},{4,28},{8,16},{12,20},{16,8},{20,12},{24,0},{28,4},{1,25},{... | collective-permute-start | bytes 393224 | tf_op jit(solution)/shard_map/ppermute | solution.py:252
  17.9 1.0 %collective-permute-start.8 = (bf16[256,256]{1,0:T(8,128)(2,1)S(1)}, bf16[256,256]{1,0:T(8,128)(2,1)S(1)}, u32[]{:S(2)}, u32[]{:S(2)}) collective-permute-start(bf16[256,256]{1,0:T(8,128)(2,1)S(1)} %get-tuple-element.79), channel_id=1, source_target_pairs={{0,8},{4,12},{8,0},{12,4},{16,24},{20,28},{24,16},{28,20},{1,9},{5... | collective-permute-start | bytes 393224 | tf_op jit(solution)/shard_map/ppermute | solution.py:252
  19.0 0.0 collective-permute-done.9
  19.0 2.7 %collective-permute-start.10 = (bf16[32,1024]{1,0:T(8,128)(2,1)S(1)}, bf16[32,1024]{1,0:T(8,128)(2,1)S(1)}, u32[]{:S(2)}, u32[]{:S(2)}) collective-permute-start(bf16[32,1024]{1,0:T(8,128)(2,1)S(1)} %slice.24), channel_id=1, source_target_pairs={{0,2},{1,3},{2,0},{3,1},{4,6},{5,7},{6,4},{7,5},{8,10},{9,11},{10,... | collective-permute-start | bytes 196616 | tf_op jit(solution)/shard_map/ppermute | solution.py:267
  21.7 1.9 %collective-permute-done.6.refs_1_ = bf16[256,256]{1,0:T(8,128)(2,1)S(1)} collective-permute-done((bf16[256,256]{1,0:T(8,128)(2,1)S(1)}, bf16[256,256]{1,0:T(8,128)(2,1)S(1)}, u32[]{:S(2)}, u32[]{:S(2)}) %collective-permute-start.6) | collective-permute-done | bytes 131104 | tf_op jit(solution)/shard_map/ppermute | solution.py:252
  23.6 0.7 %collective-permute-done.7.refs_2_ = bf16[256,256]{1,0:T(8,128)(2,1)S(1)} collective-permute-done((bf16[256,256]{1,0:T(8,128)(2,1)S(1)}, bf16[256,256]{1,0:T(8,128)(2,1)S(1)}, u32[]{:S(2)}, u32[]{:S(2)}) %collective-permute-start.7) | collective-permute-done | bytes 131104 | tf_op jit(solution)/shard_map/ppermute | solution.py:252
  24.3 0.9 %collective-permute-done.8.refs_0_ = bf16[256,256]{1,0:T(8,128)(2,1)S(1)} collective-permute-done((bf16[256,256]{1,0:T(8,128)(2,1)S(1)}, bf16[256,256]{1,0:T(8,128)(2,1)S(1)}, u32[]{:S(2)}, u32[]{:S(2)}) %collective-permute-start.8) | collective-permute-done | bytes 131104 | tf_op jit(solution)/shard_map/ppermute | solution.py:252
  25.2 0.0 collective-permute-done.10.refs_4_
  25.2 0.1 combine.1
  25.3 2.0 %collective-permute-start.11 = (bf16[288,256]{1,0:T(8,128)(2,1)S(1)}, bf16[288,256]{1,0:T(8,128)(2,1)S(1)}, u32[]{:S(2)}, u32[]{:S(2)}) collective-permute-start(bf16[288,256]{1,0:T(8,128)(2,1)S(1)} %get-tuple-element.86), channel_id=1, source_target_pairs={{0,24},{4,28},{8,16},{12,20},{16,8},{20,12},{24,0},{28,4},{1,25},{... | collective-permute-start | bytes 442376 | tf_op jit(solution)/shard_map/ppermute | solution.py:252
  27.3 1.0 %collective-permute-start.12 = (bf16[288,256]{1,0:T(8,128)(2,1)S(1)}, bf16[288,256]{1,0:T(8,128)(2,1)S(1)}, u32[]{:S(2)}, u32[]{:S(2)}) collective-permute-start(bf16[288,256]{1,0:T(8,128)(2,1)S(1)} %get-tuple-element.87), channel_id=1, source_target_pairs={{0,8},{4,12},{8,0},{12,4},{16,24},{20,28},{24,16},{28,20},{1,9},{5... | collective-permute-start | bytes 442376 | tf_op jit(solution)/shard_map/ppermute | solution.py:252
  28.3 0.5 %collective-permute-start.13 = (bf16[288,256]{1,0:T(8,128)(2,1)S(1)}, bf16[288,256]{1,0:T(8,128)(2,1)S(1)}, u32[]{:S(2)}, u32[]{:S(2)}) collective-permute-start(bf16[288,256]{1,0:T(8,128)(2,1)S(1)} %get-tuple-element.88), channel_id=1, source_target_pairs={{0,16},{4,20},{8,24},{12,28},{16,0},{20,4},{24,8},{28,12},{1,17},{... | collective-permute-start | bytes 442376 | tf_op jit(solution)/shard_map/ppermute | solution.py:252
  28.8 3.9 %collective-permute-done.11.refs_2_ = bf16[288,256]{1,0:T(8,128)(2,1)S(1)} collective-permute-done((bf16[288,256]{1,0:T(8,128)(2,1)S(1)}, bf16[288,256]{1,0:T(8,128)(2,1)S(1)}, u32[]{:S(2)}, u32[]{:S(2)}) %collective-permute-start.11) | collective-permute-done | bytes 147488 | tf_op jit(solution)/shard_map/ppermute | solution.py:252
  32.8 1.6 %collective-permute-done.12.refs_0_ = bf16[288,256]{1,0:T(8,128)(2,1)S(1)} collective-permute-done((bf16[288,256]{1,0:T(8,128)(2,1)S(1)}, bf16[288,256]{1,0:T(8,128)(2,1)S(1)}, u32[]{:S(2)}, u32[]{:S(2)}) %collective-permute-start.12) | collective-permute-done | bytes 147488 | tf_op jit(solution)/shard_map/ppermute | solution.py:252
  34.4 0.0 collective-permute-done.13.refs_1_
  34.5 0.1 collective-permute-start.14
  34.6 1.6 %collective-permute-start.15 = (f32[4,1024]{1,0:T(4,128)S(1)}, f32[4,1024]{1,0:T(4,128)S(1)}, u32[]{:S(2)}, u32[]{:S(2)}) collective-permute-start(f32[4,1024]{1,0:T(4,128)S(1)} %get-tuple-element.94), channel_id=1, source_target_pairs={{0,1},{1,0},{2,3},{3,2},{4,5},{5,4},{6,7},{7,6},{8,9},{9,8},{10,11... | collective-permute-start | bytes 49160 | tf_op jit(solution)/shard_map/ppermute | solution.py:267
  36.2 1.0 %place.2.refs_0_ = f32[1024,512]{1,0:T(8,128)} custom-call(bf16[1024,256]{1,0:T(8,128)(2,1)S(1)} %pad_maximum_fusion.src_ref), custom_call_target="tpu_custom_call" | custom-call | flops 524288 | bytes 3145728 | tf_op jit(solution)/shard_map/place/pallas_call | solution.py:375
  37.2 0.0 collective-permute-done.14.src_ref
  37.2 1.0 %place.3 = f32[1024,512]{1,0:T(8,128)} custom-call(bf16[1024,256]{1,0:T(8,128)(2,1)S(1)} %collective-permute-done.14.src_ref, f32[1024,512]{1,0:T(8,128)} %place.2.refs_0_), custom_call_target="tpu_custom_call", output_to_operand_aliasing={{}: (1, {})} | custom-call | flops 524288 | bytes 3145728 | tf_op jit(solution)/shard_map/place/pallas_call | solution.py:375
  38.3 0.1 collective-permute-done.15
  38.4 0.6 %add.8 = f32[4,1024]{1,0:T(4,128)} add(f32[4,1024]{1,0:T(4,128)S(1)} %get-tuple-element.95, f32[4,1024]{1,0:T(4,128)S(1)} %collective-permute-done.15) | non-fusion elementwise | flops 4096 | bytes 49152 | tf_op jit(solution)/shard_map/add | solution.py:389
  (12 shorter events, 0.1 us)
Async XLA Ops:
  0.6 8.7 %copy-start.2 = (s32[512]{0:T(512)S(1)}, s32[512]{0:T(512)}, u32[]{:S(2)}) copy-start(s32[512]{0:T(512)} %rel_hbm.1) | copy-start | bytes 6148
  0.6 7.6 %collective-permute-start = (bf16[16,1024]{1,0:T(8,128)(2,1)}, bf16[16,1024]{1,0:T(8,128)(2,1)S(1)}, u32[]{:S(2)}, u32[]{:S(2)}) collective-permute-start(bf16[16,1024]{1,0:T(8,128)(2,1)} %table_hbm.1), channel_id=1, source_target_pairs={{0,16},{4,20},{8,24},{12,28},{16,0},{20,4},{24,8},{28,12},{1,17},{... | collective-permute-start | bytes 98312 | tf_op jit(solution)/shard_map/ppermute | solution.py:252
  3.7 5.2 %collective-permute-start.2 = (bf16[16,1024]{1,0:T(8,128)(2,1)}, bf16[16,1024]{1,0:T(8,128)(2,1)S(1)}, u32[]{:S(2)}, u32[]{:S(2)}) collective-permute-start(bf16[16,1024]{1,0:T(8,128)(2,1)} %table_hbm.1), channel_id=1, source_target_pairs={{0,24},{4,28},{8,16},{12,20},{16,8},{20,12},{24,0},{28,4},{1,25},{... | collective-permute-start | bytes 98312 | tf_op jit(solution)/shard_map/ppermute | solution.py:252
  5.1 4.1 %collective-permute-start.1 = (bf16[16,1024]{1,0:T(8,128)(2,1)}, bf16[16,1024]{1,0:T(8,128)(2,1)S(1)}, u32[]{:S(2)}, u32[]{:S(2)}) collective-permute-start(bf16[16,1024]{1,0:T(8,128)(2,1)} %table_hbm.1), channel_id=1, source_target_pairs={{0,8},{4,12},{8,0},{12,4},{16,24},{20,28},{24,16},{28,20},{1,9},{5... | collective-permute-start | bytes 98312 | tf_op jit(solution)/shard_map/ppermute | solution.py:252
  5.2 7.9 %copy-start = (s32[512,1]{0,1:T(1,128)S(1)}, s32[512,1]{0,1:T(1,128)}, u32[]{:S(2)}) copy-start(s32[512,1]{0,1:T(1,128)} %param.9) | copy-start | bytes 6148
  5.2 7.9 %copy-start.1 = (s32[512]{0:T(512)S(1)}, s32[512]{0:T(512)}, u32[]{:S(2)}) copy-start(s32[512]{0:T(512)} %param.10) | copy-start | bytes 6148
  9.3 1.4 %collective-permute-start.3 = (bf16[64,1024]{1,0:T(8,128)(2,1)S(1)}, bf16[64,1024]{1,0:T(8,128)(2,1)S(1)}, u32[]{:S(2)}, u32[]{:S(2)}) collective-permute-start(bf16[64,1024]{1,0:T(8,128)(2,1)S(1)} %constant_dynamic-update-slice_fusion.refs_0_), channel_id=1, source_target_pairs={{0,4},{4,0},{8,12},{12,8},{16,20},{20,16},{24,28},{28,24},{1,5},{5... | collective-permute-start | bytes 393224 | tf_op jit(solution)/shard_map/ppermute | solution.py:252
  9.4 1.3 %collective-permute-start.4 = (s32[1,512]{1,0:T(1,128)S(1)}, s32[1,512]{1,0:T(1,128)S(1)}, u32[]{:S(2)}, u32[]{:S(2)}) collective-permute-start(s32[1,512]{1,0:T(1,128)S(1)} %bitcast.9), channel_id=1, source_target_pairs={{0,4},{4,0},{8,12},{12,8},{16,20},{20,16},{24,28},{28,24},{1,5},{5... | collective-permute-start | bytes 6152 | tf_op jit(solution)/shard_map/ppermute | solution.py:252
  12.8 1.7 %collective-permute-start.5 = (bf16[512,256]{1,0:T(8,128)(2,1)S(1)}, bf16[512,256]{1,0:T(8,128)(2,1)S(1)}, u32[]{:S(2)}, u32[]{:S(2)}) collective-permute-start(bf16[512,256]{1,0:T(8,128)(2,1)S(1)} %get-tuple-element.67), channel_id=1, source_target_pairs={{0,4},{4,0},{8,12},{12,8},{16,20},{20,16},{24,28},{28,24},{1,5},{5... | collective-permute-start | bytes 786440 | tf_op jit(solution)/shard_map/ppermute | solution.py:252
  15.2 3.8 %collective-permute-start.9 = (f32[64,1024]{1,0:T(8,128)S(1)}, f32[64,1024]{1,0:T(8,128)S(1)}, u32[]{:S(2)}, u32[]{:S(2)}) collective-permute-start(f32[64,1024]{1,0:T(8,128)S(1)} %get-tuple-element.84), channel_id=1, source_target_pairs={{0,4},{4,0},{8,12},{12,8},{16,20},{20,16},{24,28},{28,24},{1,5},{5... | collective-permute-start | bytes 786440 | tf_op jit(solution)/shard_map/ppermute | solution.py:252
  15.5 8.1 %collective-permute-start.6 = (bf16[256,256]{1,0:T(8,128)(2,1)S(1)}, bf16[256,256]{1,0:T(8,128)(2,1)S(1)}, u32[]{:S(2)}, u32[]{:S(2)}) collective-permute-start(bf16[256,256]{1,0:T(8,128)(2,1)S(1)} %get-tuple-element.77), channel_id=1, source_target_pairs={{0,16},{4,20},{8,24},{12,28},{16,0},{20,4},{24,8},{28,12},{1,17},{... | collective-permute-start | bytes 393224 | tf_op jit(solution)/shard_map/ppermute | solution.py:252
  17.0 7.3 %collective-permute-start.7 = (bf16[256,256]{1,0:T(8,128)(2,1)S(1)}, bf16[256,256]{1,0:T(8,128)(2,1)S(1)}, u32[]{:S(2)}, u32[]{:S(2)}) collective-permute-start(bf16[256,256]{1,0:T(8,128)(2,1)S(1)} %get-tuple-element.78), channel_id=1, source_target_pairs={{0,24},{4,28},{8,16},{12,20},{16,8},{20,12},{24,0},{28,4},{1,25},{... | collective-permute-start | bytes 393224 | tf_op jit(solution)/shard_map/ppermute | solution.py:252
  17.9 7.3 %collective-permute-start.8 = (bf16[256,256]{1,0:T(8,128)(2,1)S(1)}, bf16[256,256]{1,0:T(8,128)(2,1)S(1)}, u32[]{:S(2)}, u32[]{:S(2)}) collective-permute-start(bf16[256,256]{1,0:T(8,128)(2,1)S(1)} %get-tuple-element.79), channel_id=1, source_target_pairs={{0,8},{4,12},{8,0},{12,4},{16,24},{20,28},{24,16},{28,20},{1,9},{5... | collective-permute-start | bytes 393224 | tf_op jit(solution)/shard_map/ppermute | solution.py:252
  19.0 6.2 %collective-permute-start.10 = (bf16[32,1024]{1,0:T(8,128)(2,1)S(1)}, bf16[32,1024]{1,0:T(8,128)(2,1)S(1)}, u32[]{:S(2)}, u32[]{:S(2)}) collective-permute-start(bf16[32,1024]{1,0:T(8,128)(2,1)S(1)} %slice.24), channel_id=1, source_target_pairs={{0,2},{1,3},{2,0},{3,1},{4,6},{5,7},{6,4},{7,5},{8,10},{9,11},{10,... | collective-permute-start | bytes 196616 | tf_op jit(solution)/shard_map/ppermute | solution.py:267
  25.3 7.5 %collective-permute-start.11 = (bf16[288,256]{1,0:T(8,128)(2,1)S(1)}, bf16[288,256]{1,0:T(8,128)(2,1)S(1)}, u32[]{:S(2)}, u32[]{:S(2)}) collective-permute-start(bf16[288,256]{1,0:T(8,128)(2,1)S(1)} %get-tuple-element.86), channel_id=1, source_target_pairs={{0,24},{4,28},{8,16},{12,20},{16,8},{20,12},{24,0},{28,4},{1,25},{... | collective-permute-start | bytes 442376 | tf_op jit(solution)/shard_map/ppermute | solution.py:252
  27.3 7.1 %collective-permute-start.12 = (bf16[288,256]{1,0:T(8,128)(2,1)S(1)}, bf16[288,256]{1,0:T(8,128)(2,1)S(1)}, u32[]{:S(2)}, u32[]{:S(2)}) collective-permute-start(bf16[288,256]{1,0:T(8,128)(2,1)S(1)} %get-tuple-element.87), channel_id=1, source_target_pairs={{0,8},{4,12},{8,0},{12,4},{16,24},{20,28},{24,16},{28,20},{1,9},{5... | collective-permute-start | bytes 442376 | tf_op jit(solution)/shard_map/ppermute | solution.py:252
  28.3 6.0 %collective-permute-start.13 = (bf16[288,256]{1,0:T(8,128)(2,1)S(1)}, bf16[288,256]{1,0:T(8,128)(2,1)S(1)}, u32[]{:S(2)}, u32[]{:S(2)}) collective-permute-start(bf16[288,256]{1,0:T(8,128)(2,1)S(1)} %get-tuple-element.88), channel_id=1, source_target_pairs={{0,16},{4,20},{8,24},{12,28},{16,0},{20,4},{24,8},{28,12},{1,17},{... | collective-permute-start | bytes 442376 | tf_op jit(solution)/shard_map/ppermute | solution.py:252
  34.5 2.8 %collective-permute-start.14 = (bf16[1024,256]{1,0:T(8,128)(2,1)S(1)}, bf16[1024,256]{1,0:T(8,128)(2,1)S(1)}, u32[]{:S(2)}, u32[]{:S(2)}) collective-permute-start(bf16[1024,256]{1,0:T(8,128)(2,1)S(1)} %pad_maximum_fusion.src_ref), channel_id=1, source_target_pairs={{0,4},{4,0},{8,12},{12,8},{16,20},{20,16},{24,28},{28,24},{1,5},{5... | collective-permute-start | bytes 1572872 | tf_op jit(solution)/shard_map/ppermute | solution.py:252
  34.6 3.8 %collective-permute-start.15 = (f32[4,1024]{1,0:T(4,128)S(1)}, f32[4,1024]{1,0:T(4,128)S(1)}, u32[]{:S(2)}, u32[]{:S(2)}) collective-permute-start(f32[4,1024]{1,0:T(4,128)S(1)} %get-tuple-element.94), channel_id=1, source_target_pairs={{0,1},{1,0},{2,3},{3,2},{4,5},{5,4},{6,7},{7,6},{8,9},{9,8},{10,11... | collective-permute-start | bytes 49160 | tf_op jit(solution)/shard_map/ppermute | solution.py:267

commit v4 on v3

--- a/solution.py
+++ b/solution.py
@@ -175,22 +175,22 @@
     send_ref[...] = total[entities // 2 :]
 
 
-def scatter_kernel(mine_ref, theirs_ref, keep_ref, got_ref, *outs, peers, rows):
+def scatter_kernel(mine_ref, theirs_ref, keep_ref, got_ref, *outs, shares, rows):
     chip = lax.axis_index("ent") // 2
     ids = jnp.concatenate([mine_ref[...], theirs_ref[...]], axis=1)
     d = jnp.concatenate([keep_ref[...], got_ref[...]], axis=0)
     n = ids.shape[1]
     iota = lax.broadcasted_iota(I32, (rows, n), 0)
-    for p in range(peers):
-        base = (chip ^ p) * rows
+    for out, (p, first) in zip(outs, shares):
+        base = (chip ^ p) * (rows * (2 if p == 0 else 1)) + first
         hot = jnp.where(iota == ids - base, 1.0, 0.0).astype(BF16)
-        outs[p][...] = jnp.dot(hot, d, preferred_element_type=F32).astype(outs[p].dtype)
-
-
-def combine_kernel(own_ref, *refs, peers, cols):
+        out[...] = jnp.dot(hot, d, preferred_element_type=F32).astype(out.dtype)
+
+
+def combine_kernel(low_ref, high_ref, *refs, peers, cols):
     got_refs, (left_ref, right_ref, keep_ref), outs = refs[: peers - 1], refs[peers - 1 : peers + 2], refs[peers + 2 :]
-    rows = own_ref.shape[0]
-    total = own_ref[...]
+    total = jnp.concatenate([low_ref[...], high_ref[...]], axis=0)
+    rows = total.shape[0]
     for got_ref in got_refs:
         total = total + got_ref[...].astype(F32)
     final = total.astype(BF16)
@@ -325,18 +325,23 @@
         name="entity",
     )(w, q, cosine, sine, owner_l, row_l, *tables)
 
-    parts = pl.pallas_call(
-        functools.partial(scatter_kernel, peers=peers, rows=rows),
-        in_specs=[vm] * 4,
-        out_specs=[vm] * peers,
-        out_shape=[jax.ShapeDtypeStruct((rows, quarter), F32 if p == 0 else BF16) for p in range(peers)],
-        compiler_params=params(),
-        cost_estimate=cost(4 * n * rels * quarter, 4 * n * quarter + 2 * rels * quarter),
-        name="scatter",
-    )(rel_l, rel_mate, keep, got)
-
+    def scatter(shares, rows, dtype, work):
+        return pl.pallas_call(
+            functools.partial(scatter_kernel, shares=shares, rows=rows),
+            in_specs=[vm] * 4,
+            out_specs=[vm] * len(shares),
+            out_shape=[jax.ShapeDtypeStruct((rows, quarter), dtype)] * len(shares),
+            compiler_params=params(),
+            cost_estimate=work,
+            name="scatter",
+        )(rel_l, rel_mate, keep, got)
+
+    parts = scatter([(p, 0) for p in range(1, peers)], rows, BF16, cost(4 * n * rels * quarter, 4 * n * quarter + 2 * rels * quarter))
     *parts, ent_keep, ent_send = lax.optimization_barrier((*parts, ent_keep, ent_send))
 
+    parts = [None, *parts]
+    low, = scatter([(0, 0)], rows // 2, F32, cost(10**9, 8 * n * quarter))
+    high, = scatter([(0, rows // 2)], rows // 2, F32, cost(10**9, 8 * n * quarter))
     received = swap_each(parts, ORD["ydx"])
 
     left, right = ent_keep, swap(ent_send, 1)
@@ -347,14 +352,14 @@
     extra = span * width // quarter
     ent_own, *messages = pl.pallas_call(
         functools.partial(combine_kernel, peers=peers, cols=quarter),
-        in_specs=[vm] * (peers + 2),
+        in_specs=[vm] * (peers + 3),
         out_specs=[vm] * (peers + 1),
         out_shape=[jax.ShapeDtypeStruct((span, width), F32), jax.ShapeDtypeStruct((rows, quarter), BF16)]
         + [jax.ShapeDtypeStruct((rows + extra, quarter), BF16)] * (peers - 1),
         compiler_params=params(),
         cost_estimate=cost(4 * rows * quarter, 16 * rows * quarter),
         name="combine",
-    )(parts[0], *received, left, right)
+    )(low, high, *received, left, right)
     final, far = messages[0], swap_each(messages, ORD["dxy"])
     mine = jnp.concatenate([final] + [x[:rows] for x in far], axis=0)
     left, right = pl.pallas_call(

time: 39.1 us -> 39 us (level)
  waiting for transfers between devices: 11 us -> 10.4 us
    ppermute x14, waiting for transfers between devices: 10.9 us -> 10.3 us  [swap(): return lax.ppermute(x, 'ent', [(i, i ^ k) for i in range(n_ent)])]
    pallas_call x1 -> x3, Pallas kernels: 0.71 us -> 1.07 us  [scatter(): pl.pallas_call(functools.partial(scatter_kernel, shares=shares, rows=rows...]
  transfers between devices with their start and end apart: 16 -> 16, of which waited for: 9 -> 9; matrix products, arithmetic and copies ran while one was open for 0% -> 0% of each run, Pallas kernels for 16% -> 18%
where the time goes in v4:
time: 39 us; the launch traced here: 38.9 us
  starting transfers between devices  17.2 us (44%)
  waiting for transfers between devices  10.4 us (27%)
  Pallas kernels  9.58 us (25%)
  between operations  0.86 us (2%)
  other arithmetic  0.68 us (2%)
    ppermute x14, starting transfers between devices, swap(): return lax.ppermute(x, 'ent', [(i, i ^ k) for i in range(n_ent)])  12.9 us
    ppermute x14, waiting for transfers between devices, swap(): return lax.ppermute(x, 'ent', [(i, i ^ k) for i in range(n_ent)])  10.3 us
    ppermute x2, starting transfers between devices, swap_rel(): return lax.ppermute(x, 'rel', [(i, i ^ k) for i in range(n_rel)])  4.3 us
    pallas_call x1, Pallas kernels, local(): pl.pallas_call(functools.partial(prepare_kernel, rows_ent=rows_ent, owner...  3.02 us
    pallas_call x1, Pallas kernels, local(): pl.pallas_call(functools.partial(score_kernel, peers=peers, block=block),...  2.09 us
    pallas_call x2, Pallas kernels, place(): pl.pallas_call(functools.partial(place_kernel, side=side, peers=peers, ro...  2.03 us
    pallas_call x1, Pallas kernels, local(): pl.pallas_call(functools.partial(entity_kernel, peers=peers, n_rel=n_rel,...  1.27 us
    pallas_call x3, Pallas kernels, scatter(): pl.pallas_call(functools.partial(scatter_kernel, shares=shares, rows=rows...  1.07 us
  transfers between devices with their start and end apart: 16, of which 9 were waited for; matrix products, arithmetic and copies ran while one was open for 0% of the time, Pallas kernels for 18%

profile of v4, /device:TPU:0, one launch (start us, length us, event | category | flops | bytes accessed | tf_op | source)
XLA Modules:
  0.0 38.9 jit_solution(10640868783860854863)
XLA Ops:
  0.6 0.0 copy-start.2
  0.6 3.0 %collective-permute-start = (bf16[16,1024]{1,0:T(8,128)(2,1)}, bf16[16,1024]{1,0:T(8,128)(2,1)S(1)}, u32[]{:S(2)}, u32[]{:S(2)}) collective-permute-start(bf16[16,1024]{1,0:T(8,128)(2,1)} %table_hbm.1), channel_id=1, source_target_pairs={{0,16},{4,20},{8,24},{12,28},{16,0},{20,4},{24,8},{28,12},{1,17},{... | collective-permute-start | bytes 98312 | tf_op jit(solution)/shard_map/ppermute | solution.py:252
  3.7 1.4 %collective-permute-start.2 = (bf16[16,1024]{1,0:T(8,128)(2,1)}, bf16[16,1024]{1,0:T(8,128)(2,1)S(1)}, u32[]{:S(2)}, u32[]{:S(2)}) collective-permute-start(bf16[16,1024]{1,0:T(8,128)(2,1)} %table_hbm.1), channel_id=1, source_target_pairs={{0,24},{4,28},{8,16},{12,20},{16,8},{20,12},{24,0},{28,4},{1,25},{... | collective-permute-start | bytes 98312 | tf_op jit(solution)/shard_map/ppermute | solution.py:252
  5.1 0.1 collective-permute-start.1
  5.2 0.0 copy-start
  5.2 0.0 copy-start.1
  5.2 3.0 %prepare.1 = (f32[512,512]{1,0:T(8,128)S(1)}, f32[512,512]{1,0:T(8,128)S(1)}, s32[512,128]{1,0:T(8,128)S(1)}, bf16[16,1024]{1,0:T(8,128)(2,1)S(1)}) custom-call(s32[512]{0:T(512)} %rel_hbm.1, f32[1024,512]{1,0:T(8,128)} %phases_hbm.1, s32[1,512]{1,0:T(1,128)} %bitcast.5, s32[1,512]{1,0:T(1,128)} %bitcast.7, s32[1,512]{1,0:T(1,128)} %bitcast.14, ...), custom_call_target="tpu_custom_call" | custom-call | flops 7864320 | bytes 3145728 | tf_op jit(solution)/shard_map/prepare/pallas_call | solution.py:279
  8.3 0.0 collective-permute-done
  8.3 0.6 %collective-permute-done.2 = bf16[16,1024]{1,0:T(8,128)(2,1)S(1)} collective-permute-done((bf16[16,1024]{1,0:T(8,128)(2,1)}, bf16[16,1024]{1,0:T(8,128)(2,1)S(1)}, u32[]{:S(2)}, u32[]{:S(2)}) %collective-permute-start.2) | collective-permute-done | bytes 32800 | tf_op jit(solution)/shard_map/ppermute | solution.py:252
  8.8 0.4 collective-permute-done.1
  9.3 0.1 collective-permute-start.3
  9.3 0.0 copy-done.2
  9.4 0.5 %collective-permute-start.4 = (s32[1,512]{1,0:T(1,128)S(1)}, s32[1,512]{1,0:T(1,128)S(1)}, u32[]{:S(2)}, u32[]{:S(2)}) collective-permute-start(s32[1,512]{1,0:T(1,128)S(1)} %bitcast.9), channel_id=1, source_target_pairs={{0,4},{4,0},{8,12},{12,8},{16,20},{20,16},{24,28},{28,24},{1,5},{5... | collective-permute-start | bytes 6152 | tf_op jit(solution)/shard_map/ppermute | solution.py:252
  9.8 0.8 %collective-permute-done.4.theirs_ref = s32[1,512]{1,0:T(1,128)S(1)} collective-permute-done((s32[1,512]{1,0:T(1,128)S(1)}, s32[1,512]{1,0:T(1,128)S(1)}, u32[]{:S(2)}, u32[]{:S(2)}) %collective-permute-start.4) | collective-permute-done | bytes 2080 | tf_op jit(solution)/shard_map/ppermute | solution.py:252
  10.7 0.0 collective-permute-done.3.refs_1_
  10.7 2.1 %score.1 = (bf16[512,256]{1,0:T(8,128)(2,1)S(1)}, bf16[512,256]{1,0:T(8,128)(2,1)S(1)}, bf16[512,128]{1,0:T(8,128)(2,1)S(1)}, bf16[512,1024]{1,0:T(8,128)(2,1)S(1)}) custom-call(bf16[64,1024]{1,0:T(8,128)(2,1)S(1)} %constant_dynamic-update-slice_fusion.refs_0_, bf16[64,1024]{1,0:T(8,128)(2,1)S(1)} %collective-permute-done.3.refs_1_, ...), custom_call_target="tpu_custom_call" | custom-call | flops 402653184 | bytes 6291456 | tf_op jit(solution)/shard_map/score/pallas_call | solution.py:301
  12.8 0.4 collective-permute-start.5
  13.2 0.0 copy-done
  13.2 0.0 copy-done.1
  13.2 1.3 %entity.1 = (f32[64,1024]{1,0:T(8,128)S(1)}, f32[64,1024]{1,0:T(8,128)S(1)}) custom-call(bf16[512,128]{1,0:T(8,128)(2,1)S(1)} %get-tuple-element.69.w_ref, bf16[512,1024]{1,0:T(8,128)(2,1)S(1)} %get-tuple-element.70.q_ref, f32[512,512]{1,0:T(8,128)S(1)} %get-tuple-element.61.refs_2_.cos_ref, f32[512,512]{1,0:T(8,128)S(1)} %get-tuple-element.62.refs_3_.sin_ref, ...), custom_call_target="tpu_custom_call" | custom-call | flops 402653184 | bytes 2621440 | tf_op jit(solution)/shard_map/entity/pallas_call | solution.py:317
  14.4 0.0 collective-permute-done.5.got_ref
  14.4 0.6 %scatter.5 = (bf16[256,256]{1,0:T(8,128)(2,1)S(1)}, bf16[256,256]{1,0:T(8,128)(2,1)S(1)}, bf16[256,256]{1,0:T(8,128)(2,1)S(1)}) custom-call(s32[1,512]{1,0:T(1,128)S(1)} %bitcast.10, s32[1,512]{1,0:T(1,128)S(1)} %collective-permute-done.4.theirs_ref, bf16[512,256]{1,0:T(8,128)(2,1)S(1)} %get-tuple-element.64.keep_ref, ...), custom_call_target="tpu_custom_call" | custom-call | flops 536870912 | bytes 1048576 | tf_op jit(solution)/shard_map/scatter/pallas_call | solution.py:329
  15.0 0.3 collective-permute-start.9
  15.3 1.5 %collective-permute-start.6 = (bf16[256,256]{1,0:T(8,128)(2,1)S(1)}, bf16[256,256]{1,0:T(8,128)(2,1)S(1)}, u32[]{:S(2)}, u32[]{:S(2)}) collective-permute-start(bf16[256,256]{1,0:T(8,128)(2,1)S(1)} %get-tuple-element.73), channel_id=1, source_target_pairs={{0,16},{4,20},{8,24},{12,28},{16,0},{20,4},{24,8},{28,12},{1,17},{... | collective-permute-start | bytes 393224 | tf_op jit(solution)/shard_map/ppermute | solution.py:252
  16.9 0.9 %collective-permute-start.7 = (bf16[256,256]{1,0:T(8,128)(2,1)S(1)}, bf16[256,256]{1,0:T(8,128)(2,1)S(1)}, u32[]{:S(2)}, u32[]{:S(2)}) collective-permute-start(bf16[256,256]{1,0:T(8,128)(2,1)S(1)} %get-tuple-element.74), channel_id=1, source_target_pairs={{0,24},{4,28},{8,16},{12,20},{16,8},{20,12},{24,0},{28,4},{1,25},{... | collective-permute-start | bytes 393224 | tf_op jit(solution)/shard_map/ppermute | solution.py:252
  17.8 1.0 %collective-permute-start.8 = (bf16[256,256]{1,0:T(8,128)(2,1)S(1)}, bf16[256,256]{1,0:T(8,128)(2,1)S(1)}, u32[]{:S(2)}, u32[]{:S(2)}) collective-permute-start(bf16[256,256]{1,0:T(8,128)(2,1)S(1)} %get-tuple-element.75), channel_id=1, source_target_pairs={{0,8},{4,12},{8,0},{12,4},{16,24},{20,28},{24,16},{28,20},{1,9},{5... | collective-permute-start | bytes 393224 | tf_op jit(solution)/shard_map/ppermute | solution.py:252
  18.8 0.2 scatter.4.high_ref
  19.1 0.0 collective-permute-done.9
  19.2 2.7 %collective-permute-start.10 = (bf16[32,1024]{1,0:T(8,128)(2,1)S(1)}, bf16[32,1024]{1,0:T(8,128)(2,1)S(1)}, u32[]{:S(2)}, u32[]{:S(2)}) collective-permute-start(bf16[32,1024]{1,0:T(8,128)(2,1)S(1)} %slice.24), channel_id=1, source_target_pairs={{0,2},{1,3},{2,0},{3,1},{4,6},{5,7},{6,4},{7,5},{8,10},{9,11},{10,... | collective-permute-start | bytes 196616 | tf_op jit(solution)/shard_map/ppermute | solution.py:267
  21.8 0.2 scatter.3.low_ref
  22.1 1.4 %collective-permute-done.6.refs_1_ = bf16[256,256]{1,0:T(8,128)(2,1)S(1)} collective-permute-done((bf16[256,256]{1,0:T(8,128)(2,1)S(1)}, bf16[256,256]{1,0:T(8,128)(2,1)S(1)}, u32[]{:S(2)}, u32[]{:S(2)}) %collective-permute-start.6) | collective-permute-done | bytes 131104 | tf_op jit(solution)/shard_map/ppermute | solution.py:252
  23.5 0.7 %collective-permute-done.7.refs_2_ = bf16[256,256]{1,0:T(8,128)(2,1)S(1)} collective-permute-done((bf16[256,256]{1,0:T(8,128)(2,1)S(1)}, bf16[256,256]{1,0:T(8,128)(2,1)S(1)}, u32[]{:S(2)}, u32[]{:S(2)}) %collective-permute-start.7) | collective-permute-done | bytes 131104 | tf_op jit(solution)/shard_map/ppermute | solution.py:252
  24.2 0.9 %collective-permute-done.8.refs_0_ = bf16[256,256]{1,0:T(8,128)(2,1)S(1)} collective-permute-done((bf16[256,256]{1,0:T(8,128)(2,1)S(1)}, bf16[256,256]{1,0:T(8,128)(2,1)S(1)}, u32[]{:S(2)}, u32[]{:S(2)}) %collective-permute-start.8) | collective-permute-done | bytes 131104 | tf_op jit(solution)/shard_map/ppermute | solution.py:252
  25.1 0.0 collective-permute-done.10.refs_4_
  25.1 0.1 combine.1
  25.2 2.0 %collective-permute-start.11 = (bf16[288,256]{1,0:T(8,128)(2,1)S(1)}, bf16[288,256]{1,0:T(8,128)(2,1)S(1)}, u32[]{:S(2)}, u32[]{:S(2)}) collective-permute-start(bf16[288,256]{1,0:T(8,128)(2,1)S(1)} %get-tuple-element.82), channel_id=1, source_target_pairs={{0,24},{4,28},{8,16},{12,20},{16,8},{20,12},{24,0},{28,4},{1,25},{... | collective-permute-start | bytes 442376 | tf_op jit(solution)/shard_map/ppermute | solution.py:252
  27.2 1.0 %collective-permute-start.12 = (bf16[288,256]{1,0:T(8,128)(2,1)S(1)}, bf16[288,256]{1,0:T(8,128)(2,1)S(1)}, u32[]{:S(2)}, u32[]{:S(2)}) collective-permute-start(bf16[288,256]{1,0:T(8,128)(2,1)S(1)} %get-tuple-element.83), channel_id=1, source_target_pairs={{0,8},{4,12},{8,0},{12,4},{16,24},{20,28},{24,16},{28,20},{1,9},{5... | collective-permute-start | bytes 442376 | tf_op jit(solution)/shard_map/ppermute | solution.py:252
  28.2 0.5 %collective-permute-start.13 = (bf16[288,256]{1,0:T(8,128)(2,1)S(1)}, bf16[288,256]{1,0:T(8,128)(2,1)S(1)}, u32[]{:S(2)}, u32[]{:S(2)}) collective-permute-start(bf16[288,256]{1,0:T(8,128)(2,1)S(1)} %get-tuple-element.84), channel_id=1, source_target_pairs={{0,16},{4,20},{8,24},{12,28},{16,0},{20,4},{24,8},{28,12},{1,17},{... | collective-permute-start | bytes 442376 | tf_op jit(solution)/shard_map/ppermute | solution.py:252
  28.7 3.9 %collective-permute-done.11.refs_2_ = bf16[288,256]{1,0:T(8,128)(2,1)S(1)} collective-permute-done((bf16[288,256]{1,0:T(8,128)(2,1)S(1)}, bf16[288,256]{1,0:T(8,128)(2,1)S(1)}, u32[]{:S(2)}, u32[]{:S(2)}) %collective-permute-start.11) | collective-permute-done | bytes 147488 | tf_op jit(solution)/shard_map/ppermute | solution.py:252
  32.6 1.6 %collective-permute-done.12.refs_0_ = bf16[288,256]{1,0:T(8,128)(2,1)S(1)} collective-permute-done((bf16[288,256]{1,0:T(8,128)(2,1)S(1)}, bf16[288,256]{1,0:T(8,128)(2,1)S(1)}, u32[]{:S(2)}, u32[]{:S(2)}) %collective-permute-start.12) | collective-permute-done | bytes 147488 | tf_op jit(solution)/shard_map/ppermute | solution.py:252
  34.2 0.0 collective-permute-done.13.refs_1_
  34.3 0.1 collective-permute-start.14
  34.4 1.6 %collective-permute-start.15 = (f32[4,1024]{1,0:T(4,128)S(1)}, f32[4,1024]{1,0:T(4,128)S(1)}, u32[]{:S(2)}, u32[]{:S(2)}) collective-permute-start(f32[4,1024]{1,0:T(4,128)S(1)} %get-tuple-element.90), channel_id=1, source_target_pairs={{0,1},{1,0},{2,3},{3,2},{4,5},{5,4},{6,7},{7,6},{8,9},{9,8},{10,11... | collective-permute-start | bytes 49160 | tf_op jit(solution)/shard_map/ppermute | solution.py:267
  36.1 1.0 %place.2.refs_0_ = f32[1024,512]{1,0:T(8,128)} custom-call(bf16[1024,256]{1,0:T(8,128)(2,1)S(1)} %pad_maximum_fusion.src_ref), custom_call_target="tpu_custom_call" | custom-call | flops 524288 | bytes 3145728 | tf_op jit(solution)/shard_map/place/pallas_call | solution.py:380
  37.1 0.0 collective-permute-done.14.src_ref
  37.1 1.0 %place.3 = f32[1024,512]{1,0:T(8,128)} custom-call(bf16[1024,256]{1,0:T(8,128)(2,1)S(1)} %collective-permute-done.14.src_ref, f32[1024,512]{1,0:T(8,128)} %place.2.refs_0_), custom_call_target="tpu_custom_call", output_to_operand_aliasing={{}: (1, {})} | custom-call | flops 524288 | bytes 3145728 | tf_op jit(solution)/shard_map/place/pallas_call | solution.py:380
  38.1 0.1 collective-permute-done.15
  38.3 0.6 %add.8 = f32[4,1024]{1,0:T(4,128)} add(f32[4,1024]{1,0:T(4,128)S(1)} %get-tuple-element.91, f32[4,1024]{1,0:T(4,128)S(1)} %collective-permute-done.15) | non-fusion elementwise | flops 4096 | bytes 49152 | tf_op jit(solution)/shard_map/add | solution.py:394
  (12 shorter events, 0.1 us)
Async XLA Ops:
  0.6 8.7 %copy-start.2 = (s32[512]{0:T(512)S(1)}, s32[512]{0:T(512)}, u32[]{:S(2)}) copy-start(s32[512]{0:T(512)} %rel_hbm.1) | copy-start | bytes 6148
  0.6 7.6 %collective-permute-start = (bf16[16,1024]{1,0:T(8,128)(2,1)}, bf16[16,1024]{1,0:T(8,128)(2,1)S(1)}, u32[]{:S(2)}, u32[]{:S(2)}) collective-permute-start(bf16[16,1024]{1,0:T(8,128)(2,1)} %table_hbm.1), channel_id=1, source_target_pairs={{0,16},{4,20},{8,24},{12,28},{16,0},{20,4},{24,8},{28,12},{1,17},{... | collective-permute-start | bytes 98312 | tf_op jit(solution)/shard_map/ppermute | solution.py:252
  3.7 5.2 %collective-permute-start.2 = (bf16[16,1024]{1,0:T(8,128)(2,1)}, bf16[16,1024]{1,0:T(8,128)(2,1)S(1)}, u32[]{:S(2)}, u32[]{:S(2)}) collective-permute-start(bf16[16,1024]{1,0:T(8,128)(2,1)} %table_hbm.1), channel_id=1, source_target_pairs={{0,24},{4,28},{8,16},{12,20},{16,8},{20,12},{24,0},{28,4},{1,25},{... | collective-permute-start | bytes 98312 | tf_op jit(solution)/shard_map/ppermute | solution.py:252
  5.1 4.1 %collective-permute-start.1 = (bf16[16,1024]{1,0:T(8,128)(2,1)}, bf16[16,1024]{1,0:T(8,128)(2,1)S(1)}, u32[]{:S(2)}, u32[]{:S(2)}) collective-permute-start(bf16[16,1024]{1,0:T(8,128)(2,1)} %table_hbm.1), channel_id=1, source_target_pairs={{0,8},{4,12},{8,0},{12,4},{16,24},{20,28},{24,16},{28,20},{1,9},{5... | collective-permute-start | bytes 98312 | tf_op jit(solution)/shard_map/ppermute | solution.py:252
  5.2 7.9 %copy-start = (s32[512,1]{0,1:T(1,128)S(1)}, s32[512,1]{0,1:T(1,128)}, u32[]{:S(2)}) copy-start(s32[512,1]{0,1:T(1,128)} %param.9) | copy-start | bytes 6148
  5.2 7.9 %copy-start.1 = (s32[512]{0:T(512)S(1)}, s32[512]{0:T(512)}, u32[]{:S(2)}) copy-start(s32[512]{0:T(512)} %param.10) | copy-start | bytes 6148
  9.3 1.4 %collective-permute-start.3 = (bf16[64,1024]{1,0:T(8,128)(2,1)S(1)}, bf16[64,1024]{1,0:T(8,128)(2,1)S(1)}, u32[]{:S(2)}, u32[]{:S(2)}) collective-permute-start(bf16[64,1024]{1,0:T(8,128)(2,1)S(1)} %constant_dynamic-update-slice_fusion.refs_0_), channel_id=1, source_target_pairs={{0,4},{4,0},{8,12},{12,8},{16,20},{20,16},{24,28},{28,24},{1,5},{5... | collective-permute-start | bytes 393224 | tf_op jit(solution)/shard_map/ppermute | solution.py:252
  9.4 1.3 %collective-permute-start.4 = (s32[1,512]{1,0:T(1,128)S(1)}, s32[1,512]{1,0:T(1,128)S(1)}, u32[]{:S(2)}, u32[]{:S(2)}) collective-permute-start(s32[1,512]{1,0:T(1,128)S(1)} %bitcast.9), channel_id=1, source_target_pairs={{0,4},{4,0},{8,12},{12,8},{16,20},{20,16},{24,28},{28,24},{1,5},{5... | collective-permute-start | bytes 6152 | tf_op jit(solution)/shard_map/ppermute | solution.py:252
  12.8 1.7 %collective-permute-start.5 = (bf16[512,256]{1,0:T(8,128)(2,1)S(1)}, bf16[512,256]{1,0:T(8,128)(2,1)S(1)}, u32[]{:S(2)}, u32[]{:S(2)}) collective-permute-start(bf16[512,256]{1,0:T(8,128)(2,1)S(1)} %get-tuple-element.65), channel_id=1, source_target_pairs={{0,4},{4,0},{8,12},{12,8},{16,20},{20,16},{24,28},{28,24},{1,5},{5... | collective-permute-start | bytes 786440 | tf_op jit(solution)/shard_map/ppermute | solution.py:252
  15.0 4.0 %collective-permute-start.9 = (f32[64,1024]{1,0:T(8,128)S(1)}, f32[64,1024]{1,0:T(8,128)S(1)}, u32[]{:S(2)}, u32[]{:S(2)}) collective-permute-start(f32[64,1024]{1,0:T(8,128)S(1)} %get-tuple-element.80), channel_id=1, source_target_pairs={{0,4},{4,0},{8,12},{12,8},{16,20},{20,16},{24,28},{28,24},{1,5},{5... | collective-permute-start | bytes 786440 | tf_op jit(solution)/shard_map/ppermute | solution.py:252
  15.3 8.1 %collective-permute-start.6 = (bf16[256,256]{1,0:T(8,128)(2,1)S(1)}, bf16[256,256]{1,0:T(8,128)(2,1)S(1)}, u32[]{:S(2)}, u32[]{:S(2)}) collective-permute-start(bf16[256,256]{1,0:T(8,128)(2,1)S(1)} %get-tuple-element.73), channel_id=1, source_target_pairs={{0,16},{4,20},{8,24},{12,28},{16,0},{20,4},{24,8},{28,12},{1,17},{... | collective-permute-start | bytes 393224 | tf_op jit(solution)/shard_map/ppermute | solution.py:252
  16.9 7.3 %collective-permute-start.7 = (bf16[256,256]{1,0:T(8,128)(2,1)S(1)}, bf16[256,256]{1,0:T(8,128)(2,1)S(1)}, u32[]{:S(2)}, u32[]{:S(2)}) collective-permute-start(bf16[256,256]{1,0:T(8,128)(2,1)S(1)} %get-tuple-element.74), channel_id=1, source_target_pairs={{0,24},{4,28},{8,16},{12,20},{16,8},{20,12},{24,0},{28,4},{1,25},{... | collective-permute-start | bytes 393224 | tf_op jit(solution)/shard_map/ppermute | solution.py:252
  17.8 7.3 %collective-permute-start.8 = (bf16[256,256]{1,0:T(8,128)(2,1)S(1)}, bf16[256,256]{1,0:T(8,128)(2,1)S(1)}, u32[]{:S(2)}, u32[]{:S(2)}) collective-permute-start(bf16[256,256]{1,0:T(8,128)(2,1)S(1)} %get-tuple-element.75), channel_id=1, source_target_pairs={{0,8},{4,12},{8,0},{12,4},{16,24},{20,28},{24,16},{28,20},{1,9},{5... | collective-permute-start | bytes 393224 | tf_op jit(solution)/shard_map/ppermute | solution.py:252
  19.2 5.9 %collective-permute-start.10 = (bf16[32,1024]{1,0:T(8,128)(2,1)S(1)}, bf16[32,1024]{1,0:T(8,128)(2,1)S(1)}, u32[]{:S(2)}, u32[]{:S(2)}) collective-permute-start(bf16[32,1024]{1,0:T(8,128)(2,1)S(1)} %slice.24), channel_id=1, source_target_pairs={{0,2},{1,3},{2,0},{3,1},{4,6},{5,7},{6,4},{7,5},{8,10},{9,11},{10,... | collective-permute-start | bytes 196616 | tf_op jit(solution)/shard_map/ppermute | solution.py:267
  25.2 7.5 %collective-permute-start.11 = (bf16[288,256]{1,0:T(8,128)(2,1)S(1)}, bf16[288,256]{1,0:T(8,128)(2,1)S(1)}, u32[]{:S(2)}, u32[]{:S(2)}) collective-permute-start(bf16[288,256]{1,0:T(8,128)(2,1)S(1)} %get-tuple-element.82), channel_id=1, source_target_pairs={{0,24},{4,28},{8,16},{12,20},{16,8},{20,12},{24,0},{28,4},{1,25},{... | collective-permute-start | bytes 442376 | tf_op jit(solution)/shard_map/ppermute | solution.py:252
  27.2 7.1 %collective-permute-start.12 = (bf16[288,256]{1,0:T(8,128)(2,1)S(1)}, bf16[288,256]{1,0:T(8,128)(2,1)S(1)}, u32[]{:S(2)}, u32[]{:S(2)}) collective-permute-start(bf16[288,256]{1,0:T(8,128)(2,1)S(1)} %get-tuple-element.83), channel_id=1, source_target_pairs={{0,8},{4,12},{8,0},{12,4},{16,24},{20,28},{24,16},{28,20},{1,9},{5... | collective-permute-start | bytes 442376 | tf_op jit(solution)/shard_map/ppermute | solution.py:252
  28.2 6.0 %collective-permute-start.13 = (bf16[288,256]{1,0:T(8,128)(2,1)S(1)}, bf16[288,256]{1,0:T(8,128)(2,1)S(1)}, u32[]{:S(2)}, u32[]{:S(2)}) collective-permute-start(bf16[288,256]{1,0:T(8,128)(2,1)S(1)} %get-tuple-element.84), channel_id=1, source_target_pairs={{0,16},{4,20},{8,24},{12,28},{16,0},{20,4},{24,8},{28,12},{1,17},{... | collective-permute-start | bytes 442376 | tf_op jit(solution)/shard_map/ppermute | solution.py:252
  34.3 2.8 %collective-permute-start.14 = (bf16[1024,256]{1,0:T(8,128)(2,1)S(1)}, bf16[1024,256]{1,0:T(8,128)(2,1)S(1)}, u32[]{:S(2)}, u32[]{:S(2)}) collective-permute-start(bf16[1024,256]{1,0:T(8,128)(2,1)S(1)} %pad_maximum_fusion.src_ref), channel_id=1, source_target_pairs={{0,4},{4,0},{8,12},{12,8},{16,20},{20,16},{24,28},{28,24},{1,5},{5... | collective-permute-start | bytes 1572872 | tf_op jit(solution)/shard_map/ppermute | solution.py:252
  34.4 3.8 %collective-permute-start.15 = (f32[4,1024]{1,0:T(4,128)S(1)}, f32[4,1024]{1,0:T(4,128)S(1)}, u32[]{:S(2)}, u32[]{:S(2)}) collective-permute-start(f32[4,1024]{1,0:T(4,128)S(1)} %get-tuple-element.90), channel_id=1, source_target_pairs={{0,1},{1,0},{2,3},{3,2},{4,5},{5,4},{6,7},{7,6},{8,9},{9,8},{10,11... | collective-permute-start | bytes 49160 | tf_op jit(solution)/shard_map/ppermute | solution.py:267

commit v5 on v4

--- a/solution.py
+++ b/solution.py
@@ -274,7 +274,7 @@
     rel_l = relation.reshape(1, n)
     tail_l = tail_ids.reshape(1, n)
     known_l = known_tails.T
-    far = swap_each([entity_table] * peers, ORD["yxd"])
+    far = swap_each([entity_table] * peers, ORD["xyd"])
     fetched = [relation, phases, owner_l, row_l, tail_l, known_l, entity_table]
     cosine, sine, code, own = pl.pallas_call(
         functools.partial(prepare_kernel, rows_ent=rows_ent, owner_rows=owner_rows),
@@ -342,7 +342,7 @@
     parts = [None, *parts]
     low, = scatter([(0, 0)], rows // 2, F32, cost(10**9, 8 * n * quarter))
     high, = scatter([(0, rows // 2)], rows // 2, F32, cost(10**9, 8 * n * quarter))
-    received = swap_each(parts, ORD["ydx"])
+    received = swap_each(parts, ORD["xyd"])
 
     left, right = ent_keep, swap(ent_send, 1)
     for bit in range(n_rel.bit_length() - 2, 0, -1):

time: 39 us -> 38.3 us (0.982)
  waiting for transfers between devices: 10.4 us -> 9.8 us
    ppermute x14, waiting for transfers between devices: 10.3 us -> 9.69 us  [swap(): return lax.ppermute(x, 'ent', [(i, i ^ k) for i in range(n_ent)])]
  transfers between devices with their start and end apart: 16 -> 16, of which waited for: 9 -> 8; matrix products, arithmetic and copies ran while one was open for 0% -> 0% of each run, Pallas kernels for 18% -> 18%
where the time goes in v5:
time: 38.3 us; the launch traced here: 38.2 us
  starting transfers between devices  17.2 us (45%)
  waiting for transfers between devices  9.8 us (26%)
  Pallas kernels  9.57 us (25%)
  between operations  0.86 us (2%)
  other arithmetic  0.68 us (2%)
    ppermute x14, starting transfers between devices, swap(): return lax.ppermute(x, 'ent', [(i, i ^ k) for i in range(n_ent)])  12.9 us
    ppermute x14, waiting for transfers between devices, swap(): return lax.ppermute(x, 'ent', [(i, i ^ k) for i in range(n_ent)])  9.69 us
    ppermute x2, starting transfers between devices, swap_rel(): return lax.ppermute(x, 'rel', [(i, i ^ k) for i in range(n_rel)])  4.29 us
    pallas_call x1, Pallas kernels, local(): pl.pallas_call(functools.partial(prepare_kernel, rows_ent=rows_ent, owner...  3.02 us
    pallas_call x1, Pallas kernels, local(): pl.pallas_call(functools.partial(score_kernel, peers=peers, block=block),...  2.08 us
    pallas_call x2, Pallas kernels, place(): pl.pallas_call(functools.partial(place_kernel, side=side, peers=peers, ro...  2.03 us
    pallas_call x1, Pallas kernels, local(): pl.pallas_call(functools.partial(entity_kernel, peers=peers, n_rel=n_rel,...  1.28 us
    pallas_call x3, Pallas kernels, scatter(): pl.pallas_call(functools.partial(scatter_kernel, shares=shares, rows=rows...  1.06 us
  transfers between devices with their start and end apart: 16, of which 8 were waited for; matrix products, arithmetic and copies ran while one was open for 0% of the time, Pallas kernels for 18%

profile of v5, /device:TPU:0, one launch (start us, length us, event | category | flops | bytes accessed | tf_op | source)
XLA Modules:
  0.0 38.2 jit_solution(10166745633412100450)
XLA Ops:
  0.6 0.0 copy-start.2
  0.6 3.0 %collective-permute-start = (bf16[16,1024]{1,0:T(8,128)(2,1)}, bf16[16,1024]{1,0:T(8,128)(2,1)S(1)}, u32[]{:S(2)}, u32[]{:S(2)}) collective-permute-start(bf16[16,1024]{1,0:T(8,128)(2,1)} %table_hbm.1), channel_id=1, source_target_pairs={{0,8},{4,12},{8,0},{12,4},{16,24},{20,28},{24,16},{28,20},{1,9},{5... | collective-permute-start | bytes 98312 | tf_op jit(solution)/shard_map/ppermute | solution.py:252
  3.6 1.5 %collective-permute-start.2 = (bf16[16,1024]{1,0:T(8,128)(2,1)}, bf16[16,1024]{1,0:T(8,128)(2,1)S(1)}, u32[]{:S(2)}, u32[]{:S(2)}) collective-permute-start(bf16[16,1024]{1,0:T(8,128)(2,1)} %table_hbm.1), channel_id=1, source_target_pairs={{0,24},{4,28},{8,16},{12,20},{16,8},{20,12},{24,0},{28,4},{1,25},{... | collective-permute-start | bytes 98312 | tf_op jit(solution)/shard_map/ppermute | solution.py:252
  5.1 0.0 collective-permute-start.1
  5.2 0.0 copy-start
  5.2 0.0 copy-start.1
  5.2 3.0 %prepare.1 = (f32[512,512]{1,0:T(8,128)S(1)}, f32[512,512]{1,0:T(8,128)S(1)}, s32[512,128]{1,0:T(8,128)S(1)}, bf16[16,1024]{1,0:T(8,128)(2,1)S(1)}) custom-call(s32[512]{0:T(512)} %rel_hbm.1, f32[1024,512]{1,0:T(8,128)} %phases_hbm.1, s32[1,512]{1,0:T(1,128)} %bitcast.5, s32[1,512]{1,0:T(1,128)} %bitcast.7, s32[1,512]{1,0:T(1,128)} %bitcast.14, ...), custom_call_target="tpu_custom_call" | custom-call | flops 7864320 | bytes 3145728 | tf_op jit(solution)/shard_map/prepare/pallas_call | solution.py:279
  8.2 0.0 collective-permute-done
  8.2 0.4 %collective-permute-done.2 = bf16[16,1024]{1,0:T(8,128)(2,1)S(1)} collective-permute-done((bf16[16,1024]{1,0:T(8,128)(2,1)}, bf16[16,1024]{1,0:T(8,128)(2,1)S(1)}, u32[]{:S(2)}, u32[]{:S(2)}) %collective-permute-start.2) | collective-permute-done | bytes 32800 | tf_op jit(solution)/shard_map/ppermute | solution.py:252
  8.7 0.6 %collective-permute-done.1 = bf16[16,1024]{1,0:T(8,128)(2,1)S(1)} collective-permute-done((bf16[16,1024]{1,0:T(8,128)(2,1)}, bf16[16,1024]{1,0:T(8,128)(2,1)S(1)}, u32[]{:S(2)}, u32[]{:S(2)}) %collective-permute-start.1) | collective-permute-done | bytes 32800 | tf_op jit(solution)/shard_map/ppermute | solution.py:252
  9.3 0.1 collective-permute-start.3
  9.4 0.0 copy-done.2
  9.4 0.5 %collective-permute-start.4 = (s32[1,512]{1,0:T(1,128)S(1)}, s32[1,512]{1,0:T(1,128)S(1)}, u32[]{:S(2)}, u32[]{:S(2)}) collective-permute-start(s32[1,512]{1,0:T(1,128)S(1)} %bitcast.9), channel_id=1, source_target_pairs={{0,4},{4,0},{8,12},{12,8},{16,20},{20,16},{24,28},{28,24},{1,5},{5... | collective-permute-start | bytes 6152 | tf_op jit(solution)/shard_map/ppermute | solution.py:252
  9.9 0.8 %collective-permute-done.4.theirs_ref = s32[1,512]{1,0:T(1,128)S(1)} collective-permute-done((s32[1,512]{1,0:T(1,128)S(1)}, s32[1,512]{1,0:T(1,128)S(1)}, u32[]{:S(2)}, u32[]{:S(2)}) %collective-permute-start.4) | collective-permute-done | bytes 2080 | tf_op jit(solution)/shard_map/ppermute | solution.py:252
  10.7 0.0 collective-permute-done.3.refs_1_
  10.7 2.1 %score.1 = (bf16[512,256]{1,0:T(8,128)(2,1)S(1)}, bf16[512,256]{1,0:T(8,128)(2,1)S(1)}, bf16[512,128]{1,0:T(8,128)(2,1)S(1)}, bf16[512,1024]{1,0:T(8,128)(2,1)S(1)}) custom-call(bf16[64,1024]{1,0:T(8,128)(2,1)S(1)} %constant_dynamic-update-slice_fusion.refs_0_, bf16[64,1024]{1,0:T(8,128)(2,1)S(1)} %collective-permute-done.3.refs_1_, ...), custom_call_target="tpu_custom_call" | custom-call | flops 402653184 | bytes 6291456 | tf_op jit(solution)/shard_map/score/pallas_call | solution.py:301
  12.8 0.4 %collective-permute-start.5 = (bf16[512,256]{1,0:T(8,128)(2,1)S(1)}, bf16[512,256]{1,0:T(8,128)(2,1)S(1)}, u32[]{:S(2)}, u32[]{:S(2)}) collective-permute-start(bf16[512,256]{1,0:T(8,128)(2,1)S(1)} %get-tuple-element.65), channel_id=1, source_target_pairs={{0,4},{4,0},{8,12},{12,8},{16,20},{20,16},{24,28},{28,24},{1,5},{5... | collective-permute-start | bytes 786440 | tf_op jit(solution)/shard_map/ppermute | solution.py:252
  13.2 0.0 copy-done
  13.2 0.0 copy-done.1
  13.2 1.3 %entity.1 = (f32[64,1024]{1,0:T(8,128)S(1)}, f32[64,1024]{1,0:T(8,128)S(1)}) custom-call(bf16[512,128]{1,0:T(8,128)(2,1)S(1)} %get-tuple-element.69.w_ref, bf16[512,1024]{1,0:T(8,128)(2,1)S(1)} %get-tuple-element.70.q_ref, f32[512,512]{1,0:T(8,128)S(1)} %get-tuple-element.61.refs_2_.cos_ref, f32[512,512]{1,0:T(8,128)S(1)} %get-tuple-element.62.refs_3_.sin_ref, ...), custom_call_target="tpu_custom_call" | custom-call | flops 402653184 | bytes 2621440 | tf_op jit(solution)/shard_map/entity/pallas_call | solution.py:317
  14.5 0.0 collective-permute-done.5.got_ref
  14.5 0.6 %scatter.5 = (bf16[256,256]{1,0:T(8,128)(2,1)S(1)}, bf16[256,256]{1,0:T(8,128)(2,1)S(1)}, bf16[256,256]{1,0:T(8,128)(2,1)S(1)}) custom-call(s32[1,512]{1,0:T(1,128)S(1)} %bitcast.10, s32[1,512]{1,0:T(1,128)S(1)} %collective-permute-done.4.theirs_ref, bf16[512,256]{1,0:T(8,128)(2,1)S(1)} %get-tuple-element.64.keep_ref, ...), custom_call_target="tpu_custom_call" | custom-call | flops 536870912 | bytes 1048576 | tf_op jit(solution)/shard_map/scatter/pallas_call | solution.py:329
  15.1 0.3 collective-permute-start.9
  15.4 1.5 %collective-permute-start.6 = (bf16[256,256]{1,0:T(8,128)(2,1)S(1)}, bf16[256,256]{1,0:T(8,128)(2,1)S(1)}, u32[]{:S(2)}, u32[]{:S(2)}) collective-permute-start(bf16[256,256]{1,0:T(8,128)(2,1)S(1)} %get-tuple-element.73), channel_id=1, source_target_pairs={{0,8},{4,12},{8,0},{12,4},{16,24},{20,28},{24,16},{28,20},{1,9},{5... | collective-permute-start | bytes 393224 | tf_op jit(solution)/shard_map/ppermute | solution.py:252
  16.9 1.0 %collective-permute-start.7 = (bf16[256,256]{1,0:T(8,128)(2,1)S(1)}, bf16[256,256]{1,0:T(8,128)(2,1)S(1)}, u32[]{:S(2)}, u32[]{:S(2)}) collective-permute-start(bf16[256,256]{1,0:T(8,128)(2,1)S(1)} %get-tuple-element.74), channel_id=1, source_target_pairs={{0,16},{4,20},{8,24},{12,28},{16,0},{20,4},{24,8},{28,12},{1,17},{... | collective-permute-start | bytes 393224 | tf_op jit(solution)/shard_map/ppermute | solution.py:252
  17.9 1.0 %collective-permute-start.8 = (bf16[256,256]{1,0:T(8,128)(2,1)S(1)}, bf16[256,256]{1,0:T(8,128)(2,1)S(1)}, u32[]{:S(2)}, u32[]{:S(2)}) collective-permute-start(bf16[256,256]{1,0:T(8,128)(2,1)S(1)} %get-tuple-element.75), channel_id=1, source_target_pairs={{0,24},{4,28},{8,16},{12,20},{16,8},{20,12},{24,0},{28,4},{1,25},{... | collective-permute-start | bytes 393224 | tf_op jit(solution)/shard_map/ppermute | solution.py:252
  18.9 0.2 scatter.4.high_ref
  19.1 0.0 collective-permute-done.9
  19.2 2.6 %collective-permute-start.10 = (bf16[32,1024]{1,0:T(8,128)(2,1)S(1)}, bf16[32,1024]{1,0:T(8,128)(2,1)S(1)}, u32[]{:S(2)}, u32[]{:S(2)}) collective-permute-start(bf16[32,1024]{1,0:T(8,128)(2,1)S(1)} %slice.24), channel_id=1, source_target_pairs={{0,2},{1,3},{2,0},{3,1},{4,6},{5,7},{6,4},{7,5},{8,10},{9,11},{10,... | collective-permute-start | bytes 196616 | tf_op jit(solution)/shard_map/ppermute | solution.py:267
  21.8 0.2 scatter.3.low_ref
  22.1 0.0 collective-permute-done.6.refs_0_
  22.1 3.0 %collective-permute-done.7.refs_1_ = bf16[256,256]{1,0:T(8,128)(2,1)S(1)} collective-permute-done((bf16[256,256]{1,0:T(8,128)(2,1)S(1)}, bf16[256,256]{1,0:T(8,128)(2,1)S(1)}, u32[]{:S(2)}, u32[]{:S(2)}) %collective-permute-start.7) | collective-permute-done | bytes 131104 | tf_op jit(solution)/shard_map/ppermute | solution.py:252
  25.1 0.0 collective-permute-done.8.refs_2_
  25.1 0.0 collective-permute-done.10.refs_4_
  25.1 0.1 combine.1
  25.2 1.5 %collective-permute-start.11 = (bf16[288,256]{1,0:T(8,128)(2,1)S(1)}, bf16[288,256]{1,0:T(8,128)(2,1)S(1)}, u32[]{:S(2)}, u32[]{:S(2)}) collective-permute-start(bf16[288,256]{1,0:T(8,128)(2,1)S(1)} %get-tuple-element.82), channel_id=1, source_target_pairs={{0,24},{4,28},{8,16},{12,20},{16,8},{20,12},{24,0},{28,4},{1,25},{... | collective-permute-start | bytes 442376 | tf_op jit(solution)/shard_map/ppermute | solution.py:252
  26.6 1.0 %collective-permute-start.12 = (bf16[288,256]{1,0:T(8,128)(2,1)S(1)}, bf16[288,256]{1,0:T(8,128)(2,1)S(1)}, u32[]{:S(2)}, u32[]{:S(2)}) collective-permute-start(bf16[288,256]{1,0:T(8,128)(2,1)S(1)} %get-tuple-element.83), channel_id=1, source_target_pairs={{0,8},{4,12},{8,0},{12,4},{16,24},{20,28},{24,16},{28,20},{1,9},{5... | collective-permute-start | bytes 442376 | tf_op jit(solution)/shard_map/ppermute | solution.py:252
  27.7 1.0 %collective-permute-start.13 = (bf16[288,256]{1,0:T(8,128)(2,1)S(1)}, bf16[288,256]{1,0:T(8,128)(2,1)S(1)}, u32[]{:S(2)}, u32[]{:S(2)}) collective-permute-start(bf16[288,256]{1,0:T(8,128)(2,1)S(1)} %get-tuple-element.84), channel_id=1, source_target_pairs={{0,16},{4,20},{8,24},{12,28},{16,0},{20,4},{24,8},{28,12},{1,17},{... | collective-permute-start | bytes 442376 | tf_op jit(solution)/shard_map/ppermute | solution.py:252
  28.7 3.3 %collective-permute-done.11.refs_2_ = bf16[288,256]{1,0:T(8,128)(2,1)S(1)} collective-permute-done((bf16[288,256]{1,0:T(8,128)(2,1)S(1)}, bf16[288,256]{1,0:T(8,128)(2,1)S(1)}, u32[]{:S(2)}, u32[]{:S(2)}) %collective-permute-start.11) | collective-permute-done | bytes 147488 | tf_op jit(solution)/shard_map/ppermute | solution.py:252
  32.1 1.1 %collective-permute-done.12.refs_0_ = bf16[288,256]{1,0:T(8,128)(2,1)S(1)} collective-permute-done((bf16[288,256]{1,0:T(8,128)(2,1)S(1)}, bf16[288,256]{1,0:T(8,128)(2,1)S(1)}, u32[]{:S(2)}, u32[]{:S(2)}) %collective-permute-start.12) | collective-permute-done | bytes 147488 | tf_op jit(solution)/shard_map/ppermute | solution.py:252
  33.1 0.4 %collective-permute-done.13.refs_1_ = bf16[288,256]{1,0:T(8,128)(2,1)S(1)} collective-permute-done((bf16[288,256]{1,0:T(8,128)(2,1)S(1)}, bf16[288,256]{1,0:T(8,128)(2,1)S(1)}, u32[]{:S(2)}, u32[]{:S(2)}) %collective-permute-start.13) | collective-permute-done | bytes 147488 | tf_op jit(solution)/shard_map/ppermute | solution.py:252
  33.7 0.1 collective-permute-start.14
  33.8 1.6 %collective-permute-start.15 = (f32[4,1024]{1,0:T(4,128)S(1)}, f32[4,1024]{1,0:T(4,128)S(1)}, u32[]{:S(2)}, u32[]{:S(2)}) collective-permute-start(f32[4,1024]{1,0:T(4,128)S(1)} %get-tuple-element.90), channel_id=1, source_target_pairs={{0,1},{1,0},{2,3},{3,2},{4,5},{5,4},{6,7},{7,6},{8,9},{9,8},{10,11... | collective-permute-start | bytes 49160 | tf_op jit(solution)/shard_map/ppermute | solution.py:267
  35.4 1.0 %place.2.refs_0_ = f32[1024,512]{1,0:T(8,128)} custom-call(bf16[1024,256]{1,0:T(8,128)(2,1)S(1)} %pad_maximum_fusion.src_ref), custom_call_target="tpu_custom_call" | custom-call | flops 524288 | bytes 3145728 | tf_op jit(solution)/shard_map/place/pallas_call | solution.py:380
  36.4 0.0 collective-permute-done.14.src_ref
  36.4 1.0 %place.3 = f32[1024,512]{1,0:T(8,128)} custom-call(bf16[1024,256]{1,0:T(8,128)(2,1)S(1)} %collective-permute-done.14.src_ref, f32[1024,512]{1,0:T(8,128)} %place.2.refs_0_), custom_call_target="tpu_custom_call", output_to_operand_aliasing={{}: (1, {})} | custom-call | flops 524288 | bytes 3145728 | tf_op jit(solution)/shard_map/place/pallas_call | solution.py:380
  37.5 0.1 collective-permute-done.15
  37.6 0.6 %add.8 = f32[4,1024]{1,0:T(4,128)} add(f32[4,1024]{1,0:T(4,128)S(1)} %get-tuple-element.91, f32[4,1024]{1,0:T(4,128)S(1)} %collective-permute-done.15) | non-fusion elementwise | flops 4096 | bytes 49152 | tf_op jit(solution)/shard_map/add | solution.py:394
  (12 shorter events, 0.1 us)
Async XLA Ops:
  0.6 8.7 %copy-start.2 = (s32[512]{0:T(512)S(1)}, s32[512]{0:T(512)}, u32[]{:S(2)}) copy-start(s32[512]{0:T(512)} %rel_hbm.1) | copy-start | bytes 6148
  0.6 7.6 %collective-permute-start = (bf16[16,1024]{1,0:T(8,128)(2,1)}, bf16[16,1024]{1,0:T(8,128)(2,1)S(1)}, u32[]{:S(2)}, u32[]{:S(2)}) collective-permute-start(bf16[16,1024]{1,0:T(8,128)(2,1)} %table_hbm.1), channel_id=1, source_target_pairs={{0,8},{4,12},{8,0},{12,4},{16,24},{20,28},{24,16},{28,20},{1,9},{5... | collective-permute-start | bytes 98312 | tf_op jit(solution)/shard_map/ppermute | solution.py:252
  3.6 5.0 %collective-permute-start.2 = (bf16[16,1024]{1,0:T(8,128)(2,1)}, bf16[16,1024]{1,0:T(8,128)(2,1)S(1)}, u32[]{:S(2)}, u32[]{:S(2)}) collective-permute-start(bf16[16,1024]{1,0:T(8,128)(2,1)} %table_hbm.1), channel_id=1, source_target_pairs={{0,24},{4,28},{8,16},{12,20},{16,8},{20,12},{24,0},{28,4},{1,25},{... | collective-permute-start | bytes 98312 | tf_op jit(solution)/shard_map/ppermute | solution.py:252
  5.1 4.1 %collective-permute-start.1 = (bf16[16,1024]{1,0:T(8,128)(2,1)}, bf16[16,1024]{1,0:T(8,128)(2,1)S(1)}, u32[]{:S(2)}, u32[]{:S(2)}) collective-permute-start(bf16[16,1024]{1,0:T(8,128)(2,1)} %table_hbm.1), channel_id=1, source_target_pairs={{0,16},{4,20},{8,24},{12,28},{16,0},{20,4},{24,8},{28,12},{1,17},{... | collective-permute-start | bytes 98312 | tf_op jit(solution)/shard_map/ppermute | solution.py:252
  5.2 8.0 %copy-start = (s32[512,1]{0,1:T(1,128)S(1)}, s32[512,1]{0,1:T(1,128)}, u32[]{:S(2)}) copy-start(s32[512,1]{0,1:T(1,128)} %param.9) | copy-start | bytes 6148
  5.2 8.0 %copy-start.1 = (s32[512]{0:T(512)S(1)}, s32[512]{0:T(512)}, u32[]{:S(2)}) copy-start(s32[512]{0:T(512)} %param.10) | copy-start | bytes 6148
  9.3 1.4 %collective-permute-start.3 = (bf16[64,1024]{1,0:T(8,128)(2,1)S(1)}, bf16[64,1024]{1,0:T(8,128)(2,1)S(1)}, u32[]{:S(2)}, u32[]{:S(2)}) collective-permute-start(bf16[64,1024]{1,0:T(8,128)(2,1)S(1)} %constant_dynamic-update-slice_fusion.refs_0_), channel_id=1, source_target_pairs={{0,4},{4,0},{8,12},{12,8},{16,20},{20,16},{24,28},{28,24},{1,5},{5... | collective-permute-start | bytes 393224 | tf_op jit(solution)/shard_map/ppermute | solution.py:252
  9.4 1.3 %collective-permute-start.4 = (s32[1,512]{1,0:T(1,128)S(1)}, s32[1,512]{1,0:T(1,128)S(1)}, u32[]{:S(2)}, u32[]{:S(2)}) collective-permute-start(s32[1,512]{1,0:T(1,128)S(1)} %bitcast.9), channel_id=1, source_target_pairs={{0,4},{4,0},{8,12},{12,8},{16,20},{20,16},{24,28},{28,24},{1,5},{5... | collective-permute-start | bytes 6152 | tf_op jit(solution)/shard_map/ppermute | solution.py:252
  12.8 1.7 %collective-permute-start.5 = (bf16[512,256]{1,0:T(8,128)(2,1)S(1)}, bf16[512,256]{1,0:T(8,128)(2,1)S(1)}, u32[]{:S(2)}, u32[]{:S(2)}) collective-permute-start(bf16[512,256]{1,0:T(8,128)(2,1)S(1)} %get-tuple-element.65), channel_id=1, source_target_pairs={{0,4},{4,0},{8,12},{12,8},{16,20},{20,16},{24,28},{28,24},{1,5},{5... | collective-permute-start | bytes 786440 | tf_op jit(solution)/shard_map/ppermute | solution.py:252
  15.1 4.0 %collective-permute-start.9 = (f32[64,1024]{1,0:T(8,128)S(1)}, f32[64,1024]{1,0:T(8,128)S(1)}, u32[]{:S(2)}, u32[]{:S(2)}) collective-permute-start(f32[64,1024]{1,0:T(8,128)S(1)} %get-tuple-element.80), channel_id=1, source_target_pairs={{0,4},{4,0},{8,12},{12,8},{16,20},{20,16},{24,28},{28,24},{1,5},{5... | collective-permute-start | bytes 786440 | tf_op jit(solution)/shard_map/ppermute | solution.py:252
  15.4 6.7 %collective-permute-start.6 = (bf16[256,256]{1,0:T(8,128)(2,1)S(1)}, bf16[256,256]{1,0:T(8,128)(2,1)S(1)}, u32[]{:S(2)}, u32[]{:S(2)}) collective-permute-start(bf16[256,256]{1,0:T(8,128)(2,1)S(1)} %get-tuple-element.73), channel_id=1, source_target_pairs={{0,8},{4,12},{8,0},{12,4},{16,24},{20,28},{24,16},{28,20},{1,9},{5... | collective-permute-start | bytes 393224 | tf_op jit(solution)/shard_map/ppermute | solution.py:252
  16.9 8.2 %collective-permute-start.7 = (bf16[256,256]{1,0:T(8,128)(2,1)S(1)}, bf16[256,256]{1,0:T(8,128)(2,1)S(1)}, u32[]{:S(2)}, u32[]{:S(2)}) collective-permute-start(bf16[256,256]{1,0:T(8,128)(2,1)S(1)} %get-tuple-element.74), channel_id=1, source_target_pairs={{0,16},{4,20},{8,24},{12,28},{16,0},{20,4},{24,8},{28,12},{1,17},{... | collective-permute-start | bytes 393224 | tf_op jit(solution)/shard_map/ppermute | solution.py:252
  17.9 7.2 %collective-permute-start.8 = (bf16[256,256]{1,0:T(8,128)(2,1)S(1)}, bf16[256,256]{1,0:T(8,128)(2,1)S(1)}, u32[]{:S(2)}, u32[]{:S(2)}) collective-permute-start(bf16[256,256]{1,0:T(8,128)(2,1)S(1)} %get-tuple-element.75), channel_id=1, source_target_pairs={{0,24},{4,28},{8,16},{12,20},{16,8},{20,12},{24,0},{28,4},{1,25},{... | collective-permute-start | bytes 393224 | tf_op jit(solution)/shard_map/ppermute | solution.py:252
  19.2 5.9 %collective-permute-start.10 = (bf16[32,1024]{1,0:T(8,128)(2,1)S(1)}, bf16[32,1024]{1,0:T(8,128)(2,1)S(1)}, u32[]{:S(2)}, u32[]{:S(2)}) collective-permute-start(bf16[32,1024]{1,0:T(8,128)(2,1)S(1)} %slice.24), channel_id=1, source_target_pairs={{0,2},{1,3},{2,0},{3,1},{4,6},{5,7},{6,4},{7,5},{8,10},{9,11},{10,... | collective-permute-start | bytes 196616 | tf_op jit(solution)/shard_map/ppermute | solution.py:267
  25.2 6.9 %collective-permute-start.11 = (bf16[288,256]{1,0:T(8,128)(2,1)S(1)}, bf16[288,256]{1,0:T(8,128)(2,1)S(1)}, u32[]{:S(2)}, u32[]{:S(2)}) collective-permute-start(bf16[288,256]{1,0:T(8,128)(2,1)S(1)} %get-tuple-element.82), channel_id=1, source_target_pairs={{0,24},{4,28},{8,16},{12,20},{16,8},{20,12},{24,0},{28,4},{1,25},{... | collective-permute-start | bytes 442376 | tf_op jit(solution)/shard_map/ppermute | solution.py:252
  26.6 6.5 %collective-permute-start.12 = (bf16[288,256]{1,0:T(8,128)(2,1)S(1)}, bf16[288,256]{1,0:T(8,128)(2,1)S(1)}, u32[]{:S(2)}, u32[]{:S(2)}) collective-permute-start(bf16[288,256]{1,0:T(8,128)(2,1)S(1)} %get-tuple-element.83), channel_id=1, source_target_pairs={{0,8},{4,12},{8,0},{12,4},{16,24},{20,28},{24,16},{28,20},{1,9},{5... | collective-permute-start | bytes 442376 | tf_op jit(solution)/shard_map/ppermute | solution.py:252
  27.7 5.9 %collective-permute-start.13 = (bf16[288,256]{1,0:T(8,128)(2,1)S(1)}, bf16[288,256]{1,0:T(8,128)(2,1)S(1)}, u32[]{:S(2)}, u32[]{:S(2)}) collective-permute-start(bf16[288,256]{1,0:T(8,128)(2,1)S(1)} %get-tuple-element.84), channel_id=1, source_target_pairs={{0,16},{4,20},{8,24},{12,28},{16,0},{20,4},{24,8},{28,12},{1,17},{... | collective-permute-start | bytes 442376 | tf_op jit(solution)/shard_map/ppermute | solution.py:252
  33.7 2.8 %collective-permute-start.14 = (bf16[1024,256]{1,0:T(8,128)(2,1)S(1)}, bf16[1024,256]{1,0:T(8,128)(2,1)S(1)}, u32[]{:S(2)}, u32[]{:S(2)}) collective-permute-start(bf16[1024,256]{1,0:T(8,128)(2,1)S(1)} %pad_maximum_fusion.src_ref), channel_id=1, source_target_pairs={{0,4},{4,0},{8,12},{12,8},{16,20},{20,16},{24,28},{28,24},{1,5},{5... | collective-permute-start | bytes 1572872 | tf_op jit(solution)/shard_map/ppermute | solution.py:252
  33.8 3.8 %collective-permute-start.15 = (f32[4,1024]{1,0:T(4,128)S(1)}, f32[4,1024]{1,0:T(4,128)S(1)}, u32[]{:S(2)}, u32[]{:S(2)}) collective-permute-start(f32[4,1024]{1,0:T(4,128)S(1)} %get-tuple-element.90), channel_id=1, source_target_pairs={{0,1},{1,0},{2,3},{3,2},{4,5},{5,4},{6,7},{7,6},{8,9},{9,8},{10,11... | collective-permute-start | bytes 49160 | tf_op jit(solution)/shard_map/ppermute | solution.py:267

commit v6 on v5

--- a/solution.py
+++ b/solution.py
@@ -10,6 +10,7 @@
 F32 = jnp.float32
 BF16 = jnp.bfloat16
 I32 = jnp.int32
+DIGIT = 64
 VMEM_BYTES = 16 * 1024 * 1024
 NT = (((1,), (1,)), ((), ()))
 
@@ -94,7 +95,7 @@
 
 
 def score_kernel(*refs, peers, block):
-    own_ref, mate_ref, cos_ref, sin_ref, code_ref, keep_ref, send_ref, w_ref, q_ref = refs
+    own_ref, mate_ref, rel_ref, cos_ref, sin_ref, code_ref, keep_ref, send_ref, w_ref, q_ref = refs
     n, half = cos_ref.shape
     quarter = half // 2
     tab = candidates(own_ref, mate_ref, peers)
@@ -102,6 +103,11 @@
     norm = jnp.sum(f * f, axis=1, keepdims=True)
     tsq = jnp.broadcast_to(norm, (norm.shape[0], 128)).T[0:1]
     even = lax.axis_index("ent") % 2 == 0
+    rel = rel_ref[...].astype(F32)
+    high = jnp.floor(rel * (1.0 / DIGIT))
+    lines = [x[:, i : i + quarter] for x in (high, rel - DIGIT * high) for i in range(0, n, quarter)]
+    lines.append(jnp.zeros((send_ref.shape[0] - n - len(lines), quarter), F32))
+    send_ref[n:, :] = jnp.concatenate(lines, axis=0).astype(BF16)
     for start in range(0, n, block):
         at = slice(start, start + block)
         cosine = cos_ref[at, :]
@@ -175,10 +181,14 @@
     send_ref[...] = total[entities // 2 :]
 
 
-def scatter_kernel(mine_ref, theirs_ref, keep_ref, got_ref, *outs, shares, rows):
+def scatter_kernel(mine_ref, keep_ref, got_ref, *outs, shares, rows):
     chip = lax.axis_index("ent") // 2
-    ids = jnp.concatenate([mine_ref[...], theirs_ref[...]], axis=1)
-    d = jnp.concatenate([keep_ref[...], got_ref[...]], axis=0)
+    count, quarter = keep_ref.shape
+    lines = count // quarter
+    digits = got_ref[count:, :].astype(F32)
+    theirs = [digits[i : i + 1] * DIGIT + digits[lines + i : lines + i + 1] for i in range(lines)]
+    ids = jnp.concatenate([mine_ref[...]] + [x.astype(I32) for x in theirs], axis=1)
+    d = jnp.concatenate([keep_ref[...], got_ref[:count, :]], axis=0)
     n = ids.shape[1]
     iota = lax.broadcasted_iota(I32, (rows, n), 0)
     for out, (p, first) in zip(outs, shares):
@@ -296,22 +306,22 @@
 
     cosine, sine, code, own, *far = lax.optimization_barrier((cosine, sine, code, own, *far))
     held = jnp.concatenate([own, *far], axis=0)
-    mate, rel_mate = lax.optimization_barrier((swap(held, 1), swap(rel_l, 1)))
-    tables = [held, mate]
+    tables = [held, swap(held, 1)]
+    digit_rows = -(-2 * (n // quarter) // 16) * 16
     keep, send, w, q = pl.pallas_call(
         functools.partial(score_kernel, peers=peers, block=block),
-        in_specs=[vm] * 5,
+        in_specs=[vm] * 6,
         out_specs=[vm] * 4,
         out_shape=[
             jax.ShapeDtypeStruct((n, quarter), BF16),
-            jax.ShapeDtypeStruct((n, quarter), BF16),
+            jax.ShapeDtypeStruct((n + digit_rows, quarter), BF16),
             jax.ShapeDtypeStruct((n, entities), BF16),
             jax.ShapeDtypeStruct((n, width), BF16),
         ],
         compiler_params=params(),
         cost_estimate=cost(6 * n * entities * width, 12 * n * width),
         name="score",
-    )(*tables, cosine, sine, code)
+    )(*tables, rel_l, cosine, sine, code)
 
     got = swap(send, 1)
     ent_keep, ent_send = pl.pallas_call(
@@ -328,13 +338,13 @@
     def scatter(shares, rows, dtype, work):
         return pl.pallas_call(
             functools.partial(scatter_kernel, shares=shares, rows=rows),
-            in_specs=[vm] * 4,
+            in_specs=[vm] * 3,
             out_specs=[vm] * len(shares),
             out_shape=[jax.ShapeDtypeStruct((rows, quarter), dtype)] * len(shares),
             compiler_params=params(),
             cost_estimate=work,
             name="scatter",
-        )(rel_l, rel_mate, keep, got)
+        )(rel_l, keep, got)
 
     parts = scatter([(p, 0) for p in range(1, peers)], rows, BF16, cost(4 * n * rels * quarter, 4 * n * quarter + 2 * rels * quarter))
     *parts, ent_keep, ent_send = lax.optimization_barrier((*parts, ent_keep, ent_send))

time: 38.3 us -> 38.2 us (level)
  starting transfers between devices: 17.2 us -> 16.7 us
    ppermute x14 -> x13, starting transfers between devices: 12.9 us -> 12.4 us  [swap(): return lax.ppermute(x, 'ent', [(i, i ^ k) for i in range(n_ent)])]
    ppermute x14 -> x13, waiting for transfers between devices: 9.69 us -> 9.93 us  [swap(): return lax.ppermute(x, 'ent', [(i, i ^ k) for i in range(n_ent)])]
  transfers between devices with their start and end apart: 16 -> 15, of which waited for: 8 -> 8; matrix products, arithmetic and copies ran while one was open for 0% -> 0% of each run, Pallas kernels for 18% -> 18%
where the time goes in v6:
time: 38.2 us; the launch traced here: 38 us
  starting transfers between devices  16.7 us (44%)
  waiting for transfers between devices  10 us (26%)
  Pallas kernels  9.71 us (25%)
  between operations  0.84 us (2%)
  other arithmetic  0.69 us (2%)
    ppermute x13, starting transfers between devices, swap(): return lax.ppermute(x, 'ent', [(i, i ^ k) for i in range(n_ent)])  12.4 us
    ppermute x13, waiting for transfers between devices, swap(): return lax.ppermute(x, 'ent', [(i, i ^ k) for i in range(n_ent)])  9.93 us
    ppermute x2, starting transfers between devices, swap_rel(): return lax.ppermute(x, 'rel', [(i, i ^ k) for i in range(n_rel)])  4.31 us
    pallas_call x1, Pallas kernels, local(): pl.pallas_call(functools.partial(prepare_kernel, rows_ent=rows_ent, owner...  3.02 us
    pallas_call x1, Pallas kernels, local(): pl.pallas_call(functools.partial(score_kernel, peers=peers, block=block),...  2.14 us
    pallas_call x2, Pallas kernels, place(): pl.pallas_call(functools.partial(place_kernel, side=side, peers=peers, ro...  2.03 us
    pallas_call x1, Pallas kernels, local(): pl.pallas_call(functools.partial(entity_kernel, peers=peers, n_rel=n_rel,...  1.37 us
    pallas_call x3, Pallas kernels, scatter(): pl.pallas_call(functools.partial(scatter_kernel, shares=shares, rows=rows...  1.05 us
  transfers between devices with their start and end apart: 15, of which 8 were waited for; matrix products, arithmetic and copies ran while one was open for 0% of the time, Pallas kernels for 18%

profile of v6, /device:TPU:0, one launch (start us, length us, event | category | flops | bytes accessed | tf_op | source)
XLA Modules:
  0.0 38.0 jit_solution(2912072486051002797)
XLA Ops:
  0.6 0.0 copy-start.2
  0.6 3.0 %collective-permute-start = (bf16[16,1024]{1,0:T(8,128)(2,1)}, bf16[16,1024]{1,0:T(8,128)(2,1)S(1)}, u32[]{:S(2)}, u32[]{:S(2)}) collective-permute-start(bf16[16,1024]{1,0:T(8,128)(2,1)} %table_hbm.1), channel_id=1, source_target_pairs={{0,8},{4,12},{8,0},{12,4},{16,24},{20,28},{24,16},{28,20},{1,9},{5... | collective-permute-start | bytes 98312 | tf_op jit(solution)/shard_map/ppermute | solution.py:262
  3.6 1.5 %collective-permute-start.2 = (bf16[16,1024]{1,0:T(8,128)(2,1)}, bf16[16,1024]{1,0:T(8,128)(2,1)S(1)}, u32[]{:S(2)}, u32[]{:S(2)}) collective-permute-start(bf16[16,1024]{1,0:T(8,128)(2,1)} %table_hbm.1), channel_id=1, source_target_pairs={{0,24},{4,28},{8,16},{12,20},{16,8},{20,12},{24,0},{28,4},{1,25},{... | collective-permute-start | bytes 98312 | tf_op jit(solution)/shard_map/ppermute | solution.py:262
  5.1 0.0 collective-permute-start.1
  5.2 0.0 copy-start
  5.2 0.0 copy-start.1
  5.2 3.0 %prepare.1 = (f32[512,512]{1,0:T(8,128)S(1)}, f32[512,512]{1,0:T(8,128)S(1)}, s32[512,128]{1,0:T(8,128)S(1)}, bf16[16,1024]{1,0:T(8,128)(2,1)S(1)}) custom-call(s32[512]{0:T(512)} %rel_hbm.1, f32[1024,512]{1,0:T(8,128)} %phases_hbm.1, s32[1,512]{1,0:T(1,128)} %bitcast.5, s32[1,512]{1,0:T(1,128)} %bitcast.7, s32[1,512]{1,0:T(1,128)} %bitcast.14, ...), custom_call_target="tpu_custom_call" | custom-call | flops 7864320 | bytes 3145728 | tf_op jit(solution)/shard_map/prepare/pallas_call | solution.py:289
  8.2 0.0 collective-permute-done
  8.2 0.4 %collective-permute-done.2 = bf16[16,1024]{1,0:T(8,128)(2,1)S(1)} collective-permute-done((bf16[16,1024]{1,0:T(8,128)(2,1)}, bf16[16,1024]{1,0:T(8,128)(2,1)S(1)}, u32[]{:S(2)}, u32[]{:S(2)}) %collective-permute-start.2) | collective-permute-done | bytes 32800 | tf_op jit(solution)/shard_map/ppermute | solution.py:262
  8.7 0.6 %collective-permute-done.1 = bf16[16,1024]{1,0:T(8,128)(2,1)S(1)} collective-permute-done((bf16[16,1024]{1,0:T(8,128)(2,1)}, bf16[16,1024]{1,0:T(8,128)(2,1)S(1)}, u32[]{:S(2)}, u32[]{:S(2)}) %collective-permute-start.1) | collective-permute-done | bytes 32800 | tf_op jit(solution)/shard_map/ppermute | solution.py:262
  9.3 0.1 collective-permute-start.3
  9.4 1.3 %collective-permute-done.3.refs_1_ = bf16[64,1024]{1,0:T(8,128)(2,1)S(1)} collective-permute-done((bf16[64,1024]{1,0:T(8,128)(2,1)S(1)}, bf16[64,1024]{1,0:T(8,128)(2,1)S(1)}, u32[]{:S(2)}, u32[]{:S(2)}) %collective-permute-start.3) | collective-permute-done | bytes 131104 | tf_op jit(solution)/shard_map/ppermute | solution.py:262
  10.7 0.0 copy-done.2
  10.7 2.1 %score.1 = (bf16[512,256]{1,0:T(8,128)(2,1)S(1)}, bf16[528,256]{1,0:T(8,128)(2,1)S(1)}, bf16[512,128]{1,0:T(8,128)(2,1)S(1)}, bf16[512,1024]{1,0:T(8,128)(2,1)S(1)}) custom-call(bf16[64,1024]{1,0:T(8,128)(2,1)S(1)} %constant_dynamic-update-slice_fusion.refs_0_, bf16[64,1024]{1,0:T(8,128)(2,1)S(1)} %collective-permute-done.3.refs_1_, s32[1,512]{1,0:T(1,128)S(1)} %bitcast.9, ...), custom_call_target="tpu_custom_call" | custom-call | flops 402653184 | bytes 6291456 | tf_op jit(solution)/shard_map/score/pallas_call | solution.py:311
  12.9 0.2 collective-permute-start.4
  13.1 0.0 copy-done
  13.1 0.0 copy-done.1
  13.1 1.4 %entity.1 = (f32[64,1024]{1,0:T(8,128)S(1)}, f32[64,1024]{1,0:T(8,128)S(1)}) custom-call(bf16[512,128]{1,0:T(8,128)(2,1)S(1)} %get-tuple-element.65.w_ref, bf16[512,1024]{1,0:T(8,128)(2,1)S(1)} %get-tuple-element.66.q_ref, f32[512,512]{1,0:T(8,128)S(1)} %get-tuple-element.57.refs_3_.cos_ref, f32[512,512]{1,0:T(8,128)S(1)} %get-tuple-element.58.refs_4_.sin_ref, ...), custom_call_target="tpu_custom_call" | custom-call | flops 402653184 | bytes 2621440 | tf_op jit(solution)/shard_map/entity/pallas_call | solution.py:327
  14.4 0.0 collective-permute-done.4.got_ref
  14.5 0.6 %scatter.5 = (bf16[256,256]{1,0:T(8,128)(2,1)S(1)}, bf16[256,256]{1,0:T(8,128)(2,1)S(1)}, bf16[256,256]{1,0:T(8,128)(2,1)S(1)}) custom-call(s32[1,512]{1,0:T(1,128)S(1)} %bitcast.10, bf16[512,256]{1,0:T(8,128)(2,1)S(1)} %get-tuple-element.60.keep_ref, bf16[528,256]{1,0:T(8,128)(2,1)S(1)} %collective-permute-done.4.got_ref), custom_call_target="tpu_custom_call" | custom-call | flops 536870912 | bytes 1048576 | tf_op jit(solution)/shard_map/scatter/pallas_call | solution.py:339
  15.1 0.4 %collective-permute-start.8 = (f32[64,1024]{1,0:T(8,128)S(1)}, f32[64,1024]{1,0:T(8,128)S(1)}, u32[]{:S(2)}, u32[]{:S(2)}) collective-permute-start(f32[64,1024]{1,0:T(8,128)S(1)} %get-tuple-element.76), channel_id=1, source_target_pairs={{0,4},{4,0},{8,12},{12,8},{16,20},{20,16},{24,28},{28,24},{1,5},{5... | collective-permute-start | bytes 786440 | tf_op jit(solution)/shard_map/ppermute | solution.py:262
  15.5 1.5 %collective-permute-start.5 = (bf16[256,256]{1,0:T(8,128)(2,1)S(1)}, bf16[256,256]{1,0:T(8,128)(2,1)S(1)}, u32[]{:S(2)}, u32[]{:S(2)}) collective-permute-start(bf16[256,256]{1,0:T(8,128)(2,1)S(1)} %get-tuple-element.69), channel_id=1, source_target_pairs={{0,8},{4,12},{8,0},{12,4},{16,24},{20,28},{24,16},{28,20},{1,9},{5... | collective-permute-start | bytes 393224 | tf_op jit(solution)/shard_map/ppermute | solution.py:262
  17.0 1.0 %collective-permute-start.6 = (bf16[256,256]{1,0:T(8,128)(2,1)S(1)}, bf16[256,256]{1,0:T(8,128)(2,1)S(1)}, u32[]{:S(2)}, u32[]{:S(2)}) collective-permute-start(bf16[256,256]{1,0:T(8,128)(2,1)S(1)} %get-tuple-element.70), channel_id=1, source_target_pairs={{0,16},{4,20},{8,24},{12,28},{16,0},{20,4},{24,8},{28,12},{1,17},{... | collective-permute-start | bytes 393224 | tf_op jit(solution)/shard_map/ppermute | solution.py:262
  18.0 1.0 %collective-permute-start.7 = (bf16[256,256]{1,0:T(8,128)(2,1)S(1)}, bf16[256,256]{1,0:T(8,128)(2,1)S(1)}, u32[]{:S(2)}, u32[]{:S(2)}) collective-permute-start(bf16[256,256]{1,0:T(8,128)(2,1)S(1)} %get-tuple-element.71), channel_id=1, source_target_pairs={{0,24},{4,28},{8,16},{12,20},{16,8},{20,12},{24,0},{28,4},{1,25},{... | collective-permute-start | bytes 393224 | tf_op jit(solution)/shard_map/ppermute | solution.py:262
  19.0 0.2 scatter.4.high_ref
  19.2 0.0 collective-permute-done.8
  19.3 2.7 %collective-permute-start.9 = (bf16[32,1024]{1,0:T(8,128)(2,1)S(1)}, bf16[32,1024]{1,0:T(8,128)(2,1)S(1)}, u32[]{:S(2)}, u32[]{:S(2)}) collective-permute-start(bf16[32,1024]{1,0:T(8,128)(2,1)S(1)} %slice.24), channel_id=1, source_target_pairs={{0,2},{1,3},{2,0},{3,1},{4,6},{5,7},{6,4},{7,5},{8,10},{9,11},{10,... | collective-permute-start | bytes 196616 | tf_op jit(solution)/shard_map/ppermute | solution.py:277
  21.9 0.2 scatter.3.low_ref
  22.2 0.0 collective-permute-done.5.refs_0_
  22.2 2.9 %collective-permute-done.6.refs_1_ = bf16[256,256]{1,0:T(8,128)(2,1)S(1)} collective-permute-done((bf16[256,256]{1,0:T(8,128)(2,1)S(1)}, bf16[256,256]{1,0:T(8,128)(2,1)S(1)}, u32[]{:S(2)}, u32[]{:S(2)}) %collective-permute-start.6) | collective-permute-done | bytes 131104 | tf_op jit(solution)/shard_map/ppermute | solution.py:262
  25.1 0.0 collective-permute-done.7.refs_2_
  25.1 0.0 collective-permute-done.9.refs_4_
  25.1 0.1 combine.1
  25.2 1.5 %collective-permute-start.10 = (bf16[288,256]{1,0:T(8,128)(2,1)S(1)}, bf16[288,256]{1,0:T(8,128)(2,1)S(1)}, u32[]{:S(2)}, u32[]{:S(2)}) collective-permute-start(bf16[288,256]{1,0:T(8,128)(2,1)S(1)} %get-tuple-element.78), channel_id=1, source_target_pairs={{0,24},{4,28},{8,16},{12,20},{16,8},{20,12},{24,0},{28,4},{1,25},{... | collective-permute-start | bytes 442376 | tf_op jit(solution)/shard_map/ppermute | solution.py:262
  26.6 1.1 %collective-permute-start.11 = (bf16[288,256]{1,0:T(8,128)(2,1)S(1)}, bf16[288,256]{1,0:T(8,128)(2,1)S(1)}, u32[]{:S(2)}, u32[]{:S(2)}) collective-permute-start(bf16[288,256]{1,0:T(8,128)(2,1)S(1)} %get-tuple-element.79), channel_id=1, source_target_pairs={{0,8},{4,12},{8,0},{12,4},{16,24},{20,28},{24,16},{28,20},{1,9},{5... | collective-permute-start | bytes 442376 | tf_op jit(solution)/shard_map/ppermute | solution.py:262
  27.7 1.0 %collective-permute-start.12 = (bf16[288,256]{1,0:T(8,128)(2,1)S(1)}, bf16[288,256]{1,0:T(8,128)(2,1)S(1)}, u32[]{:S(2)}, u32[]{:S(2)}) collective-permute-start(bf16[288,256]{1,0:T(8,128)(2,1)S(1)} %get-tuple-element.80), channel_id=1, source_target_pairs={{0,16},{4,20},{8,24},{12,28},{16,0},{20,4},{24,8},{28,12},{1,17},{... | collective-permute-start | bytes 442376 | tf_op jit(solution)/shard_map/ppermute | solution.py:262
  28.7 3.2 %collective-permute-done.10.refs_2_ = bf16[288,256]{1,0:T(8,128)(2,1)S(1)} collective-permute-done((bf16[288,256]{1,0:T(8,128)(2,1)S(1)}, bf16[288,256]{1,0:T(8,128)(2,1)S(1)}, u32[]{:S(2)}, u32[]{:S(2)}) %collective-permute-start.10) | collective-permute-done | bytes 147488 | tf_op jit(solution)/shard_map/ppermute | solution.py:262
  31.9 1.1 %collective-permute-done.11.refs_0_ = bf16[288,256]{1,0:T(8,128)(2,1)S(1)} collective-permute-done((bf16[288,256]{1,0:T(8,128)(2,1)S(1)}, bf16[288,256]{1,0:T(8,128)(2,1)S(1)}, u32[]{:S(2)}, u32[]{:S(2)}) %collective-permute-start.11) | collective-permute-done | bytes 147488 | tf_op jit(solution)/shard_map/ppermute | solution.py:262
  33.0 0.4 %collective-permute-done.12.refs_1_ = bf16[288,256]{1,0:T(8,128)(2,1)S(1)} collective-permute-done((bf16[288,256]{1,0:T(8,128)(2,1)S(1)}, bf16[288,256]{1,0:T(8,128)(2,1)S(1)}, u32[]{:S(2)}, u32[]{:S(2)}) %collective-permute-start.12) | collective-permute-done | bytes 147488 | tf_op jit(solution)/shard_map/ppermute | solution.py:262
  33.5 0.1 collective-permute-start.13
  33.6 1.6 %collective-permute-start.14 = (f32[4,1024]{1,0:T(4,128)S(1)}, f32[4,1024]{1,0:T(4,128)S(1)}, u32[]{:S(2)}, u32[]{:S(2)}) collective-permute-start(f32[4,1024]{1,0:T(4,128)S(1)} %get-tuple-element.86), channel_id=1, source_target_pairs={{0,1},{1,0},{2,3},{3,2},{4,5},{5,4},{6,7},{7,6},{8,9},{9,8},{10,11... | collective-permute-start | bytes 49160 | tf_op jit(solution)/shard_map/ppermute | solution.py:277
  35.2 1.0 %place.2.refs_0_ = f32[1024,512]{1,0:T(8,128)} custom-call(bf16[1024,256]{1,0:T(8,128)(2,1)S(1)} %pad_maximum_fusion.src_ref), custom_call_target="tpu_custom_call" | custom-call | flops 524288 | bytes 3145728 | tf_op jit(solution)/shard_map/place/pallas_call | solution.py:390
  36.3 0.0 collective-permute-done.13.src_ref
  36.3 1.0 %place.3 = f32[1024,512]{1,0:T(8,128)} custom-call(bf16[1024,256]{1,0:T(8,128)(2,1)S(1)} %collective-permute-done.13.src_ref, f32[1024,512]{1,0:T(8,128)} %place.2.refs_0_), custom_call_target="tpu_custom_call", output_to_operand_aliasing={{}: (1, {})} | custom-call | flops 524288 | bytes 3145728 | tf_op jit(solution)/shard_map/place/pallas_call | solution.py:390
  37.3 0.1 collective-permute-done.14
  37.4 0.6 %add.8 = f32[4,1024]{1,0:T(4,128)} add(f32[4,1024]{1,0:T(4,128)S(1)} %get-tuple-element.87, f32[4,1024]{1,0:T(4,128)S(1)} %collective-permute-done.14) | non-fusion elementwise | flops 4096 | bytes 49152 | tf_op jit(solution)/shard_map/add | solution.py:404
  (12 shorter events, 0.2 us)
Async XLA Ops:
  0.6 10.1 %copy-start.2 = (s32[512]{0:T(512)S(1)}, s32[512]{0:T(512)}, u32[]{:S(2)}) copy-start(s32[512]{0:T(512)} %rel_hbm.1) | copy-start | bytes 6148
  0.6 7.6 %collective-permute-start = (bf16[16,1024]{1,0:T(8,128)(2,1)}, bf16[16,1024]{1,0:T(8,128)(2,1)S(1)}, u32[]{:S(2)}, u32[]{:S(2)}) collective-permute-start(bf16[16,1024]{1,0:T(8,128)(2,1)} %table_hbm.1), channel_id=1, source_target_pairs={{0,8},{4,12},{8,0},{12,4},{16,24},{20,28},{24,16},{28,20},{1,9},{5... | collective-permute-start | bytes 98312 | tf_op jit(solution)/shard_map/ppermute | solution.py:262
  3.6 5.0 %collective-permute-start.2 = (bf16[16,1024]{1,0:T(8,128)(2,1)}, bf16[16,1024]{1,0:T(8,128)(2,1)S(1)}, u32[]{:S(2)}, u32[]{:S(2)}) collective-permute-start(bf16[16,1024]{1,0:T(8,128)(2,1)} %table_hbm.1), channel_id=1, source_target_pairs={{0,24},{4,28},{8,16},{12,20},{16,8},{20,12},{24,0},{28,4},{1,25},{... | collective-permute-start | bytes 98312 | tf_op jit(solution)/shard_map/ppermute | solution.py:262
  5.1 4.1 %collective-permute-start.1 = (bf16[16,1024]{1,0:T(8,128)(2,1)}, bf16[16,1024]{1,0:T(8,128)(2,1)S(1)}, u32[]{:S(2)}, u32[]{:S(2)}) collective-permute-start(bf16[16,1024]{1,0:T(8,128)(2,1)} %table_hbm.1), channel_id=1, source_target_pairs={{0,16},{4,20},{8,24},{12,28},{16,0},{20,4},{24,8},{28,12},{1,17},{... | collective-permute-start | bytes 98312 | tf_op jit(solution)/shard_map/ppermute | solution.py:262
  5.2 7.9 %copy-start = (s32[512,1]{0,1:T(1,128)S(1)}, s32[512,1]{0,1:T(1,128)}, u32[]{:S(2)}) copy-start(s32[512,1]{0,1:T(1,128)} %param.9) | copy-start | bytes 6148
  5.2 7.9 %copy-start.1 = (s32[512]{0:T(512)S(1)}, s32[512]{0:T(512)}, u32[]{:S(2)}) copy-start(s32[512]{0:T(512)} %param.10) | copy-start | bytes 6148
  9.3 1.4 %collective-permute-start.3 = (bf16[64,1024]{1,0:T(8,128)(2,1)S(1)}, bf16[64,1024]{1,0:T(8,128)(2,1)S(1)}, u32[]{:S(2)}, u32[]{:S(2)}) collective-permute-start(bf16[64,1024]{1,0:T(8,128)(2,1)S(1)} %constant_dynamic-update-slice_fusion.refs_0_), channel_id=1, source_target_pairs={{0,4},{4,0},{8,12},{12,8},{16,20},{20,16},{24,28},{28,24},{1,5},{5... | collective-permute-start | bytes 393224 | tf_op jit(solution)/shard_map/ppermute | solution.py:262
  12.9 1.6 %collective-permute-start.4 = (bf16[528,256]{1,0:T(8,128)(2,1)S(1)}, bf16[528,256]{1,0:T(8,128)(2,1)S(1)}, u32[]{:S(2)}, u32[]{:S(2)}) collective-permute-start(bf16[528,256]{1,0:T(8,128)(2,1)S(1)} %get-tuple-element.61), channel_id=1, source_target_pairs={{0,4},{4,0},{8,12},{12,8},{16,20},{20,16},{24,28},{28,24},{1,5},{5... | collective-permute-start | bytes 811016 | tf_op jit(solution)/shard_map/ppermute | solution.py:262
  15.1 4.2 %collective-permute-start.8 = (f32[64,1024]{1,0:T(8,128)S(1)}, f32[64,1024]{1,0:T(8,128)S(1)}, u32[]{:S(2)}, u32[]{:S(2)}) collective-permute-start(f32[64,1024]{1,0:T(8,128)S(1)} %get-tuple-element.76), channel_id=1, source_target_pairs={{0,4},{4,0},{8,12},{12,8},{16,20},{20,16},{24,28},{28,24},{1,5},{5... | collective-permute-start | bytes 786440 | tf_op jit(solution)/shard_map/ppermute | solution.py:262
  15.5 6.7 %collective-permute-start.5 = (bf16[256,256]{1,0:T(8,128)(2,1)S(1)}, bf16[256,256]{1,0:T(8,128)(2,1)S(1)}, u32[]{:S(2)}, u32[]{:S(2)}) collective-permute-start(bf16[256,256]{1,0:T(8,128)(2,1)S(1)} %get-tuple-element.69), channel_id=1, source_target_pairs={{0,8},{4,12},{8,0},{12,4},{16,24},{20,28},{24,16},{28,20},{1,9},{5... | collective-permute-start | bytes 393224 | tf_op jit(solution)/shard_map/ppermute | solution.py:262
  17.0 8.1 %collective-permute-start.6 = (bf16[256,256]{1,0:T(8,128)(2,1)S(1)}, bf16[256,256]{1,0:T(8,128)(2,1)S(1)}, u32[]{:S(2)}, u32[]{:S(2)}) collective-permute-start(bf16[256,256]{1,0:T(8,128)(2,1)S(1)} %get-tuple-element.70), channel_id=1, source_target_pairs={{0,16},{4,20},{8,24},{12,28},{16,0},{20,4},{24,8},{28,12},{1,17},{... | collective-permute-start | bytes 393224 | tf_op jit(solution)/shard_map/ppermute | solution.py:262
  18.0 7.1 %collective-permute-start.7 = (bf16[256,256]{1,0:T(8,128)(2,1)S(1)}, bf16[256,256]{1,0:T(8,128)(2,1)S(1)}, u32[]{:S(2)}, u32[]{:S(2)}) collective-permute-start(bf16[256,256]{1,0:T(8,128)(2,1)S(1)} %get-tuple-element.71), channel_id=1, source_target_pairs={{0,24},{4,28},{8,16},{12,20},{16,8},{20,12},{24,0},{28,4},{1,25},{... | collective-permute-start | bytes 393224 | tf_op jit(solution)/shard_map/ppermute | solution.py:262
  19.3 5.8 %collective-permute-start.9 = (bf16[32,1024]{1,0:T(8,128)(2,1)S(1)}, bf16[32,1024]{1,0:T(8,128)(2,1)S(1)}, u32[]{:S(2)}, u32[]{:S(2)}) collective-permute-start(bf16[32,1024]{1,0:T(8,128)(2,1)S(1)} %slice.24), channel_id=1, source_target_pairs={{0,2},{1,3},{2,0},{3,1},{4,6},{5,7},{6,4},{7,5},{8,10},{9,11},{10,... | collective-permute-start | bytes 196616 | tf_op jit(solution)/shard_map/ppermute | solution.py:277
  25.2 6.7 %collective-permute-start.10 = (bf16[288,256]{1,0:T(8,128)(2,1)S(1)}, bf16[288,256]{1,0:T(8,128)(2,1)S(1)}, u32[]{:S(2)}, u32[]{:S(2)}) collective-permute-start(bf16[288,256]{1,0:T(8,128)(2,1)S(1)} %get-tuple-element.78), channel_id=1, source_target_pairs={{0,24},{4,28},{8,16},{12,20},{16,8},{20,12},{24,0},{28,4},{1,25},{... | collective-permute-start | bytes 442376 | tf_op jit(solution)/shard_map/ppermute | solution.py:262
  26.6 6.3 %collective-permute-start.11 = (bf16[288,256]{1,0:T(8,128)(2,1)S(1)}, bf16[288,256]{1,0:T(8,128)(2,1)S(1)}, u32[]{:S(2)}, u32[]{:S(2)}) collective-permute-start(bf16[288,256]{1,0:T(8,128)(2,1)S(1)} %get-tuple-element.79), channel_id=1, source_target_pairs={{0,8},{4,12},{8,0},{12,4},{16,24},{20,28},{24,16},{28,20},{1,9},{5... | collective-permute-start | bytes 442376 | tf_op jit(solution)/shard_map/ppermute | solution.py:262
  27.7 5.7 %collective-permute-start.12 = (bf16[288,256]{1,0:T(8,128)(2,1)S(1)}, bf16[288,256]{1,0:T(8,128)(2,1)S(1)}, u32[]{:S(2)}, u32[]{:S(2)}) collective-permute-start(bf16[288,256]{1,0:T(8,128)(2,1)S(1)} %get-tuple-element.80), channel_id=1, source_target_pairs={{0,16},{4,20},{8,24},{12,28},{16,0},{20,4},{24,8},{28,12},{1,17},{... | collective-permute-start | bytes 442376 | tf_op jit(solution)/shard_map/ppermute | solution.py:262
  33.5 2.8 %collective-permute-start.13 = (bf16[1024,256]{1,0:T(8,128)(2,1)S(1)}, bf16[1024,256]{1,0:T(8,128)(2,1)S(1)}, u32[]{:S(2)}, u32[]{:S(2)}) collective-permute-start(bf16[1024,256]{1,0:T(8,128)(2,1)S(1)} %pad_maximum_fusion.src_ref), channel_id=1, source_target_pairs={{0,4},{4,0},{8,12},{12,8},{16,20},{20,16},{24,28},{28,24},{1,5},{5... | collective-permute-start | bytes 1572872 | tf_op jit(solution)/shard_map/ppermute | solution.py:262
  33.6 3.8 %collective-permute-start.14 = (f32[4,1024]{1,0:T(4,128)S(1)}, f32[4,1024]{1,0:T(4,128)S(1)}, u32[]{:S(2)}, u32[]{:S(2)}) collective-permute-start(f32[4,1024]{1,0:T(4,128)S(1)} %get-tuple-element.86), channel_id=1, source_target_pairs={{0,1},{1,0},{2,3},{3,2},{4,5},{5,4},{6,7},{7,6},{8,9},{9,8},{10,11... | collective-permute-start | bytes 49160 | tf_op jit(solution)/shard_map/ppermute | solution.py:277
